TPU v7x, 32 devices: a whole 2x2x4 slice. The times are simulated.
32 devices in a mesh: dp: 4 (over z), code: 8 (over y, x, core).
Axes of the slice: x: 2, y: 2, z: 4, core: 2. Of those that a mesh axis runs over, the one named last changes fastest.
Arguments:
- residuals: bfloat16 [8192, 1024], P('dp'), may hold values from -6 to 6
- codes: int32 [8192, 128], P('dp', 'code'), may hold values from 0 to 255, as said below
- codebook: float32 [128, 256, 8], P('code'), may hold values from -6 to 6
Outputs:
- rotated: float32 [8192, 1024], P('dp', 'code')
- new_codebook: float32 [128, 256, 8], P('code')
Inputs may be any that keep to these rules, and one draw needn't show every extreme that they name: `codes`: each entry names a codeword of its subspace.
All inputs are finite; a program needn't handle non-finite values.
Results may differ from a plain program's by a relative error of at most 0.008.
Values may be sent and summed in bfloat16 or wider, within the bound.
No kernel may reach another device: no remote copies, remote signals or barrier semaphores. Data moves between devices by JAX's collectives and lax.ppermute only.
A program may use at most 64 MiB of HBM per device.

v0:
```python
import functools

import jax
import jax.numpy as jnp
from jax import lax
from jax.experimental import pallas as pl
from jax.experimental.pallas import tpu as pltpu
from jax.sharding import PartitionSpec as P

quintic_a = 3.4445
quintic_b = -4.775
quintic_c = 2.0315
prior_weight = 8.0
epsilon = 1e-06
f32, bf16 = jnp.float32, jnp.bfloat16
MIB = 1024 * 1024
ROW_CHUNKS = 4
NT = (((1,), (1,)), ((), ()))


def dot(left, right):
    return jnp.dot(left, right, preferred_element_type=f32)


def dot_nt(left, right):
    return lax.dot_general(left, right, NT, preferred_element_type=f32)


def cross_kernel(codes_hbm, book_hbm, res_hbm, *refs, dp):
    outs = refs[: dp or 1]
    codes_ref, book_ref, res_ref, recon, cross, sems = refs[dp or 1 :]
    subs, rows = codes_ref.shape
    width = book_ref.shape[0] // subs
    words = book_ref.shape[1]
    lanes = 128
    chunks = sems.shape[0] - 2
    step = rows // chunks
    loads = [
        pltpu.make_async_copy(codes_hbm, codes_ref, sems.at[0]),
        pltpu.make_async_copy(book_hbm, book_ref, sems.at[1]),
    ]
    for i in range(chunks):
        part = pl.ds(i * step, step)
        loads.append(pltpu.make_async_copy(res_hbm.at[part], res_ref.at[part], sems.at[2 + i]))
    for load in loads:
        load.start()
    loads[0].wait()
    loads[1].wait()
    total = outs[0] if dp is None else cross
    for i in range(chunks):
        part = pl.ds(i * step, step)
        for m in range(subs):
            band = pl.ds(m * width, width)
            tables = [book_ref[band, pl.ds(t * lanes, lanes)] for t in range(words // lanes)]
            for c in range(i * step // lanes, (i + 1) * step // lanes):
                cols = pl.ds(c * lanes, lanes)
                code = jnp.broadcast_to(codes_ref[pl.ds(m, 1), cols], (width, lanes))
                low = jnp.bitwise_and(code, lanes - 1)
                value = jnp.take_along_axis(tables[0], low, axis=1, mode="promise_in_bounds")
                for t in range(1, len(tables)):
                    other = jnp.take_along_axis(tables[t], low, axis=1, mode="promise_in_bounds")
                    value = jnp.where(code >= t * lanes, other, value)
                recon[band, cols] = value
        loads[2 + i].wait()
        product = dot(recon[:, part].astype(bf16), res_ref[part, :])
        total[...] = product if i == 0 else total[...] + product
    if dp is None:
        return
    place = lax.axis_index("dp")
    size = outs[0].shape[0]
    for k, out in enumerate(outs):
        at = pl.multiple_of(jnp.bitwise_xor(place, k) * size, size)
        out[...] = cross[pl.ds(at, size), :].astype(out.dtype)


def cross_partial(codes_t, book_t, residuals, dp):
    rows, dim = residuals.shape
    cols = book_t.shape[0]
    if dp is None:
        shapes = (jax.ShapeDtypeStruct((cols, dim), f32),)
    else:
        shapes = tuple(
            jax.ShapeDtypeStruct((cols // dp, dim), bf16 if k else f32) for k in range(dp)
        )
    shapes += tuple(jax.ShapeDtypeStruct(x.shape, x.dtype) for x in (codes_t, book_t, residuals))
    return pl.pallas_call(
        functools.partial(cross_kernel, dp=dp),
        out_shape=shapes,
        in_specs=[pl.BlockSpec(memory_space=pltpu.HBM)] * 3,
        out_specs=(pl.BlockSpec(memory_space=pltpu.VMEM),) * len(shapes),
        scratch_shapes=[
            pltpu.VMEM((cols, rows), f32),
            pltpu.VMEM((cols, dim), f32),
            pltpu.SemaphoreType.DMA((2 + ROW_CHUNKS,)),
        ],
        compiler_params=pltpu.CompilerParams(vmem_limit_bytes=24 * MIB),
        name="cross_partial",
    )(*[pltpu.with_memory_space_constraint(x, pltpu.HBM) for x in (codes_t, book_t, residuals)])


def polar_kernel(*refs, blocks, pieces, chunk):
    block_refs = refs[:blocks]
    rot_b = refs[blocks]
    raw, gram, gram_b, poly_b, iterate, iterate_b = refs[blocks + 1 :]
    dim = raw.shape[0]
    own = rot_b.shape[0]
    steps = dim // chunk
    at = 0
    for block in block_refs:
        raw[pl.ds(at, block.shape[0]), :] = block[...]
        at += block.shape[0]

    def band_of(i):
        return pl.ds(i * chunk, chunk)

    def lower(j):
        return pl.ds(j * chunk, dim - j * chunk), pl.ds(j * chunk, chunk)

    def mirror(target, j, value):
        rows, cols = lower(j)
        target[rows, cols] = value.astype(bf16)
        for i in range(j + 1, steps):
            at = (i - j) * chunk
            target[cols, pl.ds(i * chunk, chunk)] = value[at : at + chunk, :].T.astype(bf16)

    def gram_of(source):
        r = lax.broadcasted_iota(jnp.int32, (chunk, chunk), 0)
        c = lax.broadcasted_iota(jnp.int32, (chunk, chunk), 1)
        trace = jnp.zeros((), f32)
        for j in range(steps):
            rows, cols = lower(j)
            part = dot_nt(source[rows, :], source[cols, :])
            gram[rows, cols] = part
            mirror(gram_b, j, part)
            trace = trace + jnp.sum(jnp.where(r == c, part[:chunk, :], 0.0))
        return trace

    def poly_of(wb, wc):
        for j in range(steps):
            rows, cols = lower(j)
            square = dot(gram_b[rows, :], gram_b[:, cols])
            mirror(poly_b, j, wb * gram[rows, cols] + wc * square)

    frob = gram_of(raw)
    scale2 = 1.0 / (frob + epsilon)
    scale = lax.rsqrt(frob + epsilon)
    poly_of(quintic_b * scale2, quintic_c * scale2 * scale2)

    for i in range(steps):
        cols = band_of(i)
        value = scale * (quintic_a * raw[:, cols].astype(f32) + dot(poly_b[...], raw[:, cols]))
        iterate[:, cols] = value
        iterate_b[:, cols] = value.astype(bf16)

    gram_of(iterate_b)
    poly_of(quintic_b, quintic_c)

    for i in range(steps):
        cols = band_of(i)
        value = quintic_a * iterate[:, cols] + dot(poly_b[...], iterate_b[:, cols])
        iterate[pl.ds(0, own), cols] = value[:own, :]
        raw[:, cols] = value.astype(bf16)

    mine = pl.ds(0, own)
    g = dot_nt(raw[mine, :], raw[...])
    image = dot(g.astype(bf16), raw[...])
    square = dot_nt(image.astype(bf16), raw[...])
    last = quintic_a * iterate[mine, :] + dot(
        (quintic_b * g + quintic_c * square).astype(bf16), raw[...]
    )
    size = own // pieces
    for p in range(pieces):
        to = 0
        if pieces > 1:
            to = pl.multiple_of(jnp.bitwise_xor(lax.axis_index("dp"), p) * size, size)
        rot_b[pl.ds(to, size), :] = last[p * size : (p + 1) * size, :].astype(bf16)


LOWS = 64


def onehot_kernel(codes_ref, onehot_ref, masks_ref, counts_ref):
    subs, rows_all = codes_ref.shape
    highs = counts_ref.shape[1] // LOWS
    wide = masks_ref.shape[0] // subs
    group = min(subs, 256 // LOWS)
    low_word = lax.broadcasted_iota(jnp.int32, (LOWS, rows_all), 0)
    high_word = lax.broadcasted_iota(jnp.int32, (8, rows_all), 0)
    row = lax.broadcasted_iota(jnp.int32, (wide, rows_all), 0)
    for first in range(0, subs, group):
        onehots, marks = [], []
        for m in range(first, first + group):
            code = codes_ref[pl.ds(m, 1), :]
            low, high = jnp.bitwise_and(code, LOWS - 1), jnp.right_shift(code, 6)
            onehots.append(jnp.where(low_word == low, 1.0, 0.0).astype(bf16))
            marks.append(jnp.where(high_word == high, 1.0, 0.0))
            mask = jnp.where(row // (wide // highs) == high, 1.0, 0.0).astype(bf16)
            masks_ref[pl.ds(m * wide, wide), :] = mask
        onehot = jnp.concatenate(onehots, axis=0).T
        onehot_ref[:, pl.ds(first * LOWS, group * LOWS)] = onehot
        part = dot(jnp.concatenate(marks, axis=0).astype(bf16), onehot)
        for s in range(group):
            for h in range(highs):
                counts_ref[pl.ds(first + s, 1), pl.ds(h * LOWS, LOWS)] = part[
                    s * 8 + h : s * 8 + h + 1, s * LOWS : (s + 1) * LOWS
                ]


def onehot_call(codes_t, words, width):
    subs, rows = codes_t.shape
    vmem = pl.BlockSpec(memory_space=pltpu.VMEM)
    return pl.pallas_call(
        onehot_kernel,
        out_shape=(
            jax.ShapeDtypeStruct((rows, subs * LOWS), bf16),
            jax.ShapeDtypeStruct((subs * width * (words // LOWS), rows), bf16),
            jax.ShapeDtypeStruct((subs, words), f32),
        ),
        in_specs=[vmem],
        out_specs=(vmem, vmem, vmem),
        compiler_params=pltpu.CompilerParams(vmem_limit_bytes=24 * MIB),
        cost_estimate=pl.CostEstimate(
            flops=2 * 256 * subs * LOWS * rows, bytes_accessed=2 * subs * LOWS * rows, transcendentals=0
        ),
        name="onehot",
    )(codes_t)


def sums_kernel(rot_ref, res_ref, onehot_ref, masks_ref, counts_ref, sent_ref, sums_ref):
    subs, words = counts_ref.shape
    own = rot_ref.shape[0]
    width = own // subs
    highs = words // LOWS
    group = min(subs, 256 // LOWS)
    rot_t = dot_nt(rot_ref[...], res_ref[...])
    for first in range(0, subs, group):
        values = []
        for m in range(first, first + group):
            band = rot_t[m * width : (m + 1) * width, :]
            values.append(jnp.concatenate([band] * highs, axis=0).astype(bf16))
        wide = group * highs * width
        tall = jnp.concatenate(values, axis=0) * masks_ref[pl.ds(first // group * wide, wide), :]
        part = dot(tall, onehot_ref[:, pl.ds(first * LOWS, group * LOWS)])
        for s in range(group):
            for h in range(highs):
                at = (s * highs + h) * width
                sums_ref[pl.ds((first + s) * width, width), pl.ds(h * LOWS, LOWS)] = part[
                    at : at + width, s * LOWS : (s + 1) * LOWS
                ]
    sent_ref[pl.ds(0, own), :] = sums_ref[...].astype(bf16)
    sent_ref[pl.ds(own, subs), :] = counts_ref[...].astype(bf16)


def rotated_kernel(rot_ref, res_ref, rotated_ref):
    rows_all = res_ref.shape[0]
    step = 512

    @pl.loop(0, rows_all // step)
    def _(i):
        rows = pl.ds(pl.multiple_of(i * step, step), step)
        rotated_ref[rows, :] = dot_nt(res_ref[rows, :], rot_ref[...])


def polar(block_list, own, pieces):
    dim = block_list[0].shape[1]
    vmem = pl.BlockSpec(memory_space=pltpu.VMEM)
    kernel = functools.partial(polar_kernel, blocks=len(block_list), pieces=pieces, chunk=256)
    return pl.pallas_call(
        kernel,
        out_shape=jax.ShapeDtypeStruct((own, dim), bf16),
        in_specs=[vmem] * len(block_list),
        out_specs=vmem,
        scratch_shapes=[
            pltpu.VMEM((dim, dim), bf16),
            pltpu.VMEM((dim, dim), f32),
            pltpu.VMEM((dim, dim), bf16),
            pltpu.VMEM((dim, dim), bf16),
            pltpu.VMEM((dim, dim), f32),
            pltpu.VMEM((dim, dim), bf16),
        ],
        compiler_params=pltpu.CompilerParams(vmem_limit_bytes=36 * MIB),
        name="polar",
    )(*block_list)


def share_kernel(*refs):
    total = refs[0][...].astype(f32)
    for part in refs[1:-1]:
        total = total + part[...].astype(f32)
    refs[-1][...] = total.astype(refs[-1].dtype)


def book_kernel(book_ref, *refs):
    sums, out_ref = refs[:-1], refs[-1]
    own = book_ref.shape[0]
    subs = sums[0].shape[0] - own
    width = own // subs
    total = sums[0][...].astype(f32)
    for part in sums[1:]:
        total = total + part[...].astype(f32)
    for m in range(subs):
        band = pl.ds(m * width, width)
        count = total[own + m : own + m + 1, :] + prior_weight
        part = total[m * width : (m + 1) * width, :]
        out_ref[band, :] = (part + prior_weight * book_ref[band, :]) / count


def small_call(kernel, name, shape, dtype, *operands, scratch=()):
    vmem = pl.BlockSpec(memory_space=pltpu.VMEM)
    return pl.pallas_call(
        kernel,
        out_shape=jax.ShapeDtypeStruct(shape, dtype),
        in_specs=[vmem] * len(operands),
        out_specs=vmem,
        scratch_shapes=scratch,
        compiler_params=pltpu.CompilerParams(vmem_limit_bytes=24 * MIB),
        name=name,
    )(*operands)


def swap(value, axis, size, mask, odd_mask=None):
    odd_mask = mask if odd_mask is None else odd_mask
    return lax.ppermute(value, axis, [(i, i ^ (odd_mask if i % 2 else mask)) for i in range(size)])


def make_body(dp, code):
    def body(residuals, codes, codebook):
        rows, dim = residuals.shape
        subs, words, width = codebook.shape
        own = subs * width
        codes_t = codes.T
        book_t = jnp.transpose(codebook, (0, 2, 1)).reshape(own, words)
        size = own // dp
        thin = size % 16 != 0
        if thin:
            place = lax.axis_index("dp")
            partial, codes_v, book_v, res_v = cross_partial(codes_t, book_t, residuals, None)
            cut = [
                lax.dynamic_slice_in_dim(partial, (place ^ k) * size, size, 0) for k in range(dp)
            ]
            parts = [cut[0]] + [part.astype(bf16) for part in cut[1:]]
        else:
            *parts, codes_v, book_v, res_v = cross_partial(codes_t, book_t, residuals, dp)
        far_first = range(dp - 1, 0, -1)
        got = [swap(parts[k], "dp", dp, k) for k in far_first]
        ready = onehot_call(codes_v, words, width)
        got, ready = lax.optimization_barrier((got, ready))
        piece = small_call(share_kernel, "share", (size, dim), bf16, parts[0], *got)
        pieces = {0: piece}
        for k in far_first:
            pieces[k] = swap(piece, "dp", dp, k)
        if thin:
            block = jnp.zeros((own, dim), bf16)
            for k in range(dp):
                block = lax.dynamic_update_slice_in_dim(block, pieces[k], (place ^ k) * size, 0)
            held = [block]
        else:
            half = max(dp // 2, 1)
            held = [
                jnp.concatenate([pieces[k] for k in range(at, min(at + half, dp))], axis=0)
                for at in range(0, dp, half)
            ]
        strides = [1 << b for b in reversed(range(code.bit_length() - 1))]
        far = strides[:-1]
        for even, odd in zip(far, far[::-1]):
            held = held + [swap(t, "code", code, even, odd) for t in held]
        for stride in strides[-1:]:
            held = held + [swap(t, "code", code, stride) for t in held]
        rotation_t = polar(held, own, 1 if thin else dp)
        scratch = [pltpu.VMEM((own, words), f32)]
        operands = (rotation_t, res_v, *ready)
        sums = small_call(sums_kernel, "sums", (own + subs, words), bf16, *operands, scratch=scratch)
        rotated = small_call(rotated_kernel, "rotated", (rows, own), f32, rotation_t, res_v)
        others = [swap(sums, "dp", dp, k) for k in range(1, dp)]
        book = small_call(book_kernel, "book", (own, words), f32, book_v, sums, *others)
        return rotated, jnp.transpose(book.reshape(subs, width, words), (0, 2, 1))

    return body


def solution(mesh):
    dp, code = mesh.shape["dp"], mesh.shape["code"]
    in_specs = (P("dp", None), P("dp", "code"), P("code", None, None))
    out_specs = (P("dp", "code"), P("code", None, None))
    return jax.shard_map(
        make_body(dp, code), mesh=mesh, in_specs=in_specs, out_specs=out_specs, check_vma=False
    )
```

profile of v0, /device:TPU:0, one launch (start us, length us, event | category | flops | bytes accessed | tf_op | source)
XLA Modules:
  0.0 59.7 jit_solution(11948874248700482548)
XLA Ops:
  0.6 2.7 %cross_partial.1 = (f32[32,1024]{1,0:T(8,128)S(1)}, bf16[32,1024]{1,0:T(8,128)(2,1)S(1)}, bf16[32,1024]{1,0:T(8,128)(2,1)S(1)}, bf16[32,1024]{1,0:T(8,128)(2,1)S...) custom-call(s32[16,2048]{1,0:T(8,128)} %bitcast.7, f32[128,256]{1,0:T(8,128)} %bitcast.8, ...), custom_call_target="tpu_custom_call" | custom-call | tf_op jit(solution)/shard_map/cross_partial/pallas_call | solution.py:86
  3.3 5.1 %collective-permute-start = (bf16[32,1024]{1,0:T(8,128)(2,1)S(1)}, bf16[32,1024]{1,0:T(8,128)(2,1)S(1)}, u32[]{:S(2)}, u32[]{:S(2)}) collective-permute-start(bf16[32,1024]{1,0:T(8,128)(2,1)S(1)} %get-tuple-element.19), channel_id=1, source_target_pairs={{0,24},{8,16},{16,8},{24,0},{1,25},{9,17},{17,9},{25,1},{2,26},{10... | collective-permute-start | bytes 196616 | tf_op jit(solution)/shard_map/ppermute | solution.py:323
  8.5 0.0 collective-permute-start.1
  8.5 0.6 %collective-permute-start.2 = (bf16[32,1024]{1,0:T(8,128)(2,1)S(1)}, bf16[32,1024]{1,0:T(8,128)(2,1)S(1)}, u32[]{:S(2)}, u32[]{:S(2)}) collective-permute-start(bf16[32,1024]{1,0:T(8,128)(2,1)S(1)} %get-tuple-element.21), channel_id=1, source_target_pairs={{0,8},{8,0},{16,24},{24,16},{1,9},{9,1},{17,25},{25,17},{2,10},{10... | collective-permute-start | bytes 196616 | tf_op jit(solution)/shard_map/ppermute | solution.py:323
  9.1 1.8 %onehot.1 = (bf16[2048,1024]{1,0:T(8,128)(2,1)S(1)}, bf16[512,2048]{1,0:T(8,128)(2,1)S(1)}, f32[16,256]{1,0:T(8,128)S(1)}) custom-call(s32[16,2048]{1,0:T(8,128)S(1)} %get-tuple-element.22.codes_ref), custom_call_target="tpu_custom_call" | custom-call | flops 1073741824 | bytes 4194304 | tf_op jit(solution)/shard_map/onehot/pallas_call | solution.py:212
  10.9 0.1 collective-permute-done.refs_1_
  11.1 3.0 %collective-permute-done.1.refs_2_ = bf16[32,1024]{1,0:T(8,128)(2,1)S(1)} collective-permute-done((bf16[32,1024]{1,0:T(8,128)(2,1)S(1)}, bf16[32,1024]{1,0:T(8,128)(2,1)S(1)}, u32[]{:S(2)}, u32[]{:S(2)}) %collective-permute-start.1) | collective-permute-done | bytes 65568 | tf_op jit(solution)/shard_map/ppermute | solution.py:323
  14.1 0.0 collective-permute-done.2.refs_3_
  14.1 1.1 %collective-permute-start.3 = (bf16[32,1024]{1,0:T(8,128)(2,1)S(1)}, bf16[32,1024]{1,0:T(8,128)(2,1)S(1)}, u32[]{:S(2)}, u32[]{:S(2)}) collective-permute-start(bf16[32,1024]{1,0:T(8,128)(2,1)S(1)} %share.1), channel_id=1, source_target_pairs={{0,8},{8,0},{16,24},{24,16},{1,9},{9,1},{17,25},{25,17},{2,10},{10... | collective-permute-start | bytes 196616 | tf_op jit(solution)/shard_map/ppermute | solution.py:323
  15.3 2.0 %collective-permute-start.5 = (bf16[32,1024]{1,0:T(8,128)(2,1)S(1)}, bf16[32,1024]{1,0:T(8,128)(2,1)S(1)}, u32[]{:S(2)}, u32[]{:S(2)}) collective-permute-start(bf16[32,1024]{1,0:T(8,128)(2,1)S(1)} %share.1), channel_id=1, source_target_pairs={{0,24},{8,16},{16,8},{24,0},{1,25},{9,17},{17,9},{25,1},{2,26},{10... | collective-permute-start | bytes 196616 | tf_op jit(solution)/shard_map/ppermute | solution.py:323
  17.2 0.4 collective-permute-start.4
  17.7 1.8 %collective-permute-done.3 = bf16[32,1024]{1,0:T(8,128)(2,1)S(1)} collective-permute-done((bf16[32,1024]{1,0:T(8,128)(2,1)S(1)}, bf16[32,1024]{1,0:T(8,128)(2,1)S(1)}, u32[]{:S(2)}, u32[]{:S(2)}) %collective-permute-start.3) | collective-permute-done | bytes 65568 | tf_op jit(solution)/shard_map/ppermute | solution.py:323
  19.5 0.1 collective-permute-start.12
  19.6 0.5 collective-permute-start.8
  20.1 1.5 %collective-permute-start.6 = (bf16[64,1024]{1,0:T(8,128)(2,1)S(1)}, bf16[64,1024]{1,0:T(8,128)(2,1)S(1)}, u32[]{:S(2)}, u32[]{:S(2)}) collective-permute-start(bf16[64,1024]{1,0:T(8,128)(2,1)S(1)} %pad_maximum_fusion.refs_0_), channel_id=1, source_target_pairs={{0,4},{1,3},{2,6},{3,1},{4,0},{5,7},{6,2},{7,5},{8,12},{9,11},{10,... | collective-permute-start | bytes 393224 | tf_op jit(solution)/shard_map/ppermute | solution.py:323
  21.6 1.6 %collective-permute-done.4 = bf16[32,1024]{1,0:T(8,128)(2,1)S(1)} collective-permute-done((bf16[32,1024]{1,0:T(8,128)(2,1)S(1)}, bf16[32,1024]{1,0:T(8,128)(2,1)S(1)}, u32[]{:S(2)}, u32[]{:S(2)}) %collective-permute-start.4) | collective-permute-done | bytes 65568 | tf_op jit(solution)/shard_map/ppermute | solution.py:323
  23.2 0.0 collective-permute-done.5
  23.3 1.8 %collective-permute-start.7 = (bf16[64,1024]{1,0:T(8,128)(2,1)S(1)}, bf16[64,1024]{1,0:T(8,128)(2,1)S(1)}, u32[]{:S(2)}, u32[]{:S(2)}) collective-permute-start(bf16[64,1024]{1,0:T(8,128)(2,1)S(1)} %constant_dynamic-update-slice_fusion.refs_1_), channel_id=1, source_target_pairs={{0,4},{1,3},{2,6},{3,1},{4,0},{5,7},{6,2},{7,5},{8,12},{9,11},{10,... | collective-permute-start | bytes 393224 | tf_op jit(solution)/shard_map/ppermute | solution.py:323
  25.0 0.0 collective-permute-start.13
  25.0 0.0 collective-permute-done.12.refs_8_
  25.0 1.5 %collective-permute-start.9 = (bf16[64,1024]{1,0:T(8,128)(2,1)S(1)}, bf16[64,1024]{1,0:T(8,128)(2,1)S(1)}, u32[]{:S(2)}, u32[]{:S(2)}) collective-permute-start(bf16[64,1024]{1,0:T(8,128)(2,1)S(1)} %constant_dynamic-update-slice_fusion.refs_1_), channel_id=1, source_target_pairs={{0,2},{1,5},{2,0},{3,7},{4,6},{5,1},{6,4},{7,3},{8,10},{9,13},{10,... | collective-permute-start | bytes 393224 | tf_op jit(solution)/shard_map/ppermute | solution.py:323
  26.5 0.0 collective-permute-done.8.refs_4_
  26.5 0.0 collective-permute-start.16
  26.5 0.0 collective-permute-done.6.refs_2_
  26.5 0.7 %collective-permute-start.10 = (bf16[64,1024]{1,0:T(8,128)(2,1)S(1)}, bf16[64,1024]{1,0:T(8,128)(2,1)S(1)}, u32[]{:S(2)}, u32[]{:S(2)}) collective-permute-start(bf16[64,1024]{1,0:T(8,128)(2,1)S(1)} %collective-permute-done.6.refs_2_), channel_id=1, source_target_pairs={{0,2},{1,5},{2,0},{3,7},{4,6},{5,1},{6,4},{7,3},{8,10},{9,13},{10,... | collective-permute-start | bytes 393224 | tf_op jit(solution)/shard_map/ppermute | solution.py:323
  27.3 1.6 %collective-permute-done.7.refs_3_ = bf16[64,1024]{1,0:T(8,128)(2,1)S(1)} collective-permute-done((bf16[64,1024]{1,0:T(8,128)(2,1)S(1)}, bf16[64,1024]{1,0:T(8,128)(2,1)S(1)}, u32[]{:S(2)}, u32[]{:S(2)}) %collective-permute-start.7) | collective-permute-done | bytes 131104 | tf_op jit(solution)/shard_map/ppermute | solution.py:323
  28.9 1.4 %collective-permute-start.11 = (bf16[64,1024]{1,0:T(8,128)(2,1)S(1)}, bf16[64,1024]{1,0:T(8,128)(2,1)S(1)}, u32[]{:S(2)}, u32[]{:S(2)}) collective-permute-start(bf16[64,1024]{1,0:T(8,128)(2,1)S(1)} %collective-permute-done.7.refs_3_), channel_id=1, source_target_pairs={{0,2},{1,5},{2,0},{3,7},{4,6},{5,1},{6,4},{7,3},{8,10},{9,13},{10,... | collective-permute-start | bytes 393224 | tf_op jit(solution)/shard_map/ppermute | solution.py:323
  30.4 0.0 collective-permute-done.13.refs_9_
  30.4 0.0 collective-permute-start.14
  30.4 0.0 collective-permute-done.9.refs_5_
  30.4 0.5 collective-permute-start.15
  30.9 0.0 collective-permute-done.16.refs_12_
  30.9 0.1 collective-permute-start.17
  30.9 0.6 %collective-permute-done.10.refs_6_ = bf16[64,1024]{1,0:T(8,128)(2,1)S(1)} collective-permute-done((bf16[64,1024]{1,0:T(8,128)(2,1)S(1)}, bf16[64,1024]{1,0:T(8,128)(2,1)S(1)}, u32[]{:S(2)}, u32[]{:S(2)}) %collective-permute-start.10) | collective-permute-done | bytes 131104 | tf_op jit(solution)/shard_map/ppermute | solution.py:323
  31.6 0.0 collective-permute-start.18
  31.6 2.3 %collective-permute-done.11.refs_7_ = bf16[64,1024]{1,0:T(8,128)(2,1)S(1)} collective-permute-done((bf16[64,1024]{1,0:T(8,128)(2,1)S(1)}, bf16[64,1024]{1,0:T(8,128)(2,1)S(1)}, u32[]{:S(2)}, u32[]{:S(2)}) %collective-permute-start.11) | collective-permute-done | bytes 131104 | tf_op jit(solution)/shard_map/ppermute | solution.py:323
  33.9 0.0 collective-permute-start.19
  33.9 0.0 collective-permute-done.14.refs_10_
  33.9 0.0 collective-permute-done.17.refs_13_
  33.9 0.0 collective-permute-done.15.refs_11_
  33.9 0.0 collective-permute-done.18.refs_14_
  33.9 1.3 %collective-permute-done.19.refs_15_ = bf16[64,1024]{1,0:T(8,128)(2,1)S(1)} collective-permute-done((bf16[64,1024]{1,0:T(8,128)(2,1)S(1)}, bf16[64,1024]{1,0:T(8,128)(2,1)S(1)}, u32[]{:S(2)}, u32[]{:S(2)}) %collective-permute-start.19) | collective-permute-done | bytes 131104 | tf_op jit(solution)/shard_map/ppermute | solution.py:323
  35.2 12.2 %polar.1.rot_ref = bf16[128,1024]{1,0:T(8,128)(2,1)S(1)} custom-call(bf16[64,1024]{1,0:T(8,128)(2,1)S(1)} %pad_maximum_fusion.refs_0_, bf16[64,1024]{1,0:T(8,128)(2,1)S(1)} %constant_dynamic-update-slice_fusion.refs_1_, bf16[64,1024]{1,0:T(8,128)(2,1)S(1)} %collective-permute-done.6.refs_2_, bf16[64,1024]{1,0:T(8,128)(2,1)S(1)} %collective-permute-done.7.refs_3_, ...), custom_call_target="tpu_custom_call" | custom-call | tf_op jit(solution)/shard_map/polar/pallas_call | solution.py:268
  47.4 2.1 %sums.1.refs_0_ = bf16[144,256]{1,0:T(8,128)(2,1)S(1)} custom-call(bf16[128,1024]{1,0:T(8,128)(2,1)S(1)} %polar.1.rot_ref, bf16[2048,1024]{1,0:T(8,128)(2,1)S(1)} %get-tuple-element.29.res_ref, bf16[2048,1024]{1,0:T(8,128)(2,1)S(1)} %get-tuple-element.31.onehot_ref, bf16[512,2048]{1,0:T(8,128)(2,1)S(1)} %get-tuple-element.32.masks_ref, ...), custom_call_target="tpu_custom_call" | custom-call | tf_op jit(solution)/shard_map/sums/pallas_call | solution.py:310
  49.6 2.0 %collective-permute-start.22 = (bf16[144,256]{1,0:T(8,128)(2,1)S(1)}, bf16[144,256]{1,0:T(8,128)(2,1)S(1)}, u32[]{:S(2)}, u32[]{:S(2)}) collective-permute-start(bf16[144,256]{1,0:T(8,128)(2,1)S(1)} %sums.1.refs_0_), channel_id=1, source_target_pairs={{0,24},{8,16},{16,8},{24,0},{1,25},{9,17},{17,9},{25,1},{2,26},{10... | collective-permute-start | bytes 221192 | tf_op jit(solution)/shard_map/ppermute | solution.py:323
  51.6 0.0 collective-permute-start.21
  51.6 2.5 %collective-permute-start.20 = (bf16[144,256]{1,0:T(8,128)(2,1)S(1)}, bf16[144,256]{1,0:T(8,128)(2,1)S(1)}, u32[]{:S(2)}, u32[]{:S(2)}) collective-permute-start(bf16[144,256]{1,0:T(8,128)(2,1)S(1)} %sums.1.refs_0_), channel_id=1, source_target_pairs={{0,8},{8,0},{16,24},{24,16},{1,9},{9,1},{17,25},{25,17},{2,10},{10... | collective-permute-start | bytes 221192 | tf_op jit(solution)/shard_map/ppermute | solution.py:323
  54.1 2.7 %rotated.1 = f32[2048,128]{1,0:T(8,128)} custom-call(bf16[128,1024]{1,0:T(8,128)(2,1)S(1)} %polar.1.rot_ref, bf16[2048,1024]{1,0:T(8,128)(2,1)S(1)} %get-tuple-element.29.res_ref), custom_call_target="tpu_custom_call" | custom-call | tf_op jit(solution)/shard_map/rotated/pallas_call | solution.py:310
  56.8 0.0 collective-permute-done.22.refs_3_
  56.8 2.2 %collective-permute-done.21.refs_2_ = bf16[144,256]{1,0:T(8,128)(2,1)S(1)} collective-permute-done((bf16[144,256]{1,0:T(8,128)(2,1)S(1)}, bf16[144,256]{1,0:T(8,128)(2,1)S(1)}, u32[]{:S(2)}, u32[]{:S(2)}) %collective-permute-start.21) | collective-permute-done | bytes 73760 | tf_op jit(solution)/shard_map/ppermute | solution.py:323
  58.9 0.0 collective-permute-done.20.refs_1_
  58.9 0.7 %book.1 = f32[128,256]{1,0:T(8,128)} custom-call(f32[128,256]{1,0:T(8,128)S(1)} %get-tuple-element.30.book_ref, bf16[144,256]{1,0:T(8,128)(2,1)S(1)} %sums.1.refs_0_, bf16[144,256]{1,0:T(8,128)(2,1)S(1)} %collective-permute-done.20.refs_1_, bf16[144,256]{1,0:T(8,128)(2,1)S(1)} %collective-permute-done.21.refs_2_, ...), custom_call_target="tpu_custom_call" | custom-call | tf_op jit(solution)/shard_map/book/pallas_call | solution.py:310
  (4 shorter events, 0.1 us)
Async XLA Ops:
  3.3 7.7 %collective-permute-start = (bf16[32,1024]{1,0:T(8,128)(2,1)S(1)}, bf16[32,1024]{1,0:T(8,128)(2,1)S(1)}, u32[]{:S(2)}, u32[]{:S(2)}) collective-permute-start(bf16[32,1024]{1,0:T(8,128)(2,1)S(1)} %get-tuple-element.19), channel_id=1, source_target_pairs={{0,24},{8,16},{16,8},{24,0},{1,25},{9,17},{17,9},{25,1},{2,26},{10... | collective-permute-start | bytes 196616 | tf_op jit(solution)/shard_map/ppermute | solution.py:323
  8.5 5.6 %collective-permute-start.1 = (bf16[32,1024]{1,0:T(8,128)(2,1)S(1)}, bf16[32,1024]{1,0:T(8,128)(2,1)S(1)}, u32[]{:S(2)}, u32[]{:S(2)}) collective-permute-start(bf16[32,1024]{1,0:T(8,128)(2,1)S(1)} %get-tuple-element.20), channel_id=1, source_target_pairs={{0,16},{8,24},{16,0},{24,8},{1,17},{9,25},{17,1},{25,9},{2,18},{10... | collective-permute-start | bytes 196616 | tf_op jit(solution)/shard_map/ppermute | solution.py:323
  8.5 5.6 %collective-permute-start.2 = (bf16[32,1024]{1,0:T(8,128)(2,1)S(1)}, bf16[32,1024]{1,0:T(8,128)(2,1)S(1)}, u32[]{:S(2)}, u32[]{:S(2)}) collective-permute-start(bf16[32,1024]{1,0:T(8,128)(2,1)S(1)} %get-tuple-element.21), channel_id=1, source_target_pairs={{0,8},{8,0},{16,24},{24,16},{1,9},{9,1},{17,25},{25,17},{2,10},{10... | collective-permute-start | bytes 196616 | tf_op jit(solution)/shard_map/ppermute | solution.py:323
  14.1 5.4 %collective-permute-start.3 = (bf16[32,1024]{1,0:T(8,128)(2,1)S(1)}, bf16[32,1024]{1,0:T(8,128)(2,1)S(1)}, u32[]{:S(2)}, u32[]{:S(2)}) collective-permute-start(bf16[32,1024]{1,0:T(8,128)(2,1)S(1)} %share.1), channel_id=1, source_target_pairs={{0,8},{8,0},{16,24},{24,16},{1,9},{9,1},{17,25},{25,17},{2,10},{10... | collective-permute-start | bytes 196616 | tf_op jit(solution)/shard_map/ppermute | solution.py:323
  15.3 8.0 %collective-permute-start.5 = (bf16[32,1024]{1,0:T(8,128)(2,1)S(1)}, bf16[32,1024]{1,0:T(8,128)(2,1)S(1)}, u32[]{:S(2)}, u32[]{:S(2)}) collective-permute-start(bf16[32,1024]{1,0:T(8,128)(2,1)S(1)} %share.1), channel_id=1, source_target_pairs={{0,24},{8,16},{16,8},{24,0},{1,25},{9,17},{17,9},{25,1},{2,26},{10... | collective-permute-start | bytes 196616 | tf_op jit(solution)/shard_map/ppermute | solution.py:323
  17.2 6.0 %collective-permute-start.4 = (bf16[32,1024]{1,0:T(8,128)(2,1)S(1)}, bf16[32,1024]{1,0:T(8,128)(2,1)S(1)}, u32[]{:S(2)}, u32[]{:S(2)}) collective-permute-start(bf16[32,1024]{1,0:T(8,128)(2,1)S(1)} %share.1), channel_id=1, source_target_pairs={{0,16},{8,24},{16,0},{24,8},{1,17},{9,25},{17,1},{25,9},{2,18},{10... | collective-permute-start | bytes 196616 | tf_op jit(solution)/shard_map/ppermute | solution.py:323
  19.5 5.6 %collective-permute-start.12 = (bf16[64,1024]{1,0:T(8,128)(2,1)S(1)}, bf16[64,1024]{1,0:T(8,128)(2,1)S(1)}, u32[]{:S(2)}, u32[]{:S(2)}) collective-permute-start(bf16[64,1024]{1,0:T(8,128)(2,1)S(1)} %pad_maximum_fusion.refs_0_), channel_id=1, source_target_pairs={{0,1},{1,0},{2,3},{3,2},{4,5},{5,4},{6,7},{7,6},{8,9},{9,8},{10,11... | collective-permute-start | bytes 393224 | tf_op jit(solution)/shard_map/ppermute | solution.py:323
  19.6 7.0 %collective-permute-start.8 = (bf16[64,1024]{1,0:T(8,128)(2,1)S(1)}, bf16[64,1024]{1,0:T(8,128)(2,1)S(1)}, u32[]{:S(2)}, u32[]{:S(2)}) collective-permute-start(bf16[64,1024]{1,0:T(8,128)(2,1)S(1)} %pad_maximum_fusion.refs_0_), channel_id=1, source_target_pairs={{0,2},{1,5},{2,0},{3,7},{4,6},{5,1},{6,4},{7,3},{8,10},{9,13},{10,... | collective-permute-start | bytes 393224 | tf_op jit(solution)/shard_map/ppermute | solution.py:323
  20.1 6.4 %collective-permute-start.6 = (bf16[64,1024]{1,0:T(8,128)(2,1)S(1)}, bf16[64,1024]{1,0:T(8,128)(2,1)S(1)}, u32[]{:S(2)}, u32[]{:S(2)}) collective-permute-start(bf16[64,1024]{1,0:T(8,128)(2,1)S(1)} %pad_maximum_fusion.refs_0_), channel_id=1, source_target_pairs={{0,4},{1,3},{2,6},{3,1},{4,0},{5,7},{6,2},{7,5},{8,12},{9,11},{10,... | collective-permute-start | bytes 393224 | tf_op jit(solution)/shard_map/ppermute | solution.py:323
  23.3 5.6 %collective-permute-start.7 = (bf16[64,1024]{1,0:T(8,128)(2,1)S(1)}, bf16[64,1024]{1,0:T(8,128)(2,1)S(1)}, u32[]{:S(2)}, u32[]{:S(2)}) collective-permute-start(bf16[64,1024]{1,0:T(8,128)(2,1)S(1)} %constant_dynamic-update-slice_fusion.refs_1_), channel_id=1, source_target_pairs={{0,4},{1,3},{2,6},{3,1},{4,0},{5,7},{6,2},{7,5},{8,12},{9,11},{10,... | collective-permute-start | bytes 393224 | tf_op jit(solution)/shard_map/ppermute | solution.py:323
  25.0 5.3 %collective-permute-start.13 = (bf16[64,1024]{1,0:T(8,128)(2,1)S(1)}, bf16[64,1024]{1,0:T(8,128)(2,1)S(1)}, u32[]{:S(2)}, u32[]{:S(2)}) collective-permute-start(bf16[64,1024]{1,0:T(8,128)(2,1)S(1)} %constant_dynamic-update-slice_fusion.refs_1_), channel_id=1, source_target_pairs={{0,1},{1,0},{2,3},{3,2},{4,5},{5,4},{6,7},{7,6},{8,9},{9,8},{10,11... | collective-permute-start | bytes 393224 | tf_op jit(solution)/shard_map/ppermute | solution.py:323
  25.0 5.3 %collective-permute-start.9 = (bf16[64,1024]{1,0:T(8,128)(2,1)S(1)}, bf16[64,1024]{1,0:T(8,128)(2,1)S(1)}, u32[]{:S(2)}, u32[]{:S(2)}) collective-permute-start(bf16[64,1024]{1,0:T(8,128)(2,1)S(1)} %constant_dynamic-update-slice_fusion.refs_1_), channel_id=1, source_target_pairs={{0,2},{1,5},{2,0},{3,7},{4,6},{5,1},{6,4},{7,3},{8,10},{9,13},{10,... | collective-permute-start | bytes 393224 | tf_op jit(solution)/shard_map/ppermute | solution.py:323
  26.5 4.3 %collective-permute-start.16 = (bf16[64,1024]{1,0:T(8,128)(2,1)S(1)}, bf16[64,1024]{1,0:T(8,128)(2,1)S(1)}, u32[]{:S(2)}, u32[]{:S(2)}) collective-permute-start(bf16[64,1024]{1,0:T(8,128)(2,1)S(1)} %collective-permute-done.8.refs_4_), channel_id=1, source_target_pairs={{0,1},{1,0},{2,3},{3,2},{4,5},{5,4},{6,7},{7,6},{8,9},{9,8},{10,11... | collective-permute-start | bytes 393224 | tf_op jit(solution)/shard_map/ppermute | solution.py:323
  26.5 5.0 %collective-permute-start.10 = (bf16[64,1024]{1,0:T(8,128)(2,1)S(1)}, bf16[64,1024]{1,0:T(8,128)(2,1)S(1)}, u32[]{:S(2)}, u32[]{:S(2)}) collective-permute-start(bf16[64,1024]{1,0:T(8,128)(2,1)S(1)} %collective-permute-done.6.refs_2_), channel_id=1, source_target_pairs={{0,2},{1,5},{2,0},{3,7},{4,6},{5,1},{6,4},{7,3},{8,10},{9,13},{10,... | collective-permute-start | bytes 393224 | tf_op jit(solution)/shard_map/ppermute | solution.py:323
  28.9 5.0 %collective-permute-start.11 = (bf16[64,1024]{1,0:T(8,128)(2,1)S(1)}, bf16[64,1024]{1,0:T(8,128)(2,1)S(1)}, u32[]{:S(2)}, u32[]{:S(2)}) collective-permute-start(bf16[64,1024]{1,0:T(8,128)(2,1)S(1)} %collective-permute-done.7.refs_3_), channel_id=1, source_target_pairs={{0,2},{1,5},{2,0},{3,7},{4,6},{5,1},{6,4},{7,3},{8,10},{9,13},{10,... | collective-permute-start | bytes 393224 | tf_op jit(solution)/shard_map/ppermute | solution.py:323
  30.4 3.5 %collective-permute-start.14 = (bf16[64,1024]{1,0:T(8,128)(2,1)S(1)}, bf16[64,1024]{1,0:T(8,128)(2,1)S(1)}, u32[]{:S(2)}, u32[]{:S(2)}) collective-permute-start(bf16[64,1024]{1,0:T(8,128)(2,1)S(1)} %collective-permute-done.6.refs_2_), channel_id=1, source_target_pairs={{0,1},{1,0},{2,3},{3,2},{4,5},{5,4},{6,7},{7,6},{8,9},{9,8},{10,11... | collective-permute-start | bytes 393224 | tf_op jit(solution)/shard_map/ppermute | solution.py:323
  30.4 3.5 %collective-permute-start.15 = (bf16[64,1024]{1,0:T(8,128)(2,1)S(1)}, bf16[64,1024]{1,0:T(8,128)(2,1)S(1)}, u32[]{:S(2)}, u32[]{:S(2)}) collective-permute-start(bf16[64,1024]{1,0:T(8,128)(2,1)S(1)} %collective-permute-done.7.refs_3_), channel_id=1, source_target_pairs={{0,1},{1,0},{2,3},{3,2},{4,5},{5,4},{6,7},{7,6},{8,9},{9,8},{10,11... | collective-permute-start | bytes 393224 | tf_op jit(solution)/shard_map/ppermute | solution.py:323
  30.9 3.0 %collective-permute-start.17 = (bf16[64,1024]{1,0:T(8,128)(2,1)S(1)}, bf16[64,1024]{1,0:T(8,128)(2,1)S(1)}, u32[]{:S(2)}, u32[]{:S(2)}) collective-permute-start(bf16[64,1024]{1,0:T(8,128)(2,1)S(1)} %collective-permute-done.9.refs_5_), channel_id=1, source_target_pairs={{0,1},{1,0},{2,3},{3,2},{4,5},{5,4},{6,7},{7,6},{8,9},{9,8},{10,11... | collective-permute-start | bytes 393224 | tf_op jit(solution)/shard_map/ppermute | solution.py:323
  31.6 2.3 %collective-permute-start.18 = (bf16[64,1024]{1,0:T(8,128)(2,1)S(1)}, bf16[64,1024]{1,0:T(8,128)(2,1)S(1)}, u32[]{:S(2)}, u32[]{:S(2)}) collective-permute-start(bf16[64,1024]{1,0:T(8,128)(2,1)S(1)} %collective-permute-done.10.refs_6_), channel_id=1, source_target_pairs={{0,1},{1,0},{2,3},{3,2},{4,5},{5,4},{6,7},{7,6},{8,9},{9,8},{10,11... | collective-permute-start | bytes 393224 | tf_op jit(solution)/shard_map/ppermute | solution.py:323
  33.9 1.3 %collective-permute-start.19 = (bf16[64,1024]{1,0:T(8,128)(2,1)S(1)}, bf16[64,1024]{1,0:T(8,128)(2,1)S(1)}, u32[]{:S(2)}, u32[]{:S(2)}) collective-permute-start(bf16[64,1024]{1,0:T(8,128)(2,1)S(1)} %collective-permute-done.11.refs_7_), channel_id=1, source_target_pairs={{0,1},{1,0},{2,3},{3,2},{4,5},{5,4},{6,7},{7,6},{8,9},{9,8},{10,11... | collective-permute-start | bytes 393224 | tf_op jit(solution)/shard_map/ppermute | solution.py:323
  49.6 7.2 %collective-permute-start.22 = (bf16[144,256]{1,0:T(8,128)(2,1)S(1)}, bf16[144,256]{1,0:T(8,128)(2,1)S(1)}, u32[]{:S(2)}, u32[]{:S(2)}) collective-permute-start(bf16[144,256]{1,0:T(8,128)(2,1)S(1)} %sums.1.refs_0_), channel_id=1, source_target_pairs={{0,24},{8,16},{16,8},{24,0},{1,25},{9,17},{17,9},{25,1},{2,26},{10... | collective-permute-start | bytes 221192 | tf_op jit(solution)/shard_map/ppermute | solution.py:323
  51.6 7.3 %collective-permute-start.21 = (bf16[144,256]{1,0:T(8,128)(2,1)S(1)}, bf16[144,256]{1,0:T(8,128)(2,1)S(1)}, u32[]{:S(2)}, u32[]{:S(2)}) collective-permute-start(bf16[144,256]{1,0:T(8,128)(2,1)S(1)} %sums.1.refs_0_), channel_id=1, source_target_pairs={{0,16},{8,24},{16,0},{24,8},{1,17},{9,25},{17,1},{25,9},{2,18},{10... | collective-permute-start | bytes 221192 | tf_op jit(solution)/shard_map/ppermute | solution.py:323
  51.6 7.3 %collective-permute-start.20 = (bf16[144,256]{1,0:T(8,128)(2,1)S(1)}, bf16[144,256]{1,0:T(8,128)(2,1)S(1)}, u32[]{:S(2)}, u32[]{:S(2)}) collective-permute-start(bf16[144,256]{1,0:T(8,128)(2,1)S(1)} %sums.1.refs_0_), channel_id=1, source_target_pairs={{0,8},{8,0},{16,24},{24,16},{1,9},{9,1},{17,25},{25,17},{2,10},{10... | collective-permute-start | bytes 221192 | tf_op jit(solution)/shard_map/ppermute | solution.py:323
where the time goes:
time: 59.8 us; the launch traced here: 59.7 us
  Pallas kernels  22.3 us (37%)
  starting transfers between devices  21.9 us (37%)
  waiting for transfers between devices  14.7 us (25%)
  between operations  0.73 us (1%)
    ppermute x23, starting transfers between devices, swap(): lax.ppermute(value, axis, [(i, i ^ (odd_mask if i % 2 else mask)) for i i...  21.9 us
    ppermute x23, waiting for transfers between devices, swap(): lax.ppermute(value, axis, [(i, i ^ (odd_mask if i % 2 else mask)) for i i...  14.7 us
    pallas_call x1, Pallas kernels, polar(): pl.pallas_call(kernel, out_shape=jax.ShapeDtypeStruct((own, dim), bf16),...  12.2 us
    pallas_call x4, Pallas kernels, small_call(): pl.pallas_call(kernel, out_shape=jax.ShapeDtypeStruct(shape, dtype), in_s...  5.61 us
    pallas_call x1, Pallas kernels, cross_partial(): pl.pallas_call(functools.partial(cross_kernel, dp=dp), out_shape=shapes,...  2.71 us
    pallas_call x1, Pallas kernels, onehot_call(): pl.pallas_call(onehot_kernel, out_shape=(jax.ShapeDtypeStruct((rows, subs...  1.83 us
  transfers between devices with their start and end apart: 23, of which 9 were waited for; matrix products, arithmetic and copies ran while one was open for 0% of the time, Pallas kernels for 8%

commit v1 on v0

--- a/solution.py
+++ b/solution.py
@@ -101,7 +101,7 @@
 def polar_kernel(*refs, blocks, pieces, chunk):
     block_refs = refs[:blocks]
     rot_b = refs[blocks]
-    raw, gram, gram_b, poly_b, iterate, iterate_b = refs[blocks + 1 :]
+    raw, gram, gram_b, poly_b, iterate, iterate_b, turned = refs[blocks + 1 :]
     dim = raw.shape[0]
     own = rot_b.shape[0]
     steps = dim // chunk
@@ -123,13 +123,16 @@
             at = (i - j) * chunk
             target[cols, pl.ds(i * chunk, chunk)] = value[at : at + chunk, :].T.astype(bf16)
 
-    def gram_of(source):
+    def gram_of(source, transposed=None):
         r = lax.broadcasted_iota(jnp.int32, (chunk, chunk), 0)
         c = lax.broadcasted_iota(jnp.int32, (chunk, chunk), 1)
         trace = jnp.zeros((), f32)
         for j in range(steps):
             rows, cols = lower(j)
-            part = dot_nt(source[rows, :], source[cols, :])
+            if transposed is None:
+                part = dot_nt(source[rows, :], source[cols, :])
+            else:
+                part = dot(source[rows, :], transposed[:, cols])
             gram[rows, cols] = part
             mirror(gram_b, j, part)
             trace = trace + jnp.sum(jnp.where(r == c, part[:chunk, :], 0.0))
@@ -150,21 +153,25 @@
         cols = band_of(i)
         value = scale * (quintic_a * raw[:, cols].astype(f32) + dot(poly_b[...], raw[:, cols]))
         iterate[:, cols] = value
-        iterate_b[:, cols] = value.astype(bf16)
-
-    gram_of(iterate_b)
+        rounded = value.astype(bf16)
+        iterate_b[:, cols] = rounded
+        turned[cols, :] = rounded.T
+
+    gram_of(iterate_b, turned)
     poly_of(quintic_b, quintic_c)
 
     for i in range(steps):
         cols = band_of(i)
         value = quintic_a * iterate[:, cols] + dot(poly_b[...], iterate_b[:, cols])
         iterate[pl.ds(0, own), cols] = value[:own, :]
-        raw[:, cols] = value.astype(bf16)
+        rounded = value.astype(bf16)
+        raw[:, cols] = rounded
+        turned[cols, :] = rounded.T
 
     mine = pl.ds(0, own)
-    g = dot_nt(raw[mine, :], raw[...])
+    g = dot(raw[mine, :], turned[...])
     image = dot(g.astype(bf16), raw[...])
-    square = dot_nt(image.astype(bf16), raw[...])
+    square = dot(image.astype(bf16), turned[...])
     last = quintic_a * iterate[mine, :] + dot(
         (quintic_b * g + quintic_c * square).astype(bf16), raw[...]
     )
@@ -179,8 +186,12 @@
 LOWS = 64
 
 
-def onehot_kernel(codes_ref, onehot_ref, masks_ref, counts_ref):
+def onehot_kernel(codes_ref, res_ref, onehot_ref, masks_ref, counts_ref, turned_ref):
     subs, rows_all = codes_ref.shape
+    step = 256
+    for i in range(rows_all // step):
+        rows = pl.ds(i * step, step)
+        turned_ref[:, rows] = res_ref[rows, :].T
     highs = counts_ref.shape[1] // LOWS
     wide = masks_ref.shape[0] // subs
     group = min(subs, 256 // LOWS)
@@ -206,7 +217,7 @@
                 ]
 
 
-def onehot_call(codes_t, words, width):
+def onehot_call(codes_t, residuals, words, width):
     subs, rows = codes_t.shape
     vmem = pl.BlockSpec(memory_space=pltpu.VMEM)
     return pl.pallas_call(
@@ -215,15 +226,16 @@
             jax.ShapeDtypeStruct((rows, subs * LOWS), bf16),
             jax.ShapeDtypeStruct((subs * width * (words // LOWS), rows), bf16),
             jax.ShapeDtypeStruct((subs, words), f32),
+            jax.ShapeDtypeStruct(residuals.shape[::-1], bf16),
         ),
-        in_specs=[vmem],
-        out_specs=(vmem, vmem, vmem),
+        in_specs=[vmem, vmem],
+        out_specs=(vmem,) * 4,
         compiler_params=pltpu.CompilerParams(vmem_limit_bytes=24 * MIB),
         cost_estimate=pl.CostEstimate(
             flops=2 * 256 * subs * LOWS * rows, bytes_accessed=2 * subs * LOWS * rows, transcendentals=0
         ),
         name="onehot",
-    )(codes_t)
+    )(codes_t, residuals)
 
 
 def sums_kernel(rot_ref, res_ref, onehot_ref, masks_ref, counts_ref, sent_ref, sums_ref):
@@ -232,7 +244,7 @@
     width = own // subs
     highs = words // LOWS
     group = min(subs, 256 // LOWS)
-    rot_t = dot_nt(rot_ref[...], res_ref[...])
+    rot_t = dot(rot_ref[...], res_ref[...])
     for first in range(0, subs, group):
         values = []
         for m in range(first, first + group):
@@ -277,8 +289,9 @@
             pltpu.VMEM((dim, dim), bf16),
             pltpu.VMEM((dim, dim), f32),
             pltpu.VMEM((dim, dim), bf16),
+            pltpu.VMEM((dim, dim), bf16),
         ],
-        compiler_params=pltpu.CompilerParams(vmem_limit_bytes=36 * MIB),
+        compiler_params=pltpu.CompilerParams(vmem_limit_bytes=30 * MIB),
         name="polar",
     )(*block_list)
 
@@ -343,8 +356,8 @@
             *parts, codes_v, book_v, res_v = cross_partial(codes_t, book_t, residuals, dp)
         far_first = range(dp - 1, 0, -1)
         got = [swap(parts[k], "dp", dp, k) for k in far_first]
-        ready = onehot_call(codes_v, words, width)
-        got, ready = lax.optimization_barrier((got, ready))
+        *ready, res_t = onehot_call(codes_v, res_v, words, width)
+        got, ready, res_t = lax.optimization_barrier((got, ready, res_t))
         piece = small_call(share_kernel, "share", (size, dim), bf16, parts[0], *got)
         pieces = {0: piece}
         for k in far_first:
@@ -368,7 +381,7 @@
             held = held + [swap(t, "code", code, stride) for t in held]
         rotation_t = polar(held, own, 1 if thin else dp)
         scratch = [pltpu.VMEM((own, words), f32)]
-        operands = (rotation_t, res_v, *ready)
+        operands = (rotation_t, res_t, *ready)
         sums = small_call(sums_kernel, "sums", (own + subs, words), bf16, *operands, scratch=scratch)
         rotated = small_call(rotated_kernel, "rotated", (rows, own), f32, rotation_t, res_v)
         others = [swap(sums, "dp", dp, k) for k in range(1, dp)]

time: 59.8 us -> 58.4 us (0.977)
  waiting for transfers between devices: 14.7 us -> 13.5 us
    ppermute x23, waiting for transfers between devices: 14.7 us -> 13.5 us  [swap(): lax.ppermute(value, axis, [(i, i ^ (odd_mask if i % 2 else mask)) for i i...]
    pallas_call x1, Pallas kernels: 1.83 us -> 2.99 us  [onehot_call(): pl.pallas_call(onehot_kernel, out_shape=(jax.ShapeDtypeStruct((rows, subs...]
    pallas_call x1, Pallas kernels: 12.2 us -> 11.5 us  [polar(): pl.pallas_call(kernel, out_shape=jax.ShapeDtypeStruct((own, dim), bf16),...]
    pallas_call x4, Pallas kernels: 5.61 us -> 4.89 us  [small_call(): pl.pallas_call(kernel, out_shape=jax.ShapeDtypeStruct(shape, dtype), in_s...]
  transfers between devices with their start and end apart: 23 -> 23, of which waited for: 9 -> 8; matrix products, arithmetic and copies ran while one was open for 0% -> 0% of each run, Pallas kernels for 8% -> 10%
where the time goes in v1:
time: 58.4 us; the launch traced here: 58.2 us
  Pallas kernels  22.1 us (38%)
  starting transfers between devices  21.9 us (38%)
  waiting for transfers between devices  13.5 us (23%)
  between operations  0.74 us (1%)
    ppermute x23, starting transfers between devices, swap(): lax.ppermute(value, axis, [(i, i ^ (odd_mask if i % 2 else mask)) for i i...  21.9 us
    ppermute x23, waiting for transfers between devices, swap(): lax.ppermute(value, axis, [(i, i ^ (odd_mask if i % 2 else mask)) for i i...  13.5 us
    pallas_call x1, Pallas kernels, polar(): pl.pallas_call(kernel, out_shape=jax.ShapeDtypeStruct((own, dim), bf16),...  11.5 us
    pallas_call x4, Pallas kernels, small_call(): pl.pallas_call(kernel, out_shape=jax.ShapeDtypeStruct(shape, dtype), in_s...  4.89 us
    pallas_call x1, Pallas kernels, onehot_call(): pl.pallas_call(onehot_kernel, out_shape=(jax.ShapeDtypeStruct((rows, subs...  2.99 us
    pallas_call x1, Pallas kernels, cross_partial(): pl.pallas_call(functools.partial(cross_kernel, dp=dp), out_shape=shapes,...  2.71 us
  transfers between devices with their start and end apart: 23, of which 8 were waited for; matrix products, arithmetic and copies ran while one was open for 0% of the time, Pallas kernels for 10%

profile of v1, /device:TPU:0, one launch (start us, length us, event | category | flops | bytes accessed | tf_op | source)
XLA Modules:
  0.0 58.2 jit_solution(17335548097663527112)
XLA Ops:
  0.6 2.7 %cross_partial.1 = (f32[32,1024]{1,0:T(8,128)S(1)}, bf16[32,1024]{1,0:T(8,128)(2,1)S(1)}, bf16[32,1024]{1,0:T(8,128)(2,1)S(1)}, bf16[32,1024]{1,0:T(8,128)(2,1)S...) custom-call(s32[16,2048]{1,0:T(8,128)} %bitcast.7, f32[128,256]{1,0:T(8,128)} %bitcast.8, ...), custom_call_target="tpu_custom_call" | custom-call | tf_op jit(solution)/shard_map/cross_partial/pallas_call | solution.py:86
  3.3 5.1 %collective-permute-start = (bf16[32,1024]{1,0:T(8,128)(2,1)S(1)}, bf16[32,1024]{1,0:T(8,128)(2,1)S(1)}, u32[]{:S(2)}, u32[]{:S(2)}) collective-permute-start(bf16[32,1024]{1,0:T(8,128)(2,1)S(1)} %get-tuple-element.21), channel_id=1, source_target_pairs={{0,24},{8,16},{16,8},{24,0},{1,25},{9,17},{17,9},{25,1},{2,26},{10... | collective-permute-start | bytes 196616 | tf_op jit(solution)/shard_map/ppermute | solution.py:336
  8.5 0.0 collective-permute-start.1
  8.5 0.6 %collective-permute-start.2 = (bf16[32,1024]{1,0:T(8,128)(2,1)S(1)}, bf16[32,1024]{1,0:T(8,128)(2,1)S(1)}, u32[]{:S(2)}, u32[]{:S(2)}) collective-permute-start(bf16[32,1024]{1,0:T(8,128)(2,1)S(1)} %get-tuple-element.23), channel_id=1, source_target_pairs={{0,8},{8,0},{16,24},{24,16},{1,9},{9,1},{17,25},{25,17},{2,10},{10... | collective-permute-start | bytes 196616 | tf_op jit(solution)/shard_map/ppermute | solution.py:336
  9.1 3.0 %onehot.1 = (bf16[2048,1024]{1,0:T(8,128)(2,1)S(1)}, bf16[512,2048]{1,0:T(8,128)(2,1)S(1)}, f32[16,256]{1,0:T(8,128)S(1)}, bf16[1024,2048]{1,0:T(8,128)(2,1)S(1)}) custom-call(s32[16,2048]{1,0:T(8,128)S(1)} %get-tuple-element.24.codes_ref, bf16[2048,1024]{1,0:T(8,128)(2,1)S(1)} %get-tuple-element.25.res_ref), custom_call_target="tpu_custom_call" | custom-call | flops 1073741824 | bytes 4194304 | tf_op jit(solution)/shard_map/onehot/pallas_call | solution.py:223
  12.1 0.0 collective-permute-done.refs_1_
  12.1 2.0 %collective-permute-done.1.refs_2_ = bf16[32,1024]{1,0:T(8,128)(2,1)S(1)} collective-permute-done((bf16[32,1024]{1,0:T(8,128)(2,1)S(1)}, bf16[32,1024]{1,0:T(8,128)(2,1)S(1)}, u32[]{:S(2)}, u32[]{:S(2)}) %collective-permute-start.1) | collective-permute-done | bytes 65568 | tf_op jit(solution)/shard_map/ppermute | solution.py:336
  14.1 0.0 collective-permute-done.2.refs_3_
  14.1 1.1 %collective-permute-start.3 = (bf16[32,1024]{1,0:T(8,128)(2,1)S(1)}, bf16[32,1024]{1,0:T(8,128)(2,1)S(1)}, u32[]{:S(2)}, u32[]{:S(2)}) collective-permute-start(bf16[32,1024]{1,0:T(8,128)(2,1)S(1)} %share.1), channel_id=1, source_target_pairs={{0,8},{8,0},{16,24},{24,16},{1,9},{9,1},{17,25},{25,17},{2,10},{10... | collective-permute-start | bytes 196616 | tf_op jit(solution)/shard_map/ppermute | solution.py:336
  15.3 2.0 %collective-permute-start.5 = (bf16[32,1024]{1,0:T(8,128)(2,1)S(1)}, bf16[32,1024]{1,0:T(8,128)(2,1)S(1)}, u32[]{:S(2)}, u32[]{:S(2)}) collective-permute-start(bf16[32,1024]{1,0:T(8,128)(2,1)S(1)} %share.1), channel_id=1, source_target_pairs={{0,24},{8,16},{16,8},{24,0},{1,25},{9,17},{17,9},{25,1},{2,26},{10... | collective-permute-start | bytes 196616 | tf_op jit(solution)/shard_map/ppermute | solution.py:336
  17.2 0.4 collective-permute-start.4
  17.7 1.8 %collective-permute-done.3 = bf16[32,1024]{1,0:T(8,128)(2,1)S(1)} collective-permute-done((bf16[32,1024]{1,0:T(8,128)(2,1)S(1)}, bf16[32,1024]{1,0:T(8,128)(2,1)S(1)}, u32[]{:S(2)}, u32[]{:S(2)}) %collective-permute-start.3) | collective-permute-done | bytes 65568 | tf_op jit(solution)/shard_map/ppermute | solution.py:336
  19.5 0.1 collective-permute-start.12
  19.6 0.5 collective-permute-start.8
  20.1 1.5 %collective-permute-start.6 = (bf16[64,1024]{1,0:T(8,128)(2,1)S(1)}, bf16[64,1024]{1,0:T(8,128)(2,1)S(1)}, u32[]{:S(2)}, u32[]{:S(2)}) collective-permute-start(bf16[64,1024]{1,0:T(8,128)(2,1)S(1)} %pad_maximum_fusion.refs_0_), channel_id=1, source_target_pairs={{0,4},{1,3},{2,6},{3,1},{4,0},{5,7},{6,2},{7,5},{8,12},{9,11},{10,... | collective-permute-start | bytes 393224 | tf_op jit(solution)/shard_map/ppermute | solution.py:336
  21.6 1.6 %collective-permute-done.4 = bf16[32,1024]{1,0:T(8,128)(2,1)S(1)} collective-permute-done((bf16[32,1024]{1,0:T(8,128)(2,1)S(1)}, bf16[32,1024]{1,0:T(8,128)(2,1)S(1)}, u32[]{:S(2)}, u32[]{:S(2)}) %collective-permute-start.4) | collective-permute-done | bytes 65568 | tf_op jit(solution)/shard_map/ppermute | solution.py:336
  23.2 0.0 collective-permute-done.5
  23.3 1.8 %collective-permute-start.7 = (bf16[64,1024]{1,0:T(8,128)(2,1)S(1)}, bf16[64,1024]{1,0:T(8,128)(2,1)S(1)}, u32[]{:S(2)}, u32[]{:S(2)}) collective-permute-start(bf16[64,1024]{1,0:T(8,128)(2,1)S(1)} %constant_dynamic-update-slice_fusion.refs_1_), channel_id=1, source_target_pairs={{0,4},{1,3},{2,6},{3,1},{4,0},{5,7},{6,2},{7,5},{8,12},{9,11},{10,... | collective-permute-start | bytes 393224 | tf_op jit(solution)/shard_map/ppermute | solution.py:336
  25.0 0.0 collective-permute-start.13
  25.0 0.0 collective-permute-done.12.refs_8_
  25.0 1.5 %collective-permute-start.9 = (bf16[64,1024]{1,0:T(8,128)(2,1)S(1)}, bf16[64,1024]{1,0:T(8,128)(2,1)S(1)}, u32[]{:S(2)}, u32[]{:S(2)}) collective-permute-start(bf16[64,1024]{1,0:T(8,128)(2,1)S(1)} %constant_dynamic-update-slice_fusion.refs_1_), channel_id=1, source_target_pairs={{0,2},{1,5},{2,0},{3,7},{4,6},{5,1},{6,4},{7,3},{8,10},{9,13},{10,... | collective-permute-start | bytes 393224 | tf_op jit(solution)/shard_map/ppermute | solution.py:336
  26.5 0.0 collective-permute-done.8.refs_4_
  26.5 0.0 collective-permute-start.16
  26.5 0.0 collective-permute-done.6.refs_2_
  26.5 0.7 %collective-permute-start.10 = (bf16[64,1024]{1,0:T(8,128)(2,1)S(1)}, bf16[64,1024]{1,0:T(8,128)(2,1)S(1)}, u32[]{:S(2)}, u32[]{:S(2)}) collective-permute-start(bf16[64,1024]{1,0:T(8,128)(2,1)S(1)} %collective-permute-done.6.refs_2_), channel_id=1, source_target_pairs={{0,2},{1,5},{2,0},{3,7},{4,6},{5,1},{6,4},{7,3},{8,10},{9,13},{10,... | collective-permute-start | bytes 393224 | tf_op jit(solution)/shard_map/ppermute | solution.py:336
  27.3 1.6 %collective-permute-done.7.refs_3_ = bf16[64,1024]{1,0:T(8,128)(2,1)S(1)} collective-permute-done((bf16[64,1024]{1,0:T(8,128)(2,1)S(1)}, bf16[64,1024]{1,0:T(8,128)(2,1)S(1)}, u32[]{:S(2)}, u32[]{:S(2)}) %collective-permute-start.7) | collective-permute-done | bytes 131104 | tf_op jit(solution)/shard_map/ppermute | solution.py:336
  28.9 1.4 %collective-permute-start.11 = (bf16[64,1024]{1,0:T(8,128)(2,1)S(1)}, bf16[64,1024]{1,0:T(8,128)(2,1)S(1)}, u32[]{:S(2)}, u32[]{:S(2)}) collective-permute-start(bf16[64,1024]{1,0:T(8,128)(2,1)S(1)} %collective-permute-done.7.refs_3_), channel_id=1, source_target_pairs={{0,2},{1,5},{2,0},{3,7},{4,6},{5,1},{6,4},{7,3},{8,10},{9,13},{10,... | collective-permute-start | bytes 393224 | tf_op jit(solution)/shard_map/ppermute | solution.py:336
  30.4 0.0 collective-permute-done.13.refs_9_
  30.4 0.0 collective-permute-start.14
  30.4 0.0 collective-permute-done.9.refs_5_
  30.4 0.5 collective-permute-start.15
  30.9 0.0 collective-permute-done.16.refs_12_
  30.9 0.1 collective-permute-start.17
  30.9 0.6 %collective-permute-done.10.refs_6_ = bf16[64,1024]{1,0:T(8,128)(2,1)S(1)} collective-permute-done((bf16[64,1024]{1,0:T(8,128)(2,1)S(1)}, bf16[64,1024]{1,0:T(8,128)(2,1)S(1)}, u32[]{:S(2)}, u32[]{:S(2)}) %collective-permute-start.10) | collective-permute-done | bytes 131104 | tf_op jit(solution)/shard_map/ppermute | solution.py:336
  31.6 0.0 collective-permute-start.18
  31.6 2.3 %collective-permute-done.11.refs_7_ = bf16[64,1024]{1,0:T(8,128)(2,1)S(1)} collective-permute-done((bf16[64,1024]{1,0:T(8,128)(2,1)S(1)}, bf16[64,1024]{1,0:T(8,128)(2,1)S(1)}, u32[]{:S(2)}, u32[]{:S(2)}) %collective-permute-start.11) | collective-permute-done | bytes 131104 | tf_op jit(solution)/shard_map/ppermute | solution.py:336
  33.9 0.0 collective-permute-start.19
  33.9 0.0 collective-permute-done.14.refs_10_
  33.9 0.0 collective-permute-done.17.refs_13_
  33.9 0.0 collective-permute-done.15.refs_11_
  33.9 0.0 collective-permute-done.18.refs_14_
  33.9 1.3 %collective-permute-done.19.refs_15_ = bf16[64,1024]{1,0:T(8,128)(2,1)S(1)} collective-permute-done((bf16[64,1024]{1,0:T(8,128)(2,1)S(1)}, bf16[64,1024]{1,0:T(8,128)(2,1)S(1)}, u32[]{:S(2)}, u32[]{:S(2)}) %collective-permute-start.19) | collective-permute-done | bytes 131104 | tf_op jit(solution)/shard_map/ppermute | solution.py:336
  35.2 11.5 %polar.1.rot_ref = bf16[128,1024]{1,0:T(8,128)(2,1)S(1)} custom-call(bf16[64,1024]{1,0:T(8,128)(2,1)S(1)} %pad_maximum_fusion.refs_0_, bf16[64,1024]{1,0:T(8,128)(2,1)S(1)} %constant_dynamic-update-slice_fusion.refs_1_, bf16[64,1024]{1,0:T(8,128)(2,1)S(1)} %collective-permute-done.6.refs_2_, bf16[64,1024]{1,0:T(8,128)(2,1)S(1)} %collective-permute-done.7.refs_3_, ...), custom_call_target="tpu_custom_call" | custom-call | tf_op jit(solution)/shard_map/polar/pallas_call | solution.py:280
  46.7 1.4 %sums.1.refs_0_ = bf16[144,256]{1,0:T(8,128)(2,1)S(1)} custom-call(bf16[128,1024]{1,0:T(8,128)(2,1)S(1)} %polar.1.rot_ref, bf16[1024,2048]{1,0:T(8,128)(2,1)S(1)} %get-tuple-element.34.res_ref, bf16[2048,1024]{1,0:T(8,128)(2,1)S(1)} %get-tuple-element.35.onehot_ref, bf16[512,2048]{1,0:T(8,128)(2,1)S(1)} %get-tuple-element.36.masks_ref, ...), custom_call_target="tpu_custom_call" | custom-call | tf_op jit(solution)/shard_map/sums/pallas_call | solution.py:323
  48.2 2.0 %collective-permute-start.22 = (bf16[144,256]{1,0:T(8,128)(2,1)S(1)}, bf16[144,256]{1,0:T(8,128)(2,1)S(1)}, u32[]{:S(2)}, u32[]{:S(2)}) collective-permute-start(bf16[144,256]{1,0:T(8,128)(2,1)S(1)} %sums.1.refs_0_), channel_id=1, source_target_pairs={{0,24},{8,16},{16,8},{24,0},{1,25},{9,17},{17,9},{25,1},{2,26},{10... | collective-permute-start | bytes 221192 | tf_op jit(solution)/shard_map/ppermute | solution.py:336
  50.2 0.0 collective-permute-start.21
  50.2 2.5 %collective-permute-start.20 = (bf16[144,256]{1,0:T(8,128)(2,1)S(1)}, bf16[144,256]{1,0:T(8,128)(2,1)S(1)}, u32[]{:S(2)}, u32[]{:S(2)}) collective-permute-start(bf16[144,256]{1,0:T(8,128)(2,1)S(1)} %sums.1.refs_0_), channel_id=1, source_target_pairs={{0,8},{8,0},{16,24},{24,16},{1,9},{9,1},{17,25},{25,17},{2,10},{10... | collective-permute-start | bytes 221192 | tf_op jit(solution)/shard_map/ppermute | solution.py:336
  52.6 2.7 %rotated.1 = f32[2048,128]{1,0:T(8,128)} custom-call(bf16[128,1024]{1,0:T(8,128)(2,1)S(1)} %polar.1.rot_ref, bf16[2048,1024]{1,0:T(8,128)(2,1)S(1)} %get-tuple-element.25.res_ref), custom_call_target="tpu_custom_call" | custom-call | tf_op jit(solution)/shard_map/rotated/pallas_call | solution.py:323
  55.3 0.0 collective-permute-done.22.refs_3_
  55.3 2.2 %collective-permute-done.21.refs_2_ = bf16[144,256]{1,0:T(8,128)(2,1)S(1)} collective-permute-done((bf16[144,256]{1,0:T(8,128)(2,1)S(1)}, bf16[144,256]{1,0:T(8,128)(2,1)S(1)}, u32[]{:S(2)}, u32[]{:S(2)}) %collective-permute-start.21) | collective-permute-done | bytes 73760 | tf_op jit(solution)/shard_map/ppermute | solution.py:336
  57.5 0.0 collective-permute-done.20.refs_1_
  57.5 0.7 %book.1 = f32[128,256]{1,0:T(8,128)} custom-call(f32[128,256]{1,0:T(8,128)S(1)} %get-tuple-element.33.book_ref, bf16[144,256]{1,0:T(8,128)(2,1)S(1)} %sums.1.refs_0_, bf16[144,256]{1,0:T(8,128)(2,1)S(1)} %collective-permute-done.20.refs_1_, bf16[144,256]{1,0:T(8,128)(2,1)S(1)} %collective-permute-done.21.refs_2_, ...), custom_call_target="tpu_custom_call" | custom-call | tf_op jit(solution)/shard_map/book/pallas_call | solution.py:323
  (4 shorter events, 0.1 us)
Async XLA Ops:
  3.3 8.8 %collective-permute-start = (bf16[32,1024]{1,0:T(8,128)(2,1)S(1)}, bf16[32,1024]{1,0:T(8,128)(2,1)S(1)}, u32[]{:S(2)}, u32[]{:S(2)}) collective-permute-start(bf16[32,1024]{1,0:T(8,128)(2,1)S(1)} %get-tuple-element.21), channel_id=1, source_target_pairs={{0,24},{8,16},{16,8},{24,0},{1,25},{9,17},{17,9},{25,1},{2,26},{10... | collective-permute-start | bytes 196616 | tf_op jit(solution)/shard_map/ppermute | solution.py:336
  8.5 5.6 %collective-permute-start.1 = (bf16[32,1024]{1,0:T(8,128)(2,1)S(1)}, bf16[32,1024]{1,0:T(8,128)(2,1)S(1)}, u32[]{:S(2)}, u32[]{:S(2)}) collective-permute-start(bf16[32,1024]{1,0:T(8,128)(2,1)S(1)} %get-tuple-element.22), channel_id=1, source_target_pairs={{0,16},{8,24},{16,0},{24,8},{1,17},{9,25},{17,1},{25,9},{2,18},{10... | collective-permute-start | bytes 196616 | tf_op jit(solution)/shard_map/ppermute | solution.py:336
  8.5 5.6 %collective-permute-start.2 = (bf16[32,1024]{1,0:T(8,128)(2,1)S(1)}, bf16[32,1024]{1,0:T(8,128)(2,1)S(1)}, u32[]{:S(2)}, u32[]{:S(2)}) collective-permute-start(bf16[32,1024]{1,0:T(8,128)(2,1)S(1)} %get-tuple-element.23), channel_id=1, source_target_pairs={{0,8},{8,0},{16,24},{24,16},{1,9},{9,1},{17,25},{25,17},{2,10},{10... | collective-permute-start | bytes 196616 | tf_op jit(solution)/shard_map/ppermute | solution.py:336
  14.1 5.4 %collective-permute-start.3 = (bf16[32,1024]{1,0:T(8,128)(2,1)S(1)}, bf16[32,1024]{1,0:T(8,128)(2,1)S(1)}, u32[]{:S(2)}, u32[]{:S(2)}) collective-permute-start(bf16[32,1024]{1,0:T(8,128)(2,1)S(1)} %share.1), channel_id=1, source_target_pairs={{0,8},{8,0},{16,24},{24,16},{1,9},{9,1},{17,25},{25,17},{2,10},{10... | collective-permute-start | bytes 196616 | tf_op jit(solution)/shard_map/ppermute | solution.py:336
  15.3 8.0 %collective-permute-start.5 = (bf16[32,1024]{1,0:T(8,128)(2,1)S(1)}, bf16[32,1024]{1,0:T(8,128)(2,1)S(1)}, u32[]{:S(2)}, u32[]{:S(2)}) collective-permute-start(bf16[32,1024]{1,0:T(8,128)(2,1)S(1)} %share.1), channel_id=1, source_target_pairs={{0,24},{8,16},{16,8},{24,0},{1,25},{9,17},{17,9},{25,1},{2,26},{10... | collective-permute-start | bytes 196616 | tf_op jit(solution)/shard_map/ppermute | solution.py:336
  17.2 6.0 %collective-permute-start.4 = (bf16[32,1024]{1,0:T(8,128)(2,1)S(1)}, bf16[32,1024]{1,0:T(8,128)(2,1)S(1)}, u32[]{:S(2)}, u32[]{:S(2)}) collective-permute-start(bf16[32,1024]{1,0:T(8,128)(2,1)S(1)} %share.1), channel_id=1, source_target_pairs={{0,16},{8,24},{16,0},{24,8},{1,17},{9,25},{17,1},{25,9},{2,18},{10... | collective-permute-start | bytes 196616 | tf_op jit(solution)/shard_map/ppermute | solution.py:336
  19.5 5.6 %collective-permute-start.12 = (bf16[64,1024]{1,0:T(8,128)(2,1)S(1)}, bf16[64,1024]{1,0:T(8,128)(2,1)S(1)}, u32[]{:S(2)}, u32[]{:S(2)}) collective-permute-start(bf16[64,1024]{1,0:T(8,128)(2,1)S(1)} %pad_maximum_fusion.refs_0_), channel_id=1, source_target_pairs={{0,1},{1,0},{2,3},{3,2},{4,5},{5,4},{6,7},{7,6},{8,9},{9,8},{10,11... | collective-permute-start | bytes 393224 | tf_op jit(solution)/shard_map/ppermute | solution.py:336
  19.6 7.0 %collective-permute-start.8 = (bf16[64,1024]{1,0:T(8,128)(2,1)S(1)}, bf16[64,1024]{1,0:T(8,128)(2,1)S(1)}, u32[]{:S(2)}, u32[]{:S(2)}) collective-permute-start(bf16[64,1024]{1,0:T(8,128)(2,1)S(1)} %pad_maximum_fusion.refs_0_), channel_id=1, source_target_pairs={{0,2},{1,5},{2,0},{3,7},{4,6},{5,1},{6,4},{7,3},{8,10},{9,13},{10,... | collective-permute-start | bytes 393224 | tf_op jit(solution)/shard_map/ppermute | solution.py:336
  20.1 6.4 %collective-permute-start.6 = (bf16[64,1024]{1,0:T(8,128)(2,1)S(1)}, bf16[64,1024]{1,0:T(8,128)(2,1)S(1)}, u32[]{:S(2)}, u32[]{:S(2)}) collective-permute-start(bf16[64,1024]{1,0:T(8,128)(2,1)S(1)} %pad_maximum_fusion.refs_0_), channel_id=1, source_target_pairs={{0,4},{1,3},{2,6},{3,1},{4,0},{5,7},{6,2},{7,5},{8,12},{9,11},{10,... | collective-permute-start | bytes 393224 | tf_op jit(solution)/shard_map/ppermute | solution.py:336
  23.3 5.6 %collective-permute-start.7 = (bf16[64,1024]{1,0:T(8,128)(2,1)S(1)}, bf16[64,1024]{1,0:T(8,128)(2,1)S(1)}, u32[]{:S(2)}, u32[]{:S(2)}) collective-permute-start(bf16[64,1024]{1,0:T(8,128)(2,1)S(1)} %constant_dynamic-update-slice_fusion.refs_1_), channel_id=1, source_target_pairs={{0,4},{1,3},{2,6},{3,1},{4,0},{5,7},{6,2},{7,5},{8,12},{9,11},{10,... | collective-permute-start | bytes 393224 | tf_op jit(solution)/shard_map/ppermute | solution.py:336
  25.0 5.3 %collective-permute-start.13 = (bf16[64,1024]{1,0:T(8,128)(2,1)S(1)}, bf16[64,1024]{1,0:T(8,128)(2,1)S(1)}, u32[]{:S(2)}, u32[]{:S(2)}) collective-permute-start(bf16[64,1024]{1,0:T(8,128)(2,1)S(1)} %constant_dynamic-update-slice_fusion.refs_1_), channel_id=1, source_target_pairs={{0,1},{1,0},{2,3},{3,2},{4,5},{5,4},{6,7},{7,6},{8,9},{9,8},{10,11... | collective-permute-start | bytes 393224 | tf_op jit(solution)/shard_map/ppermute | solution.py:336
  25.0 5.3 %collective-permute-start.9 = (bf16[64,1024]{1,0:T(8,128)(2,1)S(1)}, bf16[64,1024]{1,0:T(8,128)(2,1)S(1)}, u32[]{:S(2)}, u32[]{:S(2)}) collective-permute-start(bf16[64,1024]{1,0:T(8,128)(2,1)S(1)} %constant_dynamic-update-slice_fusion.refs_1_), channel_id=1, source_target_pairs={{0,2},{1,5},{2,0},{3,7},{4,6},{5,1},{6,4},{7,3},{8,10},{9,13},{10,... | collective-permute-start | bytes 393224 | tf_op jit(solution)/shard_map/ppermute | solution.py:336
  26.5 4.3 %collective-permute-start.16 = (bf16[64,1024]{1,0:T(8,128)(2,1)S(1)}, bf16[64,1024]{1,0:T(8,128)(2,1)S(1)}, u32[]{:S(2)}, u32[]{:S(2)}) collective-permute-start(bf16[64,1024]{1,0:T(8,128)(2,1)S(1)} %collective-permute-done.8.refs_4_), channel_id=1, source_target_pairs={{0,1},{1,0},{2,3},{3,2},{4,5},{5,4},{6,7},{7,6},{8,9},{9,8},{10,11... | collective-permute-start | bytes 393224 | tf_op jit(solution)/shard_map/ppermute | solution.py:336
  26.5 5.0 %collective-permute-start.10 = (bf16[64,1024]{1,0:T(8,128)(2,1)S(1)}, bf16[64,1024]{1,0:T(8,128)(2,1)S(1)}, u32[]{:S(2)}, u32[]{:S(2)}) collective-permute-start(bf16[64,1024]{1,0:T(8,128)(2,1)S(1)} %collective-permute-done.6.refs_2_), channel_id=1, source_target_pairs={{0,2},{1,5},{2,0},{3,7},{4,6},{5,1},{6,4},{7,3},{8,10},{9,13},{10,... | collective-permute-start | bytes 393224 | tf_op jit(solution)/shard_map/ppermute | solution.py:336
  28.9 5.0 %collective-permute-start.11 = (bf16[64,1024]{1,0:T(8,128)(2,1)S(1)}, bf16[64,1024]{1,0:T(8,128)(2,1)S(1)}, u32[]{:S(2)}, u32[]{:S(2)}) collective-permute-start(bf16[64,1024]{1,0:T(8,128)(2,1)S(1)} %collective-permute-done.7.refs_3_), channel_id=1, source_target_pairs={{0,2},{1,5},{2,0},{3,7},{4,6},{5,1},{6,4},{7,3},{8,10},{9,13},{10,... | collective-permute-start | bytes 393224 | tf_op jit(solution)/shard_map/ppermute | solution.py:336
  30.4 3.5 %collective-permute-start.14 = (bf16[64,1024]{1,0:T(8,128)(2,1)S(1)}, bf16[64,1024]{1,0:T(8,128)(2,1)S(1)}, u32[]{:S(2)}, u32[]{:S(2)}) collective-permute-start(bf16[64,1024]{1,0:T(8,128)(2,1)S(1)} %collective-permute-done.6.refs_2_), channel_id=1, source_target_pairs={{0,1},{1,0},{2,3},{3,2},{4,5},{5,4},{6,7},{7,6},{8,9},{9,8},{10,11... | collective-permute-start | bytes 393224 | tf_op jit(solution)/shard_map/ppermute | solution.py:336
  30.4 3.5 %collective-permute-start.15 = (bf16[64,1024]{1,0:T(8,128)(2,1)S(1)}, bf16[64,1024]{1,0:T(8,128)(2,1)S(1)}, u32[]{:S(2)}, u32[]{:S(2)}) collective-permute-start(bf16[64,1024]{1,0:T(8,128)(2,1)S(1)} %collective-permute-done.7.refs_3_), channel_id=1, source_target_pairs={{0,1},{1,0},{2,3},{3,2},{4,5},{5,4},{6,7},{7,6},{8,9},{9,8},{10,11... | collective-permute-start | bytes 393224 | tf_op jit(solution)/shard_map/ppermute | solution.py:336
  30.9 3.0 %collective-permute-start.17 = (bf16[64,1024]{1,0:T(8,128)(2,1)S(1)}, bf16[64,1024]{1,0:T(8,128)(2,1)S(1)}, u32[]{:S(2)}, u32[]{:S(2)}) collective-permute-start(bf16[64,1024]{1,0:T(8,128)(2,1)S(1)} %collective-permute-done.9.refs_5_), channel_id=1, source_target_pairs={{0,1},{1,0},{2,3},{3,2},{4,5},{5,4},{6,7},{7,6},{8,9},{9,8},{10,11... | collective-permute-start | bytes 393224 | tf_op jit(solution)/shard_map/ppermute | solution.py:336
  31.6 2.3 %collective-permute-start.18 = (bf16[64,1024]{1,0:T(8,128)(2,1)S(1)}, bf16[64,1024]{1,0:T(8,128)(2,1)S(1)}, u32[]{:S(2)}, u32[]{:S(2)}) collective-permute-start(bf16[64,1024]{1,0:T(8,128)(2,1)S(1)} %collective-permute-done.10.refs_6_), channel_id=1, source_target_pairs={{0,1},{1,0},{2,3},{3,2},{4,5},{5,4},{6,7},{7,6},{8,9},{9,8},{10,11... | collective-permute-start | bytes 393224 | tf_op jit(solution)/shard_map/ppermute | solution.py:336
  33.9 1.3 %collective-permute-start.19 = (bf16[64,1024]{1,0:T(8,128)(2,1)S(1)}, bf16[64,1024]{1,0:T(8,128)(2,1)S(1)}, u32[]{:S(2)}, u32[]{:S(2)}) collective-permute-start(bf16[64,1024]{1,0:T(8,128)(2,1)S(1)} %collective-permute-done.11.refs_7_), channel_id=1, source_target_pairs={{0,1},{1,0},{2,3},{3,2},{4,5},{5,4},{6,7},{7,6},{8,9},{9,8},{10,11... | collective-permute-start | bytes 393224 | tf_op jit(solution)/shard_map/ppermute | solution.py:336
  48.2 7.2 %collective-permute-start.22 = (bf16[144,256]{1,0:T(8,128)(2,1)S(1)}, bf16[144,256]{1,0:T(8,128)(2,1)S(1)}, u32[]{:S(2)}, u32[]{:S(2)}) collective-permute-start(bf16[144,256]{1,0:T(8,128)(2,1)S(1)} %sums.1.refs_0_), channel_id=1, source_target_pairs={{0,24},{8,16},{16,8},{24,0},{1,25},{9,17},{17,9},{25,1},{2,26},{10... | collective-permute-start | bytes 221192 | tf_op jit(solution)/shard_map/ppermute | solution.py:336
  50.2 7.3 %collective-permute-start.21 = (bf16[144,256]{1,0:T(8,128)(2,1)S(1)}, bf16[144,256]{1,0:T(8,128)(2,1)S(1)}, u32[]{:S(2)}, u32[]{:S(2)}) collective-permute-start(bf16[144,256]{1,0:T(8,128)(2,1)S(1)} %sums.1.refs_0_), channel_id=1, source_target_pairs={{0,16},{8,24},{16,0},{24,8},{1,17},{9,25},{17,1},{25,9},{2,18},{10... | collective-permute-start | bytes 221192 | tf_op jit(solution)/shard_map/ppermute | solution.py:336
  50.2 7.3 %collective-permute-start.20 = (bf16[144,256]{1,0:T(8,128)(2,1)S(1)}, bf16[144,256]{1,0:T(8,128)(2,1)S(1)}, u32[]{:S(2)}, u32[]{:S(2)}) collective-permute-start(bf16[144,256]{1,0:T(8,128)(2,1)S(1)} %sums.1.refs_0_), channel_id=1, source_target_pairs={{0,8},{8,0},{16,24},{24,16},{1,9},{9,1},{17,25},{25,17},{2,10},{10... | collective-permute-start | bytes 221192 | tf_op jit(solution)/shard_map/ppermute | solution.py:336

commit v2 on v1

--- a/solution.py
+++ b/solution.py
@@ -118,10 +118,10 @@
 
     def mirror(target, j, value):
         rows, cols = lower(j)
-        target[rows, cols] = value.astype(bf16)
-        for i in range(j + 1, steps):
-            at = (i - j) * chunk
-            target[cols, pl.ds(i * chunk, chunk)] = value[at : at + chunk, :].T.astype(bf16)
+        rounded = value.astype(bf16)
+        target[rows, cols] = rounded
+        if j < steps - 1:
+            target[cols, pl.ds((j + 1) * chunk, dim - (j + 1) * chunk)] = rounded[chunk:, :].T
 
     def gram_of(source, transposed=None):
         r = lax.broadcasted_iota(jnp.int32, (chunk, chunk), 0)
@@ -384,8 +384,11 @@
         operands = (rotation_t, res_t, *ready)
         sums = small_call(sums_kernel, "sums", (own + subs, words), bf16, *operands, scratch=scratch)
         rotated = small_call(rotated_kernel, "rotated", (rows, own), f32, rotation_t, res_v)
-        others = [swap(sums, "dp", dp, k) for k in range(1, dp)]
-        book = small_call(book_kernel, "book", (own, words), f32, book_v, sums, *others)
+        totals = {0: sums}
+        for k in sorted(range(1, dp), key=lambda k: (bin(k).count("1"), k)):
+            totals[k] = swap(totals[k & (k - 1)], "dp", dp, k & -k)
+        totals = [totals[k] for k in range(dp)]
+        book = small_call(book_kernel, "book", (own, words), f32, book_v, *totals)
         return rotated, jnp.transpose(book.reshape(subs, width, words), (0, 2, 1))
 
     return body

time: 58.4 us -> 59.6 us (1.021)
  waiting for transfers between devices: 13.5 us -> 16.7 us
  starting transfers between devices: 21.9 us -> 20 us
    ppermute x23, waiting for transfers between devices: 13.5 us -> 16.7 us  [swap(): lax.ppermute(value, axis, [(i, i ^ (odd_mask if i % 2 else mask)) for i i...]
    ppermute x23, starting transfers between devices: 21.9 us -> 20 us  [swap(): lax.ppermute(value, axis, [(i, i ^ (odd_mask if i % 2 else mask)) for i i...]
  transfers between devices with their start and end apart: 23 -> 23, of which waited for: 8 -> 9; matrix products, arithmetic and copies ran while one was open for 0% -> 0% of each run, Pallas kernels for 10% -> 10%
where the time goes in v2:
time: 59.6 us; the launch traced here: 59.4 us
  Pallas kernels  22 us (37%)
  starting transfers between devices  20 us (34%)
  waiting for transfers between devices  16.7 us (28%)
  between operations  0.74 us (1%)
    ppermute x23, starting transfers between devices, swap(): lax.ppermute(value, axis, [(i, i ^ (odd_mask if i % 2 else mask)) for i i...  20 us
    ppermute x23, waiting for transfers between devices, swap(): lax.ppermute(value, axis, [(i, i ^ (odd_mask if i % 2 else mask)) for i i...  16.7 us
    pallas_call x1, Pallas kernels, polar(): pl.pallas_call(kernel, out_shape=jax.ShapeDtypeStruct((own, dim), bf16),...  11.4 us
    pallas_call x4, Pallas kernels, small_call(): pl.pallas_call(kernel, out_shape=jax.ShapeDtypeStruct(shape, dtype), in_s...  4.89 us
    pallas_call x1, Pallas kernels, onehot_call(): pl.pallas_call(onehot_kernel, out_shape=(jax.ShapeDtypeStruct((rows, subs...  2.99 us
    pallas_call x1, Pallas kernels, cross_partial(): pl.pallas_call(functools.partial(cross_kernel, dp=dp), out_shape=shapes,...  2.71 us
  transfers between devices with their start and end apart: 23, of which 9 were waited for; matrix products, arithmetic and copies ran while one was open for 0% of the time, Pallas kernels for 10%

profile of v2, /device:TPU:0, one launch (start us, length us, event | category | flops | bytes accessed | tf_op | source)
XLA Modules:
  0.0 59.4 jit_solution(4900877484544841057)
XLA Ops:
  0.6 2.7 %cross_partial.1 = (f32[32,1024]{1,0:T(8,128)S(1)}, bf16[32,1024]{1,0:T(8,128)(2,1)S(1)}, bf16[32,1024]{1,0:T(8,128)(2,1)S(1)}, bf16[32,1024]{1,0:T(8,128)(2,1)S...) custom-call(s32[16,2048]{1,0:T(8,128)} %bitcast.7, f32[128,256]{1,0:T(8,128)} %bitcast.8, ...), custom_call_target="tpu_custom_call" | custom-call | tf_op jit(solution)/shard_map/cross_partial/pallas_call | solution.py:86
  3.3 5.1 %collective-permute-start = (bf16[32,1024]{1,0:T(8,128)(2,1)S(1)}, bf16[32,1024]{1,0:T(8,128)(2,1)S(1)}, u32[]{:S(2)}, u32[]{:S(2)}) collective-permute-start(bf16[32,1024]{1,0:T(8,128)(2,1)S(1)} %get-tuple-element.21), channel_id=1, source_target_pairs={{0,24},{8,16},{16,8},{24,0},{1,25},{9,17},{17,9},{25,1},{2,26},{10... | collective-permute-start | bytes 196616 | tf_op jit(solution)/shard_map/ppermute | solution.py:336
  8.5 0.0 collective-permute-start.1
  8.5 0.6 %collective-permute-start.2 = (bf16[32,1024]{1,0:T(8,128)(2,1)S(1)}, bf16[32,1024]{1,0:T(8,128)(2,1)S(1)}, u32[]{:S(2)}, u32[]{:S(2)}) collective-permute-start(bf16[32,1024]{1,0:T(8,128)(2,1)S(1)} %get-tuple-element.23), channel_id=1, source_target_pairs={{0,8},{8,0},{16,24},{24,16},{1,9},{9,1},{17,25},{25,17},{2,10},{10... | collective-permute-start | bytes 196616 | tf_op jit(solution)/shard_map/ppermute | solution.py:336
  9.1 3.0 %onehot.1 = (bf16[2048,1024]{1,0:T(8,128)(2,1)S(1)}, bf16[512,2048]{1,0:T(8,128)(2,1)S(1)}, f32[16,256]{1,0:T(8,128)S(1)}, bf16[1024,2048]{1,0:T(8,128)(2,1)S(1)}) custom-call(s32[16,2048]{1,0:T(8,128)S(1)} %get-tuple-element.24.codes_ref, bf16[2048,1024]{1,0:T(8,128)(2,1)S(1)} %get-tuple-element.25.res_ref), custom_call_target="tpu_custom_call" | custom-call | flops 1073741824 | bytes 4194304 | tf_op jit(solution)/shard_map/onehot/pallas_call | solution.py:223
  12.1 0.0 collective-permute-done.refs_1_
  12.1 2.0 %collective-permute-done.1.refs_2_ = bf16[32,1024]{1,0:T(8,128)(2,1)S(1)} collective-permute-done((bf16[32,1024]{1,0:T(8,128)(2,1)S(1)}, bf16[32,1024]{1,0:T(8,128)(2,1)S(1)}, u32[]{:S(2)}, u32[]{:S(2)}) %collective-permute-start.1) | collective-permute-done | bytes 65568 | tf_op jit(solution)/shard_map/ppermute | solution.py:336
  14.1 0.0 collective-permute-done.2.refs_3_
  14.1 1.1 %collective-permute-start.3 = (bf16[32,1024]{1,0:T(8,128)(2,1)S(1)}, bf16[32,1024]{1,0:T(8,128)(2,1)S(1)}, u32[]{:S(2)}, u32[]{:S(2)}) collective-permute-start(bf16[32,1024]{1,0:T(8,128)(2,1)S(1)} %share.1), channel_id=1, source_target_pairs={{0,8},{8,0},{16,24},{24,16},{1,9},{9,1},{17,25},{25,17},{2,10},{10... | collective-permute-start | bytes 196616 | tf_op jit(solution)/shard_map/ppermute | solution.py:336
  15.3 2.0 %collective-permute-start.5 = (bf16[32,1024]{1,0:T(8,128)(2,1)S(1)}, bf16[32,1024]{1,0:T(8,128)(2,1)S(1)}, u32[]{:S(2)}, u32[]{:S(2)}) collective-permute-start(bf16[32,1024]{1,0:T(8,128)(2,1)S(1)} %share.1), channel_id=1, source_target_pairs={{0,24},{8,16},{16,8},{24,0},{1,25},{9,17},{17,9},{25,1},{2,26},{10... | collective-permute-start | bytes 196616 | tf_op jit(solution)/shard_map/ppermute | solution.py:336
  17.2 0.4 collective-permute-start.4
  17.7 1.8 %collective-permute-done.3 = bf16[32,1024]{1,0:T(8,128)(2,1)S(1)} collective-permute-done((bf16[32,1024]{1,0:T(8,128)(2,1)S(1)}, bf16[32,1024]{1,0:T(8,128)(2,1)S(1)}, u32[]{:S(2)}, u32[]{:S(2)}) %collective-permute-start.3) | collective-permute-done | bytes 65568 | tf_op jit(solution)/shard_map/ppermute | solution.py:336
  19.5 0.1 collective-permute-start.12
  19.6 0.5 collective-permute-start.8
  20.1 1.5 %collective-permute-start.6 = (bf16[64,1024]{1,0:T(8,128)(2,1)S(1)}, bf16[64,1024]{1,0:T(8,128)(2,1)S(1)}, u32[]{:S(2)}, u32[]{:S(2)}) collective-permute-start(bf16[64,1024]{1,0:T(8,128)(2,1)S(1)} %pad_maximum_fusion.refs_0_), channel_id=1, source_target_pairs={{0,4},{1,3},{2,6},{3,1},{4,0},{5,7},{6,2},{7,5},{8,12},{9,11},{10,... | collective-permute-start | bytes 393224 | tf_op jit(solution)/shard_map/ppermute | solution.py:336
  21.6 1.6 %collective-permute-done.4 = bf16[32,1024]{1,0:T(8,128)(2,1)S(1)} collective-permute-done((bf16[32,1024]{1,0:T(8,128)(2,1)S(1)}, bf16[32,1024]{1,0:T(8,128)(2,1)S(1)}, u32[]{:S(2)}, u32[]{:S(2)}) %collective-permute-start.4) | collective-permute-done | bytes 65568 | tf_op jit(solution)/shard_map/ppermute | solution.py:336
  23.2 0.0 collective-permute-done.5
  23.3 1.8 %collective-permute-start.7 = (bf16[64,1024]{1,0:T(8,128)(2,1)S(1)}, bf16[64,1024]{1,0:T(8,128)(2,1)S(1)}, u32[]{:S(2)}, u32[]{:S(2)}) collective-permute-start(bf16[64,1024]{1,0:T(8,128)(2,1)S(1)} %constant_dynamic-update-slice_fusion.refs_1_), channel_id=1, source_target_pairs={{0,4},{1,3},{2,6},{3,1},{4,0},{5,7},{6,2},{7,5},{8,12},{9,11},{10,... | collective-permute-start | bytes 393224 | tf_op jit(solution)/shard_map/ppermute | solution.py:336
  25.0 0.0 collective-permute-start.13
  25.0 0.0 collective-permute-done.12.refs_8_
  25.0 1.5 %collective-permute-start.9 = (bf16[64,1024]{1,0:T(8,128)(2,1)S(1)}, bf16[64,1024]{1,0:T(8,128)(2,1)S(1)}, u32[]{:S(2)}, u32[]{:S(2)}) collective-permute-start(bf16[64,1024]{1,0:T(8,128)(2,1)S(1)} %constant_dynamic-update-slice_fusion.refs_1_), channel_id=1, source_target_pairs={{0,2},{1,5},{2,0},{3,7},{4,6},{5,1},{6,4},{7,3},{8,10},{9,13},{10,... | collective-permute-start | bytes 393224 | tf_op jit(solution)/shard_map/ppermute | solution.py:336
  26.5 0.0 collective-permute-done.8.refs_4_
  26.5 0.0 collective-permute-start.16
  26.5 0.0 collective-permute-done.6.refs_2_
  26.5 0.7 %collective-permute-start.10 = (bf16[64,1024]{1,0:T(8,128)(2,1)S(1)}, bf16[64,1024]{1,0:T(8,128)(2,1)S(1)}, u32[]{:S(2)}, u32[]{:S(2)}) collective-permute-start(bf16[64,1024]{1,0:T(8,128)(2,1)S(1)} %collective-permute-done.6.refs_2_), channel_id=1, source_target_pairs={{0,2},{1,5},{2,0},{3,7},{4,6},{5,1},{6,4},{7,3},{8,10},{9,13},{10,... | collective-permute-start | bytes 393224 | tf_op jit(solution)/shard_map/ppermute | solution.py:336
  27.3 1.6 %collective-permute-done.7.refs_3_ = bf16[64,1024]{1,0:T(8,128)(2,1)S(1)} collective-permute-done((bf16[64,1024]{1,0:T(8,128)(2,1)S(1)}, bf16[64,1024]{1,0:T(8,128)(2,1)S(1)}, u32[]{:S(2)}, u32[]{:S(2)}) %collective-permute-start.7) | collective-permute-done | bytes 131104 | tf_op jit(solution)/shard_map/ppermute | solution.py:336
  28.9 1.4 %collective-permute-start.11 = (bf16[64,1024]{1,0:T(8,128)(2,1)S(1)}, bf16[64,1024]{1,0:T(8,128)(2,1)S(1)}, u32[]{:S(2)}, u32[]{:S(2)}) collective-permute-start(bf16[64,1024]{1,0:T(8,128)(2,1)S(1)} %collective-permute-done.7.refs_3_), channel_id=1, source_target_pairs={{0,2},{1,5},{2,0},{3,7},{4,6},{5,1},{6,4},{7,3},{8,10},{9,13},{10,... | collective-permute-start | bytes 393224 | tf_op jit(solution)/shard_map/ppermute | solution.py:336
  30.4 0.0 collective-permute-done.13.refs_9_
  30.4 0.0 collective-permute-start.14
  30.4 0.0 collective-permute-done.9.refs_5_
  30.4 0.5 collective-permute-start.15
  30.9 0.0 collective-permute-done.16.refs_12_
  30.9 0.1 collective-permute-start.17
  30.9 0.6 %collective-permute-done.10.refs_6_ = bf16[64,1024]{1,0:T(8,128)(2,1)S(1)} collective-permute-done((bf16[64,1024]{1,0:T(8,128)(2,1)S(1)}, bf16[64,1024]{1,0:T(8,128)(2,1)S(1)}, u32[]{:S(2)}, u32[]{:S(2)}) %collective-permute-start.10) | collective-permute-done | bytes 131104 | tf_op jit(solution)/shard_map/ppermute | solution.py:336
  31.6 0.0 collective-permute-start.18
  31.6 2.3 %collective-permute-done.11.refs_7_ = bf16[64,1024]{1,0:T(8,128)(2,1)S(1)} collective-permute-done((bf16[64,1024]{1,0:T(8,128)(2,1)S(1)}, bf16[64,1024]{1,0:T(8,128)(2,1)S(1)}, u32[]{:S(2)}, u32[]{:S(2)}) %collective-permute-start.11) | collective-permute-done | bytes 131104 | tf_op jit(solution)/shard_map/ppermute | solution.py:336
  33.9 0.0 collective-permute-start.19
  33.9 0.0 collective-permute-done.14.refs_10_
  33.9 0.0 collective-permute-done.17.refs_13_
  33.9 0.0 collective-permute-done.15.refs_11_
  33.9 0.0 collective-permute-done.18.refs_14_
  33.9 1.3 %collective-permute-done.19.refs_15_ = bf16[64,1024]{1,0:T(8,128)(2,1)S(1)} collective-permute-done((bf16[64,1024]{1,0:T(8,128)(2,1)S(1)}, bf16[64,1024]{1,0:T(8,128)(2,1)S(1)}, u32[]{:S(2)}, u32[]{:S(2)}) %collective-permute-start.19) | collective-permute-done | bytes 131104 | tf_op jit(solution)/shard_map/ppermute | solution.py:336
  35.2 11.4 %polar.1.rot_ref = bf16[128,1024]{1,0:T(8,128)(2,1)S(1)} custom-call(bf16[64,1024]{1,0:T(8,128)(2,1)S(1)} %pad_maximum_fusion.refs_0_, bf16[64,1024]{1,0:T(8,128)(2,1)S(1)} %constant_dynamic-update-slice_fusion.refs_1_, bf16[64,1024]{1,0:T(8,128)(2,1)S(1)} %collective-permute-done.6.refs_2_, bf16[64,1024]{1,0:T(8,128)(2,1)S(1)} %collective-permute-done.7.refs_3_, ...), custom_call_target="tpu_custom_call" | custom-call | tf_op jit(solution)/shard_map/polar/pallas_call | solution.py:280
  46.6 1.4 %sums.1.refs_0_ = bf16[144,256]{1,0:T(8,128)(2,1)S(1)} custom-call(bf16[128,1024]{1,0:T(8,128)(2,1)S(1)} %polar.1.rot_ref, bf16[1024,2048]{1,0:T(8,128)(2,1)S(1)} %get-tuple-element.34.res_ref, bf16[2048,1024]{1,0:T(8,128)(2,1)S(1)} %get-tuple-element.35.onehot_ref, bf16[512,2048]{1,0:T(8,128)(2,1)S(1)} %get-tuple-element.36.masks_ref, ...), custom_call_target="tpu_custom_call" | custom-call | tf_op jit(solution)/shard_map/sums/pallas_call | solution.py:323
  48.1 0.7 %collective-permute-start.21 = (bf16[144,256]{1,0:T(8,128)(2,1)S(1)}, bf16[144,256]{1,0:T(8,128)(2,1)S(1)}, u32[]{:S(2)}, u32[]{:S(2)}) collective-permute-start(bf16[144,256]{1,0:T(8,128)(2,1)S(1)} %sums.1.refs_0_), channel_id=1, source_target_pairs={{0,16},{8,24},{16,0},{24,8},{1,17},{9,25},{17,1},{25,9},{2,18},{10... | collective-permute-start | bytes 221192 | tf_op jit(solution)/shard_map/ppermute | solution.py:336
  48.8 1.8 %collective-permute-start.20 = (bf16[144,256]{1,0:T(8,128)(2,1)S(1)}, bf16[144,256]{1,0:T(8,128)(2,1)S(1)}, u32[]{:S(2)}, u32[]{:S(2)}) collective-permute-start(bf16[144,256]{1,0:T(8,128)(2,1)S(1)} %sums.1.refs_0_), channel_id=1, source_target_pairs={{0,8},{8,0},{16,24},{24,16},{1,9},{9,1},{17,25},{25,17},{2,10},{10... | collective-permute-start | bytes 221192 | tf_op jit(solution)/shard_map/ppermute | solution.py:336
  50.7 3.7 %collective-permute-done.21.refs_2_ = bf16[144,256]{1,0:T(8,128)(2,1)S(1)} collective-permute-done((bf16[144,256]{1,0:T(8,128)(2,1)S(1)}, bf16[144,256]{1,0:T(8,128)(2,1)S(1)}, u32[]{:S(2)}, u32[]{:S(2)}) %collective-permute-start.21) | collective-permute-done | bytes 73760 | tf_op jit(solution)/shard_map/ppermute | solution.py:336
  54.4 0.0 collective-permute-start.22
  54.4 2.7 %rotated.1 = f32[2048,128]{1,0:T(8,128)} custom-call(bf16[128,1024]{1,0:T(8,128)(2,1)S(1)} %polar.1.rot_ref, bf16[2048,1024]{1,0:T(8,128)(2,1)S(1)} %get-tuple-element.25.res_ref), custom_call_target="tpu_custom_call" | custom-call | tf_op jit(solution)/shard_map/rotated/pallas_call | solution.py:323
  57.1 0.0 collective-permute-done.20.refs_1_
  57.1 1.6 %collective-permute-done.22.refs_3_ = bf16[144,256]{1,0:T(8,128)(2,1)S(1)} collective-permute-done((bf16[144,256]{1,0:T(8,128)(2,1)S(1)}, bf16[144,256]{1,0:T(8,128)(2,1)S(1)}, u32[]{:S(2)}, u32[]{:S(2)}) %collective-permute-start.22) | collective-permute-done | bytes 73760 | tf_op jit(solution)/shard_map/ppermute | solution.py:336
  58.7 0.7 %book.1 = f32[128,256]{1,0:T(8,128)} custom-call(f32[128,256]{1,0:T(8,128)S(1)} %get-tuple-element.33.book_ref, bf16[144,256]{1,0:T(8,128)(2,1)S(1)} %sums.1.refs_0_, bf16[144,256]{1,0:T(8,128)(2,1)S(1)} %collective-permute-done.20.refs_1_, bf16[144,256]{1,0:T(8,128)(2,1)S(1)} %collective-permute-done.21.refs_2_, ...), custom_call_target="tpu_custom_call" | custom-call | tf_op jit(solution)/shard_map/book/pallas_call | solution.py:323
  (4 shorter events, 0.1 us)
Async XLA Ops:
  3.3 8.8 %collective-permute-start = (bf16[32,1024]{1,0:T(8,128)(2,1)S(1)}, bf16[32,1024]{1,0:T(8,128)(2,1)S(1)}, u32[]{:S(2)}, u32[]{:S(2)}) collective-permute-start(bf16[32,1024]{1,0:T(8,128)(2,1)S(1)} %get-tuple-element.21), channel_id=1, source_target_pairs={{0,24},{8,16},{16,8},{24,0},{1,25},{9,17},{17,9},{25,1},{2,26},{10... | collective-permute-start | bytes 196616 | tf_op jit(solution)/shard_map/ppermute | solution.py:336
  8.5 5.6 %collective-permute-start.1 = (bf16[32,1024]{1,0:T(8,128)(2,1)S(1)}, bf16[32,1024]{1,0:T(8,128)(2,1)S(1)}, u32[]{:S(2)}, u32[]{:S(2)}) collective-permute-start(bf16[32,1024]{1,0:T(8,128)(2,1)S(1)} %get-tuple-element.22), channel_id=1, source_target_pairs={{0,16},{8,24},{16,0},{24,8},{1,17},{9,25},{17,1},{25,9},{2,18},{10... | collective-permute-start | bytes 196616 | tf_op jit(solution)/shard_map/ppermute | solution.py:336
  8.5 5.6 %collective-permute-start.2 = (bf16[32,1024]{1,0:T(8,128)(2,1)S(1)}, bf16[32,1024]{1,0:T(8,128)(2,1)S(1)}, u32[]{:S(2)}, u32[]{:S(2)}) collective-permute-start(bf16[32,1024]{1,0:T(8,128)(2,1)S(1)} %get-tuple-element.23), channel_id=1, source_target_pairs={{0,8},{8,0},{16,24},{24,16},{1,9},{9,1},{17,25},{25,17},{2,10},{10... | collective-permute-start | bytes 196616 | tf_op jit(solution)/shard_map/ppermute | solution.py:336
  14.1 5.4 %collective-permute-start.3 = (bf16[32,1024]{1,0:T(8,128)(2,1)S(1)}, bf16[32,1024]{1,0:T(8,128)(2,1)S(1)}, u32[]{:S(2)}, u32[]{:S(2)}) collective-permute-start(bf16[32,1024]{1,0:T(8,128)(2,1)S(1)} %share.1), channel_id=1, source_target_pairs={{0,8},{8,0},{16,24},{24,16},{1,9},{9,1},{17,25},{25,17},{2,10},{10... | collective-permute-start | bytes 196616 | tf_op jit(solution)/shard_map/ppermute | solution.py:336
  15.3 8.0 %collective-permute-start.5 = (bf16[32,1024]{1,0:T(8,128)(2,1)S(1)}, bf16[32,1024]{1,0:T(8,128)(2,1)S(1)}, u32[]{:S(2)}, u32[]{:S(2)}) collective-permute-start(bf16[32,1024]{1,0:T(8,128)(2,1)S(1)} %share.1), channel_id=1, source_target_pairs={{0,24},{8,16},{16,8},{24,0},{1,25},{9,17},{17,9},{25,1},{2,26},{10... | collective-permute-start | bytes 196616 | tf_op jit(solution)/shard_map/ppermute | solution.py:336
  17.2 6.0 %collective-permute-start.4 = (bf16[32,1024]{1,0:T(8,128)(2,1)S(1)}, bf16[32,1024]{1,0:T(8,128)(2,1)S(1)}, u32[]{:S(2)}, u32[]{:S(2)}) collective-permute-start(bf16[32,1024]{1,0:T(8,128)(2,1)S(1)} %share.1), channel_id=1, source_target_pairs={{0,16},{8,24},{16,0},{24,8},{1,17},{9,25},{17,1},{25,9},{2,18},{10... | collective-permute-start | bytes 196616 | tf_op jit(solution)/shard_map/ppermute | solution.py:336
  19.5 5.6 %collective-permute-start.12 = (bf16[64,1024]{1,0:T(8,128)(2,1)S(1)}, bf16[64,1024]{1,0:T(8,128)(2,1)S(1)}, u32[]{:S(2)}, u32[]{:S(2)}) collective-permute-start(bf16[64,1024]{1,0:T(8,128)(2,1)S(1)} %pad_maximum_fusion.refs_0_), channel_id=1, source_target_pairs={{0,1},{1,0},{2,3},{3,2},{4,5},{5,4},{6,7},{7,6},{8,9},{9,8},{10,11... | collective-permute-start | bytes 393224 | tf_op jit(solution)/shard_map/ppermute | solution.py:336
  19.6 7.0 %collective-permute-start.8 = (bf16[64,1024]{1,0:T(8,128)(2,1)S(1)}, bf16[64,1024]{1,0:T(8,128)(2,1)S(1)}, u32[]{:S(2)}, u32[]{:S(2)}) collective-permute-start(bf16[64,1024]{1,0:T(8,128)(2,1)S(1)} %pad_maximum_fusion.refs_0_), channel_id=1, source_target_pairs={{0,2},{1,5},{2,0},{3,7},{4,6},{5,1},{6,4},{7,3},{8,10},{9,13},{10,... | collective-permute-start | bytes 393224 | tf_op jit(solution)/shard_map/ppermute | solution.py:336
  20.1 6.4 %collective-permute-start.6 = (bf16[64,1024]{1,0:T(8,128)(2,1)S(1)}, bf16[64,1024]{1,0:T(8,128)(2,1)S(1)}, u32[]{:S(2)}, u32[]{:S(2)}) collective-permute-start(bf16[64,1024]{1,0:T(8,128)(2,1)S(1)} %pad_maximum_fusion.refs_0_), channel_id=1, source_target_pairs={{0,4},{1,3},{2,6},{3,1},{4,0},{5,7},{6,2},{7,5},{8,12},{9,11},{10,... | collective-permute-start | bytes 393224 | tf_op jit(solution)/shard_map/ppermute | solution.py:336
  23.3 5.6 %collective-permute-start.7 = (bf16[64,1024]{1,0:T(8,128)(2,1)S(1)}, bf16[64,1024]{1,0:T(8,128)(2,1)S(1)}, u32[]{:S(2)}, u32[]{:S(2)}) collective-permute-start(bf16[64,1024]{1,0:T(8,128)(2,1)S(1)} %constant_dynamic-update-slice_fusion.refs_1_), channel_id=1, source_target_pairs={{0,4},{1,3},{2,6},{3,1},{4,0},{5,7},{6,2},{7,5},{8,12},{9,11},{10,... | collective-permute-start | bytes 393224 | tf_op jit(solution)/shard_map/ppermute | solution.py:336
  25.0 5.3 %collective-permute-start.13 = (bf16[64,1024]{1,0:T(8,128)(2,1)S(1)}, bf16[64,1024]{1,0:T(8,128)(2,1)S(1)}, u32[]{:S(2)}, u32[]{:S(2)}) collective-permute-start(bf16[64,1024]{1,0:T(8,128)(2,1)S(1)} %constant_dynamic-update-slice_fusion.refs_1_), channel_id=1, source_target_pairs={{0,1},{1,0},{2,3},{3,2},{4,5},{5,4},{6,7},{7,6},{8,9},{9,8},{10,11... | collective-permute-start | bytes 393224 | tf_op jit(solution)/shard_map/ppermute | solution.py:336
  25.0 5.3 %collective-permute-start.9 = (bf16[64,1024]{1,0:T(8,128)(2,1)S(1)}, bf16[64,1024]{1,0:T(8,128)(2,1)S(1)}, u32[]{:S(2)}, u32[]{:S(2)}) collective-permute-start(bf16[64,1024]{1,0:T(8,128)(2,1)S(1)} %constant_dynamic-update-slice_fusion.refs_1_), channel_id=1, source_target_pairs={{0,2},{1,5},{2,0},{3,7},{4,6},{5,1},{6,4},{7,3},{8,10},{9,13},{10,... | collective-permute-start | bytes 393224 | tf_op jit(solution)/shard_map/ppermute | solution.py:336
  26.5 4.3 %collective-permute-start.16 = (bf16[64,1024]{1,0:T(8,128)(2,1)S(1)}, bf16[64,1024]{1,0:T(8,128)(2,1)S(1)}, u32[]{:S(2)}, u32[]{:S(2)}) collective-permute-start(bf16[64,1024]{1,0:T(8,128)(2,1)S(1)} %collective-permute-done.8.refs_4_), channel_id=1, source_target_pairs={{0,1},{1,0},{2,3},{3,2},{4,5},{5,4},{6,7},{7,6},{8,9},{9,8},{10,11... | collective-permute-start | bytes 393224 | tf_op jit(solution)/shard_map/ppermute | solution.py:336
  26.5 5.0 %collective-permute-start.10 = (bf16[64,1024]{1,0:T(8,128)(2,1)S(1)}, bf16[64,1024]{1,0:T(8,128)(2,1)S(1)}, u32[]{:S(2)}, u32[]{:S(2)}) collective-permute-start(bf16[64,1024]{1,0:T(8,128)(2,1)S(1)} %collective-permute-done.6.refs_2_), channel_id=1, source_target_pairs={{0,2},{1,5},{2,0},{3,7},{4,6},{5,1},{6,4},{7,3},{8,10},{9,13},{10,... | collective-permute-start | bytes 393224 | tf_op jit(solution)/shard_map/ppermute | solution.py:336
  28.9 5.0 %collective-permute-start.11 = (bf16[64,1024]{1,0:T(8,128)(2,1)S(1)}, bf16[64,1024]{1,0:T(8,128)(2,1)S(1)}, u32[]{:S(2)}, u32[]{:S(2)}) collective-permute-start(bf16[64,1024]{1,0:T(8,128)(2,1)S(1)} %collective-permute-done.7.refs_3_), channel_id=1, source_target_pairs={{0,2},{1,5},{2,0},{3,7},{4,6},{5,1},{6,4},{7,3},{8,10},{9,13},{10,... | collective-permute-start | bytes 393224 | tf_op jit(solution)/shard_map/ppermute | solution.py:336
  30.4 3.5 %collective-permute-start.14 = (bf16[64,1024]{1,0:T(8,128)(2,1)S(1)}, bf16[64,1024]{1,0:T(8,128)(2,1)S(1)}, u32[]{:S(2)}, u32[]{:S(2)}) collective-permute-start(bf16[64,1024]{1,0:T(8,128)(2,1)S(1)} %collective-permute-done.6.refs_2_), channel_id=1, source_target_pairs={{0,1},{1,0},{2,3},{3,2},{4,5},{5,4},{6,7},{7,6},{8,9},{9,8},{10,11... | collective-permute-start | bytes 393224 | tf_op jit(solution)/shard_map/ppermute | solution.py:336
  30.4 3.5 %collective-permute-start.15 = (bf16[64,1024]{1,0:T(8,128)(2,1)S(1)}, bf16[64,1024]{1,0:T(8,128)(2,1)S(1)}, u32[]{:S(2)}, u32[]{:S(2)}) collective-permute-start(bf16[64,1024]{1,0:T(8,128)(2,1)S(1)} %collective-permute-done.7.refs_3_), channel_id=1, source_target_pairs={{0,1},{1,0},{2,3},{3,2},{4,5},{5,4},{6,7},{7,6},{8,9},{9,8},{10,11... | collective-permute-start | bytes 393224 | tf_op jit(solution)/shard_map/ppermute | solution.py:336
  30.9 3.0 %collective-permute-start.17 = (bf16[64,1024]{1,0:T(8,128)(2,1)S(1)}, bf16[64,1024]{1,0:T(8,128)(2,1)S(1)}, u32[]{:S(2)}, u32[]{:S(2)}) collective-permute-start(bf16[64,1024]{1,0:T(8,128)(2,1)S(1)} %collective-permute-done.9.refs_5_), channel_id=1, source_target_pairs={{0,1},{1,0},{2,3},{3,2},{4,5},{5,4},{6,7},{7,6},{8,9},{9,8},{10,11... | collective-permute-start | bytes 393224 | tf_op jit(solution)/shard_map/ppermute | solution.py:336
  31.6 2.3 %collective-permute-start.18 = (bf16[64,1024]{1,0:T(8,128)(2,1)S(1)}, bf16[64,1024]{1,0:T(8,128)(2,1)S(1)}, u32[]{:S(2)}, u32[]{:S(2)}) collective-permute-start(bf16[64,1024]{1,0:T(8,128)(2,1)S(1)} %collective-permute-done.10.refs_6_), channel_id=1, source_target_pairs={{0,1},{1,0},{2,3},{3,2},{4,5},{5,4},{6,7},{7,6},{8,9},{9,8},{10,11... | collective-permute-start | bytes 393224 | tf_op jit(solution)/shard_map/ppermute | solution.py:336
  33.9 1.3 %collective-permute-start.19 = (bf16[64,1024]{1,0:T(8,128)(2,1)S(1)}, bf16[64,1024]{1,0:T(8,128)(2,1)S(1)}, u32[]{:S(2)}, u32[]{:S(2)}) collective-permute-start(bf16[64,1024]{1,0:T(8,128)(2,1)S(1)} %collective-permute-done.11.refs_7_), channel_id=1, source_target_pairs={{0,1},{1,0},{2,3},{3,2},{4,5},{5,4},{6,7},{7,6},{8,9},{9,8},{10,11... | collective-permute-start | bytes 393224 | tf_op jit(solution)/shard_map/ppermute | solution.py:336
  48.1 6.3 %collective-permute-start.21 = (bf16[144,256]{1,0:T(8,128)(2,1)S(1)}, bf16[144,256]{1,0:T(8,128)(2,1)S(1)}, u32[]{:S(2)}, u32[]{:S(2)}) collective-permute-start(bf16[144,256]{1,0:T(8,128)(2,1)S(1)} %sums.1.refs_0_), channel_id=1, source_target_pairs={{0,16},{8,24},{16,0},{24,8},{1,17},{9,25},{17,1},{25,9},{2,18},{10... | collective-permute-start | bytes 221192 | tf_op jit(solution)/shard_map/ppermute | solution.py:336
  48.8 8.3 %collective-permute-start.20 = (bf16[144,256]{1,0:T(8,128)(2,1)S(1)}, bf16[144,256]{1,0:T(8,128)(2,1)S(1)}, u32[]{:S(2)}, u32[]{:S(2)}) collective-permute-start(bf16[144,256]{1,0:T(8,128)(2,1)S(1)} %sums.1.refs_0_), channel_id=1, source_target_pairs={{0,8},{8,0},{16,24},{24,16},{1,9},{9,1},{17,25},{25,17},{2,10},{10... | collective-permute-start | bytes 221192 | tf_op jit(solution)/shard_map/ppermute | solution.py:336
  54.4 4.4 %collective-permute-start.22 = (bf16[144,256]{1,0:T(8,128)(2,1)S(1)}, bf16[144,256]{1,0:T(8,128)(2,1)S(1)}, u32[]{:S(2)}, u32[]{:S(2)}) collective-permute-start(bf16[144,256]{1,0:T(8,128)(2,1)S(1)} %collective-permute-done.21.refs_2_), channel_id=1, source_target_pairs={{0,8},{8,0},{16,24},{24,16},{1,9},{9,1},{17,25},{25,17},{2,10},{10... | collective-permute-start | bytes 221192 | tf_op jit(solution)/shard_map/ppermute | solution.py:336

commit v3 on v2

--- a/solution.py
+++ b/solution.py
@@ -98,14 +98,50 @@
     )(*[pltpu.with_memory_space_constraint(x, pltpu.HBM) for x in (codes_t, book_t, residuals)])
 
 
-def polar_kernel(*refs, blocks, pieces, chunk):
+def early_kernel(*refs, chunk):
+    *block_refs, raw, gram, gram_b = refs
+    at = 0
+    for block in block_refs:
+        raw[pl.ds(at, block.shape[0]), :] = block[...]
+        at += block.shape[0]
+    for j in range(at // chunk):
+        cols = pl.ds(j * chunk, chunk)
+        rows = pl.ds(j * chunk, at - j * chunk)
+        part = dot_nt(raw[rows, :], raw[cols, :])
+        gram[rows, cols] = part
+        rounded = part.astype(bf16)
+        gram_b[rows, cols] = rounded
+        if (j + 1) * chunk < at:
+            gram_b[cols, pl.ds((j + 1) * chunk, at - (j + 1) * chunk)] = rounded[chunk:, :].T
+
+
+def early_gram(blocks, chunk):
+    rows, dim = sum(block.shape[0] for block in blocks), blocks[0].shape[1]
+    vmem = pl.BlockSpec(memory_space=pltpu.VMEM)
+    return pl.pallas_call(
+        functools.partial(early_kernel, chunk=chunk),
+        out_shape=(
+            jax.ShapeDtypeStruct((rows, dim), bf16),
+            jax.ShapeDtypeStruct((rows, rows), f32),
+            jax.ShapeDtypeStruct((rows, rows), bf16),
+        ),
+        in_specs=[vmem] * len(blocks),
+        out_specs=(vmem,) * 3,
+        compiler_params=pltpu.CompilerParams(vmem_limit_bytes=16 * MIB),
+        name="early_gram",
+    )(*blocks)
+
+
+def polar_kernel(early_raw, early, early_b, *refs, blocks, pieces, chunk):
     block_refs = refs[:blocks]
     rot_b = refs[blocks]
     raw, gram, gram_b, poly_b, iterate, iterate_b, turned = refs[blocks + 1 :]
     dim = raw.shape[0]
     own = rot_b.shape[0]
     steps = dim // chunk
-    at = 0
+    known = early_raw.shape[0]
+    raw[pl.ds(0, known), :] = early_raw[...]
+    at = known
     for block in block_refs:
         raw[pl.ds(at, block.shape[0]), :] = block[...]
         at += block.shape[0]
@@ -123,20 +159,30 @@
         if j < steps - 1:
             target[cols, pl.ds((j + 1) * chunk, dim - (j + 1) * chunk)] = rounded[chunk:, :].T
 
-    def gram_of(source, transposed=None):
+    def first_gram():
         r = lax.broadcasted_iota(jnp.int32, (chunk, chunk), 0)
         c = lax.broadcasted_iota(jnp.int32, (chunk, chunk), 1)
-        trace = jnp.zeros((), f32)
+        rest = pl.ds(known, dim - known)
+        part = dot_nt(raw[...], raw[rest, :])
+        rounded = part.astype(bf16)
+        gram_b[pl.ds(0, known), pl.ds(0, known)] = early_b[...]
+        gram_b[:, rest] = rounded
+        gram_b[rest, pl.ds(0, known)] = rounded[:known, :].T
+        gram[rest, rest] = part[known:, :]
+        trace = jnp.sum(jnp.where(r == c, part[known:, :], 0.0))
+        for j in range(known // chunk):
+            rows, cols = pl.ds(j * chunk, known - j * chunk), band_of(j)
+            gram[rows, cols] = early[rows, cols]
+            gram[rest, cols] = part[j * chunk : (j + 1) * chunk, :].T
+            trace = trace + jnp.sum(jnp.where(r == c, early[cols, cols], 0.0))
+        return trace
+
+    def gram_of(source, transposed):
         for j in range(steps):
             rows, cols = lower(j)
-            if transposed is None:
-                part = dot_nt(source[rows, :], source[cols, :])
-            else:
-                part = dot(source[rows, :], transposed[:, cols])
+            part = dot(source[rows, :], transposed[:, cols])
             gram[rows, cols] = part
             mirror(gram_b, j, part)
-            trace = trace + jnp.sum(jnp.where(r == c, part[:chunk, :], 0.0))
-        return trace
 
     def poly_of(wb, wc):
         for j in range(steps):
@@ -144,7 +190,7 @@
             square = dot(gram_b[rows, :], gram_b[:, cols])
             mirror(poly_b, j, wb * gram[rows, cols] + wc * square)
 
-    frob = gram_of(raw)
+    frob = first_gram()
     scale2 = 1.0 / (frob + epsilon)
     scale = lax.rsqrt(frob + epsilon)
     poly_of(quintic_b * scale2, quintic_c * scale2 * scale2)
@@ -273,14 +319,14 @@
         rotated_ref[rows, :] = dot_nt(res_ref[rows, :], rot_ref[...])
 
 
-def polar(block_list, own, pieces):
+def polar(early, block_list, own, pieces, chunk):
     dim = block_list[0].shape[1]
     vmem = pl.BlockSpec(memory_space=pltpu.VMEM)
-    kernel = functools.partial(polar_kernel, blocks=len(block_list), pieces=pieces, chunk=256)
+    kernel = functools.partial(polar_kernel, blocks=len(block_list), pieces=pieces, chunk=chunk)
     return pl.pallas_call(
         kernel,
         out_shape=jax.ShapeDtypeStruct((own, dim), bf16),
-        in_specs=[vmem] * len(block_list),
+        in_specs=[vmem] * (3 + len(block_list)),
         out_specs=vmem,
         scratch_shapes=[
             pltpu.VMEM((dim, dim), bf16),
@@ -293,7 +339,7 @@
         ],
         compiler_params=pltpu.CompilerParams(vmem_limit_bytes=30 * MIB),
         name="polar",
-    )(*block_list)
+    )(*early, *block_list)
 
 
 def share_kernel(*refs):
@@ -377,18 +423,20 @@
         far = strides[:-1]
         for even, odd in zip(far, far[::-1]):
             held = held + [swap(t, "code", code, even, odd) for t in held]
-        for stride in strides[-1:]:
-            held = held + [swap(t, "code", code, stride) for t in held]
-        rotation_t = polar(held, own, 1 if thin else dp)
+        chunk = 256
+        near, last = strides[-1:], held.pop()
+        held += [swap(t, "code", code, stride) for stride in near for t in held]
+        count = (dim - chunk) // last.shape[0]
+        early = early_gram(held[:count], chunk)
+        last, early = lax.optimization_barrier((last, early))
+        held = held[count:] + [last] + [swap(last, "code", code, stride) for stride in near]
+        rotation_t = polar(early, held, own, 1 if thin else dp, chunk)
         scratch = [pltpu.VMEM((own, words), f32)]
         operands = (rotation_t, res_t, *ready)
         sums = small_call(sums_kernel, "sums", (own + subs, words), bf16, *operands, scratch=scratch)
         rotated = small_call(rotated_kernel, "rotated", (rows, own), f32, rotation_t, res_v)
-        totals = {0: sums}
-        for k in sorted(range(1, dp), key=lambda k: (bin(k).count("1"), k)):
-            totals[k] = swap(totals[k & (k - 1)], "dp", dp, k & -k)
-        totals = [totals[k] for k in range(dp)]
-        book = small_call(book_kernel, "book", (own, words), f32, book_v, *totals)
+        others = [swap(sums, "dp", dp, k) for k in far_first]
+        book = small_call(book_kernel, "book", (own, words), f32, book_v, sums, *others)
         return rotated, jnp.transpose(book.reshape(subs, width, words), (0, 2, 1))
 
     return body

time: 59.6 us -> 59.8 us (level)
  waiting for transfers between devices: 16.7 us -> 10.8 us
  starting transfers between devices: 20 us -> 25 us
  Pallas kernels: 22 us -> 23.1 us
    ppermute x23, waiting for transfers between devices: 16.7 us -> 10.8 us  [swap(): lax.ppermute(value, axis, [(i, i ^ (odd_mask if i % 2 else mask)) for i i...]
    ppermute x23, starting transfers between devices: 20 us -> 25 us  [swap(): lax.ppermute(value, axis, [(i, i ^ (odd_mask if i % 2 else mask)) for i i...]
    pallas_call x0 -> x1, Pallas kernels: none -> 1.11 us  [early_gram(): pl.pallas_call(functools.partial(early_kernel, chunk=chunk), out_shape=(j...]
  transfers between devices with their start and end apart: 23 -> 23, of which waited for: 9 -> 10; matrix products, arithmetic and copies ran while one was open for 0% -> 0% of each run, Pallas kernels for 10% -> 11%
where the time goes in v3:
time: 59.8 us; the launch traced here: 59.6 us
  starting transfers between devices  25 us (42%)
  Pallas kernels  23.1 us (39%)
  waiting for transfers between devices  10.8 us (18%)
  between operations  0.72 us (1%)
    ppermute x23, starting transfers between devices, swap(): lax.ppermute(value, axis, [(i, i ^ (odd_mask if i % 2 else mask)) for i i...  25 us
    pallas_call x1, Pallas kernels, polar(): pl.pallas_call(kernel, out_shape=jax.ShapeDtypeStruct((own, dim), bf16),...  11.5 us
    ppermute x23, waiting for transfers between devices, swap(): lax.ppermute(value, axis, [(i, i ^ (odd_mask if i % 2 else mask)) for i i...  10.8 us
    pallas_call x4, Pallas kernels, small_call(): pl.pallas_call(kernel, out_shape=jax.ShapeDtypeStruct(shape, dtype), in_s...  4.84 us
    pallas_call x1, Pallas kernels, onehot_call(): pl.pallas_call(onehot_kernel, out_shape=(jax.ShapeDtypeStruct((rows, subs...  3 us
    pallas_call x1, Pallas kernels, cross_partial(): pl.pallas_call(functools.partial(cross_kernel, dp=dp), out_shape=shapes,...  2.71 us
  transfers between devices with their start and end apart: 23, of which 10 were waited for; matrix products, arithmetic and copies ran while one was open for 0% of the time, Pallas kernels for 11%

profile of v3, /device:TPU:0, one launch (start us, length us, event | category | flops | bytes accessed | tf_op | source)
XLA Modules:
  0.0 59.6 jit_solution(16179064178262405050)
XLA Ops:
  0.6 2.7 %cross_partial.1 = (f32[32,1024]{1,0:T(8,128)S(1)}, bf16[32,1024]{1,0:T(8,128)(2,1)S(1)}, bf16[32,1024]{1,0:T(8,128)(2,1)S(1)}, bf16[32,1024]{1,0:T(8,128)(2,1)S...) custom-call(s32[16,2048]{1,0:T(8,128)} %bitcast.7, f32[128,256]{1,0:T(8,128)} %bitcast.8, ...), custom_call_target="tpu_custom_call" | custom-call | tf_op jit(solution)/shard_map/cross_partial/pallas_call | solution.py:86
  3.3 5.1 %collective-permute-start = (bf16[32,1024]{1,0:T(8,128)(2,1)S(1)}, bf16[32,1024]{1,0:T(8,128)(2,1)S(1)}, u32[]{:S(2)}, u32[]{:S(2)}) collective-permute-start(bf16[32,1024]{1,0:T(8,128)(2,1)S(1)} %get-tuple-element.28), channel_id=1, source_target_pairs={{0,24},{8,16},{16,8},{24,0},{1,25},{9,17},{17,9},{25,1},{2,26},{10... | collective-permute-start | bytes 196616 | tf_op jit(solution)/shard_map/ppermute | solution.py:382
  8.5 0.0 collective-permute-start.1
  8.5 0.6 %collective-permute-start.2 = (bf16[32,1024]{1,0:T(8,128)(2,1)S(1)}, bf16[32,1024]{1,0:T(8,128)(2,1)S(1)}, u32[]{:S(2)}, u32[]{:S(2)}) collective-permute-start(bf16[32,1024]{1,0:T(8,128)(2,1)S(1)} %get-tuple-element.30), channel_id=1, source_target_pairs={{0,8},{8,0},{16,24},{24,16},{1,9},{9,1},{17,25},{25,17},{2,10},{10... | collective-permute-start | bytes 196616 | tf_op jit(solution)/shard_map/ppermute | solution.py:382
  9.1 3.0 %onehot.1 = (bf16[2048,1024]{1,0:T(8,128)(2,1)S(1)}, bf16[512,2048]{1,0:T(8,128)(2,1)S(1)}, f32[16,256]{1,0:T(8,128)S(1)}, bf16[1024,2048]{1,0:T(8,128)(2,1)S(1)}) custom-call(s32[16,2048]{1,0:T(8,128)S(1)} %get-tuple-element.31.codes_ref, bf16[2048,1024]{1,0:T(8,128)(2,1)S(1)} %get-tuple-element.32.res_ref), custom_call_target="tpu_custom_call" | custom-call | flops 1073741824 | bytes 4194304 | tf_op jit(solution)/shard_map/onehot/pallas_call | solution.py:269
  12.1 0.0 collective-permute-done.refs_1_
  12.1 1.9 %collective-permute-done.1.refs_2_ = bf16[32,1024]{1,0:T(8,128)(2,1)S(1)} collective-permute-done((bf16[32,1024]{1,0:T(8,128)(2,1)S(1)}, bf16[32,1024]{1,0:T(8,128)(2,1)S(1)}, u32[]{:S(2)}, u32[]{:S(2)}) %collective-permute-start.1) | collective-permute-done | bytes 65568 | tf_op jit(solution)/shard_map/ppermute | solution.py:382
  14.1 0.0 collective-permute-done.2.refs_3_
  14.1 1.1 %collective-permute-start.7 = (bf16[32,1024]{1,0:T(8,128)(2,1)S(1)}, bf16[32,1024]{1,0:T(8,128)(2,1)S(1)}, u32[]{:S(2)}, u32[]{:S(2)}) collective-permute-start(bf16[32,1024]{1,0:T(8,128)(2,1)S(1)} %share.1), channel_id=1, source_target_pairs={{0,8},{8,0},{16,24},{24,16},{1,9},{9,1},{17,25},{25,17},{2,10},{10... | collective-permute-start | bytes 196616 | tf_op jit(solution)/shard_map/ppermute | solution.py:382
  15.3 2.2 %collective-permute-start.3 = (bf16[32,1024]{1,0:T(8,128)(2,1)S(1)}, bf16[32,1024]{1,0:T(8,128)(2,1)S(1)}, u32[]{:S(2)}, u32[]{:S(2)}) collective-permute-start(bf16[32,1024]{1,0:T(8,128)(2,1)S(1)} %share.1), channel_id=1, source_target_pairs={{0,16},{8,24},{16,0},{24,8},{1,17},{9,25},{17,1},{25,9},{2,18},{10... | collective-permute-start | bytes 196616 | tf_op jit(solution)/shard_map/ppermute | solution.py:382
  17.5 1.1 %collective-permute-start.4 = (bf16[32,1024]{1,0:T(8,128)(2,1)S(1)}, bf16[32,1024]{1,0:T(8,128)(2,1)S(1)}, u32[]{:S(2)}, u32[]{:S(2)}) collective-permute-start(bf16[32,1024]{1,0:T(8,128)(2,1)S(1)} %share.1), channel_id=1, source_target_pairs={{0,24},{8,16},{16,8},{24,0},{1,25},{9,17},{17,9},{25,1},{2,26},{10... | collective-permute-start | bytes 196616 | tf_op jit(solution)/shard_map/ppermute | solution.py:382
  18.6 0.3 collective-permute-done.7
  18.8 1.8 %collective-permute-start.8 = (bf16[64,1024]{1,0:T(8,128)(2,1)S(1)}, bf16[64,1024]{1,0:T(8,128)(2,1)S(1)}, u32[]{:S(2)}, u32[]{:S(2)}) collective-permute-start(bf16[64,1024]{1,0:T(8,128)(2,1)S(1)} %pad_maximum_fusion.refs_0_), channel_id=1, source_target_pairs={{0,4},{1,3},{2,6},{3,1},{4,0},{5,7},{6,2},{7,5},{8,12},{9,11},{10,... | collective-permute-start | bytes 393224 | tf_op jit(solution)/shard_map/ppermute | solution.py:382
  20.6 1.5 %collective-permute-start.9 = (bf16[64,1024]{1,0:T(8,128)(2,1)S(1)}, bf16[64,1024]{1,0:T(8,128)(2,1)S(1)}, u32[]{:S(2)}, u32[]{:S(2)}) collective-permute-start(bf16[64,1024]{1,0:T(8,128)(2,1)S(1)} %pad_maximum_fusion.refs_0_), channel_id=1, source_target_pairs={{0,2},{1,5},{2,0},{3,7},{4,6},{5,1},{6,4},{7,3},{8,10},{9,13},{10,... | collective-permute-start | bytes 393224 | tf_op jit(solution)/shard_map/ppermute | solution.py:382
  22.1 0.0 collective-permute-start.12
  22.1 0.0 collective-permute-done.3
  22.1 1.4 %collective-permute-done.4 = bf16[32,1024]{1,0:T(8,128)(2,1)S(1)} collective-permute-done((bf16[32,1024]{1,0:T(8,128)(2,1)S(1)}, bf16[32,1024]{1,0:T(8,128)(2,1)S(1)}, u32[]{:S(2)}, u32[]{:S(2)}) %collective-permute-start.4) | collective-permute-done | bytes 65568 | tf_op jit(solution)/shard_map/ppermute | solution.py:382
  23.5 1.5 %collective-permute-start.5 = (bf16[64,1024]{1,0:T(8,128)(2,1)S(1)}, bf16[64,1024]{1,0:T(8,128)(2,1)S(1)}, u32[]{:S(2)}, u32[]{:S(2)}) collective-permute-start(bf16[64,1024]{1,0:T(8,128)(2,1)S(1)} %constant_dynamic-update-slice_fusion.refs_1_), channel_id=1, source_target_pairs={{0,4},{1,3},{2,6},{3,1},{4,0},{5,7},{6,2},{7,5},{8,12},{9,11},{10,... | collective-permute-start | bytes 393224 | tf_op jit(solution)/shard_map/ppermute | solution.py:382
  25.0 1.5 %collective-permute-start.10 = (bf16[64,1024]{1,0:T(8,128)(2,1)S(1)}, bf16[64,1024]{1,0:T(8,128)(2,1)S(1)}, u32[]{:S(2)}, u32[]{:S(2)}) collective-permute-start(bf16[64,1024]{1,0:T(8,128)(2,1)S(1)} %constant_dynamic-update-slice_fusion.refs_1_), channel_id=1, source_target_pairs={{0,2},{1,5},{2,0},{3,7},{4,6},{5,1},{6,4},{7,3},{8,10},{9,13},{10,... | collective-permute-start | bytes 393224 | tf_op jit(solution)/shard_map/ppermute | solution.py:382
  26.5 0.0 collective-permute-done.8.refs_2_
  26.5 0.0 collective-permute-start.13
  26.5 0.0 collective-permute-done.9.refs_4_
  26.5 1.7 %collective-permute-start.11 = (bf16[64,1024]{1,0:T(8,128)(2,1)S(1)}, bf16[64,1024]{1,0:T(8,128)(2,1)S(1)}, u32[]{:S(2)}, u32[]{:S(2)}) collective-permute-start(bf16[64,1024]{1,0:T(8,128)(2,1)S(1)} %collective-permute-done.8.refs_2_), channel_id=1, source_target_pairs={{0,2},{1,5},{2,0},{3,7},{4,6},{5,1},{6,4},{7,3},{8,10},{9,13},{10,... | collective-permute-start | bytes 393224 | tf_op jit(solution)/shard_map/ppermute | solution.py:382
  28.3 0.0 collective-permute-done.12.refs_7_
  28.3 0.0 collective-permute-start.14
  28.3 0.2 collective-permute-done.5.refs_3_
  28.5 0.3 collective-permute-start.16
  28.8 1.2 %collective-permute-done.10.refs_5_ = bf16[64,1024]{1,0:T(8,128)(2,1)S(1)} collective-permute-done((bf16[64,1024]{1,0:T(8,128)(2,1)S(1)}, bf16[64,1024]{1,0:T(8,128)(2,1)S(1)}, u32[]{:S(2)}, u32[]{:S(2)}) %collective-permute-start.10) | collective-permute-done | bytes 131104 | tf_op jit(solution)/shard_map/ppermute | solution.py:382
  30.0 0.0 collective-permute-start.15
  30.0 0.0 collective-permute-done.13.refs_8_
  30.0 1.5 %collective-permute-start.6 = (bf16[64,1024]{1,0:T(8,128)(2,1)S(1)}, bf16[64,1024]{1,0:T(8,128)(2,1)S(1)}, u32[]{:S(2)}, u32[]{:S(2)}) collective-permute-start(bf16[64,1024]{1,0:T(8,128)(2,1)S(1)} %collective-permute-done.5.refs_3_), channel_id=1, source_target_pairs={{0,2},{1,5},{2,0},{3,7},{4,6},{5,1},{6,4},{7,3},{8,10},{9,13},{10,... | collective-permute-start | bytes 393224 | tf_op jit(solution)/shard_map/ppermute | solution.py:382
  31.5 0.1 collective-permute-done.11.refs_6_
  31.6 0.0 collective-permute-start.17
  31.6 0.0 collective-permute-done.14.refs_9_
  31.6 0.0 collective-permute-done.16.refs_11_
  31.6 0.0 collective-permute-done.15.refs_10_
  31.6 1.1 %early_gram.1 = (bf16[768,1024]{1,0:T(8,128)(2,1)S(1)}, f32[768,768]{1,0:T(8,128)S(1)}, bf16[768,768]{1,0:T(8,128)(2,1)S(1)}) custom-call(bf16[64,1024]{1,0:T(8,128)(2,1)S(1)} %pad_maximum_fusion.refs_0_, bf16[64,1024]{1,0:T(8,128)(2,1)S(1)} %constant_dynamic-update-slice_fusion.refs_1_, bf16[64,1024]{1,0:T(8,128)(2,1)S(1)} %collective-permute-done.8.refs_2_, ...), custom_call_target="tpu_custom_call" | custom-call | tf_op jit(solution)/shard_map/early_gram/pallas_call | solution.py:121
  32.7 2.3 %collective-permute-done.6.refs_2_ = bf16[64,1024]{1,0:T(8,128)(2,1)S(1)} collective-permute-done((bf16[64,1024]{1,0:T(8,128)(2,1)S(1)}, bf16[64,1024]{1,0:T(8,128)(2,1)S(1)}, u32[]{:S(2)}, u32[]{:S(2)}) %collective-permute-start.6) | collective-permute-done | bytes 131104 | tf_op jit(solution)/shard_map/ppermute | solution.py:382
  35.0 0.0 collective-permute-start.19
  35.0 0.5 collective-permute-start.18
  35.5 0.0 collective-permute-done.17.refs_0_
  35.5 0.8 %collective-permute-done.19.refs_3_ = bf16[64,1024]{1,0:T(8,128)(2,1)S(1)} collective-permute-done((bf16[64,1024]{1,0:T(8,128)(2,1)S(1)}, bf16[64,1024]{1,0:T(8,128)(2,1)S(1)}, u32[]{:S(2)}, u32[]{:S(2)}) %collective-permute-start.19) | collective-permute-done | bytes 131104 | tf_op jit(solution)/shard_map/ppermute | solution.py:382
  36.3 0.2 collective-permute-done.18.refs_1_
  36.5 11.5 %polar.1.rot_ref = bf16[128,1024]{1,0:T(8,128)(2,1)S(1)} custom-call(bf16[768,1024]{1,0:T(8,128)(2,1)S(1)} %get-tuple-element.43.early_raw, f32[768,768]{1,0:T(8,128)S(1)} %get-tuple-element.44.early, bf16[768,768]{1,0:T(8,128)(2,1)S(1)} %get-tuple-element.45.early_b, bf16[64,1024]{1,0:T(8,128)(2,1)S(1)} %collective-permute-done.17.refs_0_, ...), custom_call_target="tpu_custom_call" | custom-call | tf_op jit(solution)/shard_map/polar/pallas_call | solution.py:326
  48.0 1.4 %sums.1.refs_0_ = bf16[144,256]{1,0:T(8,128)(2,1)S(1)} custom-call(bf16[128,1024]{1,0:T(8,128)(2,1)S(1)} %polar.1.rot_ref, bf16[1024,2048]{1,0:T(8,128)(2,1)S(1)} %get-tuple-element.48.res_ref, bf16[2048,1024]{1,0:T(8,128)(2,1)S(1)} %get-tuple-element.49.onehot_ref, bf16[512,2048]{1,0:T(8,128)(2,1)S(1)} %get-tuple-element.50.masks_ref, ...), custom_call_target="tpu_custom_call" | custom-call | tf_op jit(solution)/shard_map/sums/pallas_call | solution.py:369
  49.4 1.2 %collective-permute-start.20 = (bf16[144,256]{1,0:T(8,128)(2,1)S(1)}, bf16[144,256]{1,0:T(8,128)(2,1)S(1)}, u32[]{:S(2)}, u32[]{:S(2)}) collective-permute-start(bf16[144,256]{1,0:T(8,128)(2,1)S(1)} %sums.1.refs_0_), channel_id=1, source_target_pairs={{0,24},{8,16},{16,8},{24,0},{1,25},{9,17},{17,9},{25,1},{2,26},{10... | collective-permute-start | bytes 221192 | tf_op jit(solution)/shard_map/ppermute | solution.py:382
  50.6 0.0 collective-permute-start.21
  50.6 3.2 %collective-permute-start.22 = (bf16[144,256]{1,0:T(8,128)(2,1)S(1)}, bf16[144,256]{1,0:T(8,128)(2,1)S(1)}, u32[]{:S(2)}, u32[]{:S(2)}) collective-permute-start(bf16[144,256]{1,0:T(8,128)(2,1)S(1)} %sums.1.refs_0_), channel_id=1, source_target_pairs={{0,8},{8,0},{16,24},{24,16},{1,9},{9,1},{17,25},{25,17},{2,10},{10... | collective-permute-start | bytes 221192 | tf_op jit(solution)/shard_map/ppermute | solution.py:382
  53.8 2.7 %rotated.1 = f32[2048,128]{1,0:T(8,128)} custom-call(bf16[128,1024]{1,0:T(8,128)(2,1)S(1)} %polar.1.rot_ref, bf16[2048,1024]{1,0:T(8,128)(2,1)S(1)} %get-tuple-element.32.res_ref), custom_call_target="tpu_custom_call" | custom-call | tf_op jit(solution)/shard_map/rotated/pallas_call | solution.py:369
  56.5 0.0 collective-permute-done.20.refs_1_
  56.6 2.3 %collective-permute-done.21.refs_2_ = bf16[144,256]{1,0:T(8,128)(2,1)S(1)} collective-permute-done((bf16[144,256]{1,0:T(8,128)(2,1)S(1)}, bf16[144,256]{1,0:T(8,128)(2,1)S(1)}, u32[]{:S(2)}, u32[]{:S(2)}) %collective-permute-start.21) | collective-permute-done | bytes 73760 | tf_op jit(solution)/shard_map/ppermute | solution.py:382
  58.9 0.0 collective-permute-done.22.refs_3_
  58.9 0.7 %book.1 = f32[128,256]{1,0:T(8,128)} custom-call(f32[128,256]{1,0:T(8,128)S(1)} %get-tuple-element.47.book_ref, bf16[144,256]{1,0:T(8,128)(2,1)S(1)} %sums.1.refs_0_, bf16[144,256]{1,0:T(8,128)(2,1)S(1)} %collective-permute-done.20.refs_1_, bf16[144,256]{1,0:T(8,128)(2,1)S(1)} %collective-permute-done.21.refs_2_, ...), custom_call_target="tpu_custom_call" | custom-call | tf_op jit(solution)/shard_map/book/pallas_call | solution.py:369
  (4 shorter events, 0.1 us)
Async XLA Ops:
  3.3 8.8 %collective-permute-start = (bf16[32,1024]{1,0:T(8,128)(2,1)S(1)}, bf16[32,1024]{1,0:T(8,128)(2,1)S(1)}, u32[]{:S(2)}, u32[]{:S(2)}) collective-permute-start(bf16[32,1024]{1,0:T(8,128)(2,1)S(1)} %get-tuple-element.28), channel_id=1, source_target_pairs={{0,24},{8,16},{16,8},{24,0},{1,25},{9,17},{17,9},{25,1},{2,26},{10... | collective-permute-start | bytes 196616 | tf_op jit(solution)/shard_map/ppermute | solution.py:382
  8.5 5.6 %collective-permute-start.1 = (bf16[32,1024]{1,0:T(8,128)(2,1)S(1)}, bf16[32,1024]{1,0:T(8,128)(2,1)S(1)}, u32[]{:S(2)}, u32[]{:S(2)}) collective-permute-start(bf16[32,1024]{1,0:T(8,128)(2,1)S(1)} %get-tuple-element.29), channel_id=1, source_target_pairs={{0,16},{8,24},{16,0},{24,8},{1,17},{9,25},{17,1},{25,9},{2,18},{10... | collective-permute-start | bytes 196616 | tf_op jit(solution)/shard_map/ppermute | solution.py:382
  8.5 5.6 %collective-permute-start.2 = (bf16[32,1024]{1,0:T(8,128)(2,1)S(1)}, bf16[32,1024]{1,0:T(8,128)(2,1)S(1)}, u32[]{:S(2)}, u32[]{:S(2)}) collective-permute-start(bf16[32,1024]{1,0:T(8,128)(2,1)S(1)} %get-tuple-element.30), channel_id=1, source_target_pairs={{0,8},{8,0},{16,24},{24,16},{1,9},{9,1},{17,25},{25,17},{2,10},{10... | collective-permute-start | bytes 196616 | tf_op jit(solution)/shard_map/ppermute | solution.py:382
  14.1 4.7 %collective-permute-start.7 = (bf16[32,1024]{1,0:T(8,128)(2,1)S(1)}, bf16[32,1024]{1,0:T(8,128)(2,1)S(1)}, u32[]{:S(2)}, u32[]{:S(2)}) collective-permute-start(bf16[32,1024]{1,0:T(8,128)(2,1)S(1)} %share.1), channel_id=1, source_target_pairs={{0,8},{8,0},{16,24},{24,16},{1,9},{9,1},{17,25},{25,17},{2,10},{10... | collective-permute-start | bytes 196616 | tf_op jit(solution)/shard_map/ppermute | solution.py:382
  15.3 6.8 %collective-permute-start.3 = (bf16[32,1024]{1,0:T(8,128)(2,1)S(1)}, bf16[32,1024]{1,0:T(8,128)(2,1)S(1)}, u32[]{:S(2)}, u32[]{:S(2)}) collective-permute-start(bf16[32,1024]{1,0:T(8,128)(2,1)S(1)} %share.1), channel_id=1, source_target_pairs={{0,16},{8,24},{16,0},{24,8},{1,17},{9,25},{17,1},{25,9},{2,18},{10... | collective-permute-start | bytes 196616 | tf_op jit(solution)/shard_map/ppermute | solution.py:382
  17.5 6.1 %collective-permute-start.4 = (bf16[32,1024]{1,0:T(8,128)(2,1)S(1)}, bf16[32,1024]{1,0:T(8,128)(2,1)S(1)}, u32[]{:S(2)}, u32[]{:S(2)}) collective-permute-start(bf16[32,1024]{1,0:T(8,128)(2,1)S(1)} %share.1), channel_id=1, source_target_pairs={{0,24},{8,16},{16,8},{24,0},{1,25},{9,17},{17,9},{25,1},{2,26},{10... | collective-permute-start | bytes 196616 | tf_op jit(solution)/shard_map/ppermute | solution.py:382
  18.8 7.7 %collective-permute-start.8 = (bf16[64,1024]{1,0:T(8,128)(2,1)S(1)}, bf16[64,1024]{1,0:T(8,128)(2,1)S(1)}, u32[]{:S(2)}, u32[]{:S(2)}) collective-permute-start(bf16[64,1024]{1,0:T(8,128)(2,1)S(1)} %pad_maximum_fusion.refs_0_), channel_id=1, source_target_pairs={{0,4},{1,3},{2,6},{3,1},{4,0},{5,7},{6,2},{7,5},{8,12},{9,11},{10,... | collective-permute-start | bytes 393224 | tf_op jit(solution)/shard_map/ppermute | solution.py:382
  20.6 6.0 %collective-permute-start.9 = (bf16[64,1024]{1,0:T(8,128)(2,1)S(1)}, bf16[64,1024]{1,0:T(8,128)(2,1)S(1)}, u32[]{:S(2)}, u32[]{:S(2)}) collective-permute-start(bf16[64,1024]{1,0:T(8,128)(2,1)S(1)} %pad_maximum_fusion.refs_0_), channel_id=1, source_target_pairs={{0,2},{1,5},{2,0},{3,7},{4,6},{5,1},{6,4},{7,3},{8,10},{9,13},{10,... | collective-permute-start | bytes 393224 | tf_op jit(solution)/shard_map/ppermute | solution.py:382
  22.1 6.2 %collective-permute-start.12 = (bf16[64,1024]{1,0:T(8,128)(2,1)S(1)}, bf16[64,1024]{1,0:T(8,128)(2,1)S(1)}, u32[]{:S(2)}, u32[]{:S(2)}) collective-permute-start(bf16[64,1024]{1,0:T(8,128)(2,1)S(1)} %pad_maximum_fusion.refs_0_), channel_id=1, source_target_pairs={{0,1},{1,0},{2,3},{3,2},{4,5},{5,4},{6,7},{7,6},{8,9},{9,8},{10,11... | collective-permute-start | bytes 393224 | tf_op jit(solution)/shard_map/ppermute | solution.py:382
  23.5 5.0 %collective-permute-start.5 = (bf16[64,1024]{1,0:T(8,128)(2,1)S(1)}, bf16[64,1024]{1,0:T(8,128)(2,1)S(1)}, u32[]{:S(2)}, u32[]{:S(2)}) collective-permute-start(bf16[64,1024]{1,0:T(8,128)(2,1)S(1)} %constant_dynamic-update-slice_fusion.refs_1_), channel_id=1, source_target_pairs={{0,4},{1,3},{2,6},{3,1},{4,0},{5,7},{6,2},{7,5},{8,12},{9,11},{10,... | collective-permute-start | bytes 393224 | tf_op jit(solution)/shard_map/ppermute | solution.py:382
  25.0 5.0 %collective-permute-start.10 = (bf16[64,1024]{1,0:T(8,128)(2,1)S(1)}, bf16[64,1024]{1,0:T(8,128)(2,1)S(1)}, u32[]{:S(2)}, u32[]{:S(2)}) collective-permute-start(bf16[64,1024]{1,0:T(8,128)(2,1)S(1)} %constant_dynamic-update-slice_fusion.refs_1_), channel_id=1, source_target_pairs={{0,2},{1,5},{2,0},{3,7},{4,6},{5,1},{6,4},{7,3},{8,10},{9,13},{10,... | collective-permute-start | bytes 393224 | tf_op jit(solution)/shard_map/ppermute | solution.py:382
  26.5 3.5 %collective-permute-start.13 = (bf16[64,1024]{1,0:T(8,128)(2,1)S(1)}, bf16[64,1024]{1,0:T(8,128)(2,1)S(1)}, u32[]{:S(2)}, u32[]{:S(2)}) collective-permute-start(bf16[64,1024]{1,0:T(8,128)(2,1)S(1)} %constant_dynamic-update-slice_fusion.refs_1_), channel_id=1, source_target_pairs={{0,1},{1,0},{2,3},{3,2},{4,5},{5,4},{6,7},{7,6},{8,9},{9,8},{10,11... | collective-permute-start | bytes 393224 | tf_op jit(solution)/shard_map/ppermute | solution.py:382
  26.5 5.0 %collective-permute-start.11 = (bf16[64,1024]{1,0:T(8,128)(2,1)S(1)}, bf16[64,1024]{1,0:T(8,128)(2,1)S(1)}, u32[]{:S(2)}, u32[]{:S(2)}) collective-permute-start(bf16[64,1024]{1,0:T(8,128)(2,1)S(1)} %collective-permute-done.8.refs_2_), channel_id=1, source_target_pairs={{0,2},{1,5},{2,0},{3,7},{4,6},{5,1},{6,4},{7,3},{8,10},{9,13},{10,... | collective-permute-start | bytes 393224 | tf_op jit(solution)/shard_map/ppermute | solution.py:382
  28.3 3.3 %collective-permute-start.14 = (bf16[64,1024]{1,0:T(8,128)(2,1)S(1)}, bf16[64,1024]{1,0:T(8,128)(2,1)S(1)}, u32[]{:S(2)}, u32[]{:S(2)}) collective-permute-start(bf16[64,1024]{1,0:T(8,128)(2,1)S(1)} %collective-permute-done.8.refs_2_), channel_id=1, source_target_pairs={{0,1},{1,0},{2,3},{3,2},{4,5},{5,4},{6,7},{7,6},{8,9},{9,8},{10,11... | collective-permute-start | bytes 393224 | tf_op jit(solution)/shard_map/ppermute | solution.py:382
  28.5 3.1 %collective-permute-start.16 = (bf16[64,1024]{1,0:T(8,128)(2,1)S(1)}, bf16[64,1024]{1,0:T(8,128)(2,1)S(1)}, u32[]{:S(2)}, u32[]{:S(2)}) collective-permute-start(bf16[64,1024]{1,0:T(8,128)(2,1)S(1)} %collective-permute-done.9.refs_4_), channel_id=1, source_target_pairs={{0,1},{1,0},{2,3},{3,2},{4,5},{5,4},{6,7},{7,6},{8,9},{9,8},{10,11... | collective-permute-start | bytes 393224 | tf_op jit(solution)/shard_map/ppermute | solution.py:382
  30.0 1.6 %collective-permute-start.15 = (bf16[64,1024]{1,0:T(8,128)(2,1)S(1)}, bf16[64,1024]{1,0:T(8,128)(2,1)S(1)}, u32[]{:S(2)}, u32[]{:S(2)}) collective-permute-start(bf16[64,1024]{1,0:T(8,128)(2,1)S(1)} %collective-permute-done.5.refs_3_), channel_id=1, source_target_pairs={{0,1},{1,0},{2,3},{3,2},{4,5},{5,4},{6,7},{7,6},{8,9},{9,8},{10,11... | collective-permute-start | bytes 393224 | tf_op jit(solution)/shard_map/ppermute | solution.py:382
  30.0 5.0 %collective-permute-start.6 = (bf16[64,1024]{1,0:T(8,128)(2,1)S(1)}, bf16[64,1024]{1,0:T(8,128)(2,1)S(1)}, u32[]{:S(2)}, u32[]{:S(2)}) collective-permute-start(bf16[64,1024]{1,0:T(8,128)(2,1)S(1)} %collective-permute-done.5.refs_3_), channel_id=1, source_target_pairs={{0,2},{1,5},{2,0},{3,7},{4,6},{5,1},{6,4},{7,3},{8,10},{9,13},{10,... | collective-permute-start | bytes 393224 | tf_op jit(solution)/shard_map/ppermute | solution.py:382
  31.6 3.9 %collective-permute-start.17 = (bf16[64,1024]{1,0:T(8,128)(2,1)S(1)}, bf16[64,1024]{1,0:T(8,128)(2,1)S(1)}, u32[]{:S(2)}, u32[]{:S(2)}) collective-permute-start(bf16[64,1024]{1,0:T(8,128)(2,1)S(1)} %collective-permute-done.10.refs_5_), channel_id=1, source_target_pairs={{0,1},{1,0},{2,3},{3,2},{4,5},{5,4},{6,7},{7,6},{8,9},{9,8},{10,11... | collective-permute-start | bytes 393224 | tf_op jit(solution)/shard_map/ppermute | solution.py:382
  35.0 1.3 %collective-permute-start.19 = (bf16[64,1024]{1,0:T(8,128)(2,1)S(1)}, bf16[64,1024]{1,0:T(8,128)(2,1)S(1)}, u32[]{:S(2)}, u32[]{:S(2)}) collective-permute-start(bf16[64,1024]{1,0:T(8,128)(2,1)S(1)} %collective-permute-done.6.refs_2_), channel_id=1, source_target_pairs={{0,1},{1,0},{2,3},{3,2},{4,5},{5,4},{6,7},{7,6},{8,9},{9,8},{10,11... | collective-permute-start | bytes 393224 | tf_op jit(solution)/shard_map/ppermute | solution.py:382
  35.0 1.5 %collective-permute-start.18 = (bf16[64,1024]{1,0:T(8,128)(2,1)S(1)}, bf16[64,1024]{1,0:T(8,128)(2,1)S(1)}, u32[]{:S(2)}, u32[]{:S(2)}) collective-permute-start(bf16[64,1024]{1,0:T(8,128)(2,1)S(1)} %collective-permute-done.11.refs_6_), channel_id=1, source_target_pairs={{0,1},{1,0},{2,3},{3,2},{4,5},{5,4},{6,7},{7,6},{8,9},{9,8},{10,11... | collective-permute-start | bytes 393224 | tf_op jit(solution)/shard_map/ppermute | solution.py:382
  49.4 7.2 %collective-permute-start.20 = (bf16[144,256]{1,0:T(8,128)(2,1)S(1)}, bf16[144,256]{1,0:T(8,128)(2,1)S(1)}, u32[]{:S(2)}, u32[]{:S(2)}) collective-permute-start(bf16[144,256]{1,0:T(8,128)(2,1)S(1)} %sums.1.refs_0_), channel_id=1, source_target_pairs={{0,24},{8,16},{16,8},{24,0},{1,25},{9,17},{17,9},{25,1},{2,26},{10... | collective-permute-start | bytes 221192 | tf_op jit(solution)/shard_map/ppermute | solution.py:382
  50.6 8.3 %collective-permute-start.21 = (bf16[144,256]{1,0:T(8,128)(2,1)S(1)}, bf16[144,256]{1,0:T(8,128)(2,1)S(1)}, u32[]{:S(2)}, u32[]{:S(2)}) collective-permute-start(bf16[144,256]{1,0:T(8,128)(2,1)S(1)} %sums.1.refs_0_), channel_id=1, source_target_pairs={{0,16},{8,24},{16,0},{24,8},{1,17},{9,25},{17,1},{25,9},{2,18},{10... | collective-permute-start | bytes 221192 | tf_op jit(solution)/shard_map/ppermute | solution.py:382
  50.6 8.3 %collective-permute-start.22 = (bf16[144,256]{1,0:T(8,128)(2,1)S(1)}, bf16[144,256]{1,0:T(8,128)(2,1)S(1)}, u32[]{:S(2)}, u32[]{:S(2)}) collective-permute-start(bf16[144,256]{1,0:T(8,128)(2,1)S(1)} %sums.1.refs_0_), channel_id=1, source_target_pairs={{0,8},{8,0},{16,24},{24,16},{1,9},{9,1},{17,25},{25,17},{2,10},{10... | collective-permute-start | bytes 221192 | tf_op jit(solution)/shard_map/ppermute | solution.py:382

commit v4 on v2

--- a/solution.py
+++ b/solution.py
@@ -377,18 +377,18 @@
         far = strides[:-1]
         for even, odd in zip(far, far[::-1]):
             held = held + [swap(t, "code", code, even, odd) for t in held]
-        for stride in strides[-1:]:
-            held = held + [swap(t, "code", code, stride) for t in held]
+        near = strides[-1:]
+        crossed = [swap(t, "code", code, stride) for stride in near for t in held[:-1]]
+        last, early = lax.optimization_barrier((held[-1], crossed[: len(held) // 2 + 1]))
+        held = held[:-1] + [last] + early + crossed[len(held) // 2 + 1 :]
+        held += [swap(last, "code", code, stride) for stride in near]
         rotation_t = polar(held, own, 1 if thin else dp)
         scratch = [pltpu.VMEM((own, words), f32)]
         operands = (rotation_t, res_t, *ready)
         sums = small_call(sums_kernel, "sums", (own + subs, words), bf16, *operands, scratch=scratch)
         rotated = small_call(rotated_kernel, "rotated", (rows, own), f32, rotation_t, res_v)
-        totals = {0: sums}
-        for k in sorted(range(1, dp), key=lambda k: (bin(k).count("1"), k)):
-            totals[k] = swap(totals[k & (k - 1)], "dp", dp, k & -k)
-        totals = [totals[k] for k in range(dp)]
-        book = small_call(book_kernel, "book", (own, words), f32, book_v, *totals)
+        others = [swap(sums, "dp", dp, k) for k in range(1, dp)]
+        book = small_call(book_kernel, "book", (own, words), f32, book_v, sums, *others)
         return rotated, jnp.transpose(book.reshape(subs, width, words), (0, 2, 1))
 
     return body

time: 59.6 us -> 60.1 us (level)
  starting transfers between devices: 20 us -> 22.9 us
  waiting for transfers between devices: 16.7 us -> 14.3 us
    ppermute x23, starting transfers between devices: 20 us -> 22.9 us  [swap(): lax.ppermute(value, axis, [(i, i ^ (odd_mask if i % 2 else mask)) for i i...]
    ppermute x23, waiting for transfers between devices: 16.7 us -> 14.3 us  [swap(): lax.ppermute(value, axis, [(i, i ^ (odd_mask if i % 2 else mask)) for i i...]
  transfers between devices with their start and end apart: 23 -> 23, of which waited for: 9 -> 9; matrix products, arithmetic and copies ran while one was open for 0% -> 0% of each run, Pallas kernels for 10% -> 9%
where the time goes in v4:
time: 60.1 us; the launch traced here: 60 us
  starting transfers between devices  22.9 us (38%)
  Pallas kernels  22 us (37%)
  waiting for transfers between devices  14.3 us (24%)
  between operations  0.72 us (1%)
    ppermute x23, starting transfers between devices, swap(): lax.ppermute(value, axis, [(i, i ^ (odd_mask if i % 2 else mask)) for i i...  22.9 us
    ppermute x23, waiting for transfers between devices, swap(): lax.ppermute(value, axis, [(i, i ^ (odd_mask if i % 2 else mask)) for i i...  14.3 us
    pallas_call x1, Pallas kernels, polar(): pl.pallas_call(kernel, out_shape=jax.ShapeDtypeStruct((own, dim), bf16),...  11.4 us
    pallas_call x4, Pallas kernels, small_call(): pl.pallas_call(kernel, out_shape=jax.ShapeDtypeStruct(shape, dtype), in_s...  4.9 us
    pallas_call x1, Pallas kernels, onehot_call(): pl.pallas_call(onehot_kernel, out_shape=(jax.ShapeDtypeStruct((rows, subs...  2.99 us
    pallas_call x1, Pallas kernels, cross_partial(): pl.pallas_call(functools.partial(cross_kernel, dp=dp), out_shape=shapes,...  2.71 us
  transfers between devices with their start and end apart: 23, of which 9 were waited for; matrix products, arithmetic and copies ran while one was open for 0% of the time, Pallas kernels for 9%

profile of v4, /device:TPU:0, one launch (start us, length us, event | category | flops | bytes accessed | tf_op | source)
XLA Modules:
  0.0 60.0 jit_solution(6423253296106820713)
XLA Ops:
  0.6 2.7 %cross_partial.1 = (f32[32,1024]{1,0:T(8,128)S(1)}, bf16[32,1024]{1,0:T(8,128)(2,1)S(1)}, bf16[32,1024]{1,0:T(8,128)(2,1)S(1)}, bf16[32,1024]{1,0:T(8,128)(2,1)S...) custom-call(s32[16,2048]{1,0:T(8,128)} %bitcast.7, f32[128,256]{1,0:T(8,128)} %bitcast.8, ...), custom_call_target="tpu_custom_call" | custom-call | tf_op jit(solution)/shard_map/cross_partial/pallas_call | solution.py:86
  3.3 5.1 %collective-permute-start = (bf16[32,1024]{1,0:T(8,128)(2,1)S(1)}, bf16[32,1024]{1,0:T(8,128)(2,1)S(1)}, u32[]{:S(2)}, u32[]{:S(2)}) collective-permute-start(bf16[32,1024]{1,0:T(8,128)(2,1)S(1)} %get-tuple-element.27), channel_id=1, source_target_pairs={{0,24},{8,16},{16,8},{24,0},{1,25},{9,17},{17,9},{25,1},{2,26},{10... | collective-permute-start | bytes 196616 | tf_op jit(solution)/shard_map/ppermute | solution.py:336
  8.5 0.0 collective-permute-start.1
  8.5 0.6 %collective-permute-start.2 = (bf16[32,1024]{1,0:T(8,128)(2,1)S(1)}, bf16[32,1024]{1,0:T(8,128)(2,1)S(1)}, u32[]{:S(2)}, u32[]{:S(2)}) collective-permute-start(bf16[32,1024]{1,0:T(8,128)(2,1)S(1)} %get-tuple-element.29), channel_id=1, source_target_pairs={{0,8},{8,0},{16,24},{24,16},{1,9},{9,1},{17,25},{25,17},{2,10},{10... | collective-permute-start | bytes 196616 | tf_op jit(solution)/shard_map/ppermute | solution.py:336
  9.1 3.0 %onehot.1 = (bf16[2048,1024]{1,0:T(8,128)(2,1)S(1)}, bf16[512,2048]{1,0:T(8,128)(2,1)S(1)}, f32[16,256]{1,0:T(8,128)S(1)}, bf16[1024,2048]{1,0:T(8,128)(2,1)S(1)}) custom-call(s32[16,2048]{1,0:T(8,128)S(1)} %get-tuple-element.30.codes_ref, bf16[2048,1024]{1,0:T(8,128)(2,1)S(1)} %get-tuple-element.31.res_ref), custom_call_target="tpu_custom_call" | custom-call | flops 1073741824 | bytes 4194304 | tf_op jit(solution)/shard_map/onehot/pallas_call | solution.py:223
  12.1 0.0 collective-permute-done.refs_1_
  12.1 2.0 %collective-permute-done.1.refs_2_ = bf16[32,1024]{1,0:T(8,128)(2,1)S(1)} collective-permute-done((bf16[32,1024]{1,0:T(8,128)(2,1)S(1)}, bf16[32,1024]{1,0:T(8,128)(2,1)S(1)}, u32[]{:S(2)}, u32[]{:S(2)}) %collective-permute-start.1) | collective-permute-done | bytes 65568 | tf_op jit(solution)/shard_map/ppermute | solution.py:336
  14.1 0.0 collective-permute-done.2.refs_3_
  14.1 1.1 %collective-permute-start.3 = (bf16[32,1024]{1,0:T(8,128)(2,1)S(1)}, bf16[32,1024]{1,0:T(8,128)(2,1)S(1)}, u32[]{:S(2)}, u32[]{:S(2)}) collective-permute-start(bf16[32,1024]{1,0:T(8,128)(2,1)S(1)} %share.1), channel_id=1, source_target_pairs={{0,8},{8,0},{16,24},{24,16},{1,9},{9,1},{17,25},{25,17},{2,10},{10... | collective-permute-start | bytes 196616 | tf_op jit(solution)/shard_map/ppermute | solution.py:336
  15.3 2.0 %collective-permute-start.5 = (bf16[32,1024]{1,0:T(8,128)(2,1)S(1)}, bf16[32,1024]{1,0:T(8,128)(2,1)S(1)}, u32[]{:S(2)}, u32[]{:S(2)}) collective-permute-start(bf16[32,1024]{1,0:T(8,128)(2,1)S(1)} %share.1), channel_id=1, source_target_pairs={{0,24},{8,16},{16,8},{24,0},{1,25},{9,17},{17,9},{25,1},{2,26},{10... | collective-permute-start | bytes 196616 | tf_op jit(solution)/shard_map/ppermute | solution.py:336
  17.2 0.4 collective-permute-start.4
  17.7 1.8 %collective-permute-done.3 = bf16[32,1024]{1,0:T(8,128)(2,1)S(1)} collective-permute-done((bf16[32,1024]{1,0:T(8,128)(2,1)S(1)}, bf16[32,1024]{1,0:T(8,128)(2,1)S(1)}, u32[]{:S(2)}, u32[]{:S(2)}) %collective-permute-start.3) | collective-permute-done | bytes 65568 | tf_op jit(solution)/shard_map/ppermute | solution.py:336
  19.5 0.1 collective-permute-start.12
  19.6 0.5 collective-permute-start.8
  20.1 1.5 %collective-permute-start.6 = (bf16[64,1024]{1,0:T(8,128)(2,1)S(1)}, bf16[64,1024]{1,0:T(8,128)(2,1)S(1)}, u32[]{:S(2)}, u32[]{:S(2)}) collective-permute-start(bf16[64,1024]{1,0:T(8,128)(2,1)S(1)} %pad_maximum_fusion.refs_0_), channel_id=1, source_target_pairs={{0,4},{1,3},{2,6},{3,1},{4,0},{5,7},{6,2},{7,5},{8,12},{9,11},{10,... | collective-permute-start | bytes 393224 | tf_op jit(solution)/shard_map/ppermute | solution.py:336
  21.6 1.6 %collective-permute-done.4 = bf16[32,1024]{1,0:T(8,128)(2,1)S(1)} collective-permute-done((bf16[32,1024]{1,0:T(8,128)(2,1)S(1)}, bf16[32,1024]{1,0:T(8,128)(2,1)S(1)}, u32[]{:S(2)}, u32[]{:S(2)}) %collective-permute-start.4) | collective-permute-done | bytes 65568 | tf_op jit(solution)/shard_map/ppermute | solution.py:336
  23.2 0.0 collective-permute-done.5
  23.3 1.8 %collective-permute-start.7 = (bf16[64,1024]{1,0:T(8,128)(2,1)S(1)}, bf16[64,1024]{1,0:T(8,128)(2,1)S(1)}, u32[]{:S(2)}, u32[]{:S(2)}) collective-permute-start(bf16[64,1024]{1,0:T(8,128)(2,1)S(1)} %constant_dynamic-update-slice_fusion.refs_1_), channel_id=1, source_target_pairs={{0,4},{1,3},{2,6},{3,1},{4,0},{5,7},{6,2},{7,5},{8,12},{9,11},{10,... | collective-permute-start | bytes 393224 | tf_op jit(solution)/shard_map/ppermute | solution.py:336
  25.0 0.0 collective-permute-start.13
  25.0 0.0 collective-permute-done.12.refs_8_
  25.0 1.5 %collective-permute-start.9 = (bf16[64,1024]{1,0:T(8,128)(2,1)S(1)}, bf16[64,1024]{1,0:T(8,128)(2,1)S(1)}, u32[]{:S(2)}, u32[]{:S(2)}) collective-permute-start(bf16[64,1024]{1,0:T(8,128)(2,1)S(1)} %constant_dynamic-update-slice_fusion.refs_1_), channel_id=1, source_target_pairs={{0,2},{1,5},{2,0},{3,7},{4,6},{5,1},{6,4},{7,3},{8,10},{9,13},{10,... | collective-permute-start | bytes 393224 | tf_op jit(solution)/shard_map/ppermute | solution.py:336
  26.5 0.0 collective-permute-done.8.refs_4_
  26.5 0.0 collective-permute-start.16
  26.5 0.0 collective-permute-done.6.refs_2_
  26.5 0.5 collective-permute-start.14
  27.0 1.7 %collective-permute-done.7.refs_3_ = bf16[64,1024]{1,0:T(8,128)(2,1)S(1)} collective-permute-done((bf16[64,1024]{1,0:T(8,128)(2,1)S(1)}, bf16[64,1024]{1,0:T(8,128)(2,1)S(1)}, u32[]{:S(2)}, u32[]{:S(2)}) %collective-permute-start.7) | collective-permute-done | bytes 131104 | tf_op jit(solution)/shard_map/ppermute | solution.py:336
  28.8 0.0 collective-permute-start.15
  28.8 0.0 collective-permute-done.13.refs_9_
  28.8 1.6 %collective-permute-start.11 = (bf16[64,1024]{1,0:T(8,128)(2,1)S(1)}, bf16[64,1024]{1,0:T(8,128)(2,1)S(1)}, u32[]{:S(2)}, u32[]{:S(2)}) collective-permute-start(bf16[64,1024]{1,0:T(8,128)(2,1)S(1)} %collective-permute-done.7.refs_3_), channel_id=1, source_target_pairs={{0,2},{1,5},{2,0},{3,7},{4,6},{5,1},{6,4},{7,3},{8,10},{9,13},{10,... | collective-permute-start | bytes 393224 | tf_op jit(solution)/shard_map/ppermute | solution.py:336
  30.4 0.0 collective-permute-done.9.refs_5_
  30.4 1.1 %collective-permute-start.10 = (bf16[64,1024]{1,0:T(8,128)(2,1)S(1)}, bf16[64,1024]{1,0:T(8,128)(2,1)S(1)}, u32[]{:S(2)}, u32[]{:S(2)}) collective-permute-start(bf16[64,1024]{1,0:T(8,128)(2,1)S(1)} %collective-permute-done.6.refs_2_), channel_id=1, source_target_pairs={{0,2},{1,5},{2,0},{3,7},{4,6},{5,1},{6,4},{7,3},{8,10},{9,13},{10,... | collective-permute-start | bytes 393224 | tf_op jit(solution)/shard_map/ppermute | solution.py:336
  31.5 0.0 collective-permute-done.16.refs_12_
  31.5 0.1 collective-permute-start.17
  31.6 0.0 collective-permute-done.14.refs_10_
  31.6 0.0 collective-permute-done.15.refs_11_
  31.6 2.2 %collective-permute-done.11.refs_7_ = bf16[64,1024]{1,0:T(8,128)(2,1)S(1)} collective-permute-done((bf16[64,1024]{1,0:T(8,128)(2,1)S(1)}, bf16[64,1024]{1,0:T(8,128)(2,1)S(1)}, u32[]{:S(2)}, u32[]{:S(2)}) %collective-permute-start.11) | collective-permute-done | bytes 131104 | tf_op jit(solution)/shard_map/ppermute | solution.py:336
  33.8 1.6 %collective-permute-done.10.refs_6_ = bf16[64,1024]{1,0:T(8,128)(2,1)S(1)} collective-permute-done((bf16[64,1024]{1,0:T(8,128)(2,1)S(1)}, bf16[64,1024]{1,0:T(8,128)(2,1)S(1)}, u32[]{:S(2)}, u32[]{:S(2)}) %collective-permute-start.10) | collective-permute-done | bytes 131104 | tf_op jit(solution)/shard_map/ppermute | solution.py:336
  35.3 0.1 collective-permute-start.18
  35.5 0.4 collective-permute-start.19
  35.8 0.0 collective-permute-done.17.refs_13_
  35.9 0.8 %collective-permute-done.18.refs_14_ = bf16[64,1024]{1,0:T(8,128)(2,1)S(1)} collective-permute-done((bf16[64,1024]{1,0:T(8,128)(2,1)S(1)}, bf16[64,1024]{1,0:T(8,128)(2,1)S(1)}, u32[]{:S(2)}, u32[]{:S(2)}) %collective-permute-start.18) | collective-permute-done | bytes 131104 | tf_op jit(solution)/shard_map/ppermute | solution.py:336
  36.7 0.2 collective-permute-done.19.refs_15_
  36.9 11.4 %polar.1.rot_ref = bf16[128,1024]{1,0:T(8,128)(2,1)S(1)} custom-call(bf16[64,1024]{1,0:T(8,128)(2,1)S(1)} %pad_maximum_fusion.refs_0_, bf16[64,1024]{1,0:T(8,128)(2,1)S(1)} %constant_dynamic-update-slice_fusion.refs_1_, bf16[64,1024]{1,0:T(8,128)(2,1)S(1)} %collective-permute-done.6.refs_2_, bf16[64,1024]{1,0:T(8,128)(2,1)S(1)} %collective-permute-done.7.refs_3_, ...), custom_call_target="tpu_custom_call" | custom-call | tf_op jit(solution)/shard_map/polar/pallas_call | solution.py:280
  48.3 1.4 %sums.1.refs_0_ = bf16[144,256]{1,0:T(8,128)(2,1)S(1)} custom-call(bf16[128,1024]{1,0:T(8,128)(2,1)S(1)} %polar.1.rot_ref, bf16[1024,2048]{1,0:T(8,128)(2,1)S(1)} %get-tuple-element.46.res_ref, bf16[2048,1024]{1,0:T(8,128)(2,1)S(1)} %get-tuple-element.47.onehot_ref, bf16[512,2048]{1,0:T(8,128)(2,1)S(1)} %get-tuple-element.48.masks_ref, ...), custom_call_target="tpu_custom_call" | custom-call | tf_op jit(solution)/shard_map/sums/pallas_call | solution.py:323
  49.7 2.0 %collective-permute-start.22 = (bf16[144,256]{1,0:T(8,128)(2,1)S(1)}, bf16[144,256]{1,0:T(8,128)(2,1)S(1)}, u32[]{:S(2)}, u32[]{:S(2)}) collective-permute-start(bf16[144,256]{1,0:T(8,128)(2,1)S(1)} %sums.1.refs_0_), channel_id=1, source_target_pairs={{0,24},{8,16},{16,8},{24,0},{1,25},{9,17},{17,9},{25,1},{2,26},{10... | collective-permute-start | bytes 221192 | tf_op jit(solution)/shard_map/ppermute | solution.py:336
  51.7 0.0 collective-permute-start.21
  51.7 2.4 %collective-permute-start.20 = (bf16[144,256]{1,0:T(8,128)(2,1)S(1)}, bf16[144,256]{1,0:T(8,128)(2,1)S(1)}, u32[]{:S(2)}, u32[]{:S(2)}) collective-permute-start(bf16[144,256]{1,0:T(8,128)(2,1)S(1)} %sums.1.refs_0_), channel_id=1, source_target_pairs={{0,8},{8,0},{16,24},{24,16},{1,9},{9,1},{17,25},{25,17},{2,10},{10... | collective-permute-start | bytes 221192 | tf_op jit(solution)/shard_map/ppermute | solution.py:336
  54.2 2.7 %rotated.1 = f32[2048,128]{1,0:T(8,128)} custom-call(bf16[128,1024]{1,0:T(8,128)(2,1)S(1)} %polar.1.rot_ref, bf16[2048,1024]{1,0:T(8,128)(2,1)S(1)} %get-tuple-element.31.res_ref), custom_call_target="tpu_custom_call" | custom-call | tf_op jit(solution)/shard_map/rotated/pallas_call | solution.py:323
  56.9 0.0 collective-permute-done.22.refs_3_
  56.9 2.3 %collective-permute-done.21.refs_2_ = bf16[144,256]{1,0:T(8,128)(2,1)S(1)} collective-permute-done((bf16[144,256]{1,0:T(8,128)(2,1)S(1)}, bf16[144,256]{1,0:T(8,128)(2,1)S(1)}, u32[]{:S(2)}, u32[]{:S(2)}) %collective-permute-start.21) | collective-permute-done | bytes 73760 | tf_op jit(solution)/shard_map/ppermute | solution.py:336
  59.2 0.0 collective-permute-done.20.refs_1_
  59.2 0.7 %book.1 = f32[128,256]{1,0:T(8,128)} custom-call(f32[128,256]{1,0:T(8,128)S(1)} %get-tuple-element.45.book_ref, bf16[144,256]{1,0:T(8,128)(2,1)S(1)} %sums.1.refs_0_, bf16[144,256]{1,0:T(8,128)(2,1)S(1)} %collective-permute-done.20.refs_1_, bf16[144,256]{1,0:T(8,128)(2,1)S(1)} %collective-permute-done.21.refs_2_, ...), custom_call_target="tpu_custom_call" | custom-call | tf_op jit(solution)/shard_map/book/pallas_call | solution.py:323
  (4 shorter events, 0.1 us)
Async XLA Ops:
  3.3 8.8 %collective-permute-start = (bf16[32,1024]{1,0:T(8,128)(2,1)S(1)}, bf16[32,1024]{1,0:T(8,128)(2,1)S(1)}, u32[]{:S(2)}, u32[]{:S(2)}) collective-permute-start(bf16[32,1024]{1,0:T(8,128)(2,1)S(1)} %get-tuple-element.27), channel_id=1, source_target_pairs={{0,24},{8,16},{16,8},{24,0},{1,25},{9,17},{17,9},{25,1},{2,26},{10... | collective-permute-start | bytes 196616 | tf_op jit(solution)/shard_map/ppermute | solution.py:336
  8.5 5.6 %collective-permute-start.1 = (bf16[32,1024]{1,0:T(8,128)(2,1)S(1)}, bf16[32,1024]{1,0:T(8,128)(2,1)S(1)}, u32[]{:S(2)}, u32[]{:S(2)}) collective-permute-start(bf16[32,1024]{1,0:T(8,128)(2,1)S(1)} %get-tuple-element.28), channel_id=1, source_target_pairs={{0,16},{8,24},{16,0},{24,8},{1,17},{9,25},{17,1},{25,9},{2,18},{10... | collective-permute-start | bytes 196616 | tf_op jit(solution)/shard_map/ppermute | solution.py:336
  8.5 5.6 %collective-permute-start.2 = (bf16[32,1024]{1,0:T(8,128)(2,1)S(1)}, bf16[32,1024]{1,0:T(8,128)(2,1)S(1)}, u32[]{:S(2)}, u32[]{:S(2)}) collective-permute-start(bf16[32,1024]{1,0:T(8,128)(2,1)S(1)} %get-tuple-element.29), channel_id=1, source_target_pairs={{0,8},{8,0},{16,24},{24,16},{1,9},{9,1},{17,25},{25,17},{2,10},{10... | collective-permute-start | bytes 196616 | tf_op jit(solution)/shard_map/ppermute | solution.py:336
  14.1 5.4 %collective-permute-start.3 = (bf16[32,1024]{1,0:T(8,128)(2,1)S(1)}, bf16[32,1024]{1,0:T(8,128)(2,1)S(1)}, u32[]{:S(2)}, u32[]{:S(2)}) collective-permute-start(bf16[32,1024]{1,0:T(8,128)(2,1)S(1)} %share.1), channel_id=1, source_target_pairs={{0,8},{8,0},{16,24},{24,16},{1,9},{9,1},{17,25},{25,17},{2,10},{10... | collective-permute-start | bytes 196616 | tf_op jit(solution)/shard_map/ppermute | solution.py:336
  15.3 8.0 %collective-permute-start.5 = (bf16[32,1024]{1,0:T(8,128)(2,1)S(1)}, bf16[32,1024]{1,0:T(8,128)(2,1)S(1)}, u32[]{:S(2)}, u32[]{:S(2)}) collective-permute-start(bf16[32,1024]{1,0:T(8,128)(2,1)S(1)} %share.1), channel_id=1, source_target_pairs={{0,24},{8,16},{16,8},{24,0},{1,25},{9,17},{17,9},{25,1},{2,26},{10... | collective-permute-start | bytes 196616 | tf_op jit(solution)/shard_map/ppermute | solution.py:336
  17.2 6.0 %collective-permute-start.4 = (bf16[32,1024]{1,0:T(8,128)(2,1)S(1)}, bf16[32,1024]{1,0:T(8,128)(2,1)S(1)}, u32[]{:S(2)}, u32[]{:S(2)}) collective-permute-start(bf16[32,1024]{1,0:T(8,128)(2,1)S(1)} %share.1), channel_id=1, source_target_pairs={{0,16},{8,24},{16,0},{24,8},{1,17},{9,25},{17,1},{25,9},{2,18},{10... | collective-permute-start | bytes 196616 | tf_op jit(solution)/shard_map/ppermute | solution.py:336
  19.5 5.6 %collective-permute-start.12 = (bf16[64,1024]{1,0:T(8,128)(2,1)S(1)}, bf16[64,1024]{1,0:T(8,128)(2,1)S(1)}, u32[]{:S(2)}, u32[]{:S(2)}) collective-permute-start(bf16[64,1024]{1,0:T(8,128)(2,1)S(1)} %pad_maximum_fusion.refs_0_), channel_id=1, source_target_pairs={{0,1},{1,0},{2,3},{3,2},{4,5},{5,4},{6,7},{7,6},{8,9},{9,8},{10,11... | collective-permute-start | bytes 393224 | tf_op jit(solution)/shard_map/ppermute | solution.py:336
  19.6 7.0 %collective-permute-start.8 = (bf16[64,1024]{1,0:T(8,128)(2,1)S(1)}, bf16[64,1024]{1,0:T(8,128)(2,1)S(1)}, u32[]{:S(2)}, u32[]{:S(2)}) collective-permute-start(bf16[64,1024]{1,0:T(8,128)(2,1)S(1)} %pad_maximum_fusion.refs_0_), channel_id=1, source_target_pairs={{0,2},{1,5},{2,0},{3,7},{4,6},{5,1},{6,4},{7,3},{8,10},{9,13},{10,... | collective-permute-start | bytes 393224 | tf_op jit(solution)/shard_map/ppermute | solution.py:336
  20.1 6.4 %collective-permute-start.6 = (bf16[64,1024]{1,0:T(8,128)(2,1)S(1)}, bf16[64,1024]{1,0:T(8,128)(2,1)S(1)}, u32[]{:S(2)}, u32[]{:S(2)}) collective-permute-start(bf16[64,1024]{1,0:T(8,128)(2,1)S(1)} %pad_maximum_fusion.refs_0_), channel_id=1, source_target_pairs={{0,4},{1,3},{2,6},{3,1},{4,0},{5,7},{6,2},{7,5},{8,12},{9,11},{10,... | collective-permute-start | bytes 393224 | tf_op jit(solution)/shard_map/ppermute | solution.py:336
  23.3 5.5 %collective-permute-start.7 = (bf16[64,1024]{1,0:T(8,128)(2,1)S(1)}, bf16[64,1024]{1,0:T(8,128)(2,1)S(1)}, u32[]{:S(2)}, u32[]{:S(2)}) collective-permute-start(bf16[64,1024]{1,0:T(8,128)(2,1)S(1)} %constant_dynamic-update-slice_fusion.refs_1_), channel_id=1, source_target_pairs={{0,4},{1,3},{2,6},{3,1},{4,0},{5,7},{6,2},{7,5},{8,12},{9,11},{10,... | collective-permute-start | bytes 393224 | tf_op jit(solution)/shard_map/ppermute | solution.py:336
  25.0 3.8 %collective-permute-start.13 = (bf16[64,1024]{1,0:T(8,128)(2,1)S(1)}, bf16[64,1024]{1,0:T(8,128)(2,1)S(1)}, u32[]{:S(2)}, u32[]{:S(2)}) collective-permute-start(bf16[64,1024]{1,0:T(8,128)(2,1)S(1)} %constant_dynamic-update-slice_fusion.refs_1_), channel_id=1, source_target_pairs={{0,1},{1,0},{2,3},{3,2},{4,5},{5,4},{6,7},{7,6},{8,9},{9,8},{10,11... | collective-permute-start | bytes 393224 | tf_op jit(solution)/shard_map/ppermute | solution.py:336
  25.0 5.3 %collective-permute-start.9 = (bf16[64,1024]{1,0:T(8,128)(2,1)S(1)}, bf16[64,1024]{1,0:T(8,128)(2,1)S(1)}, u32[]{:S(2)}, u32[]{:S(2)}) collective-permute-start(bf16[64,1024]{1,0:T(8,128)(2,1)S(1)} %constant_dynamic-update-slice_fusion.refs_1_), channel_id=1, source_target_pairs={{0,2},{1,5},{2,0},{3,7},{4,6},{5,1},{6,4},{7,3},{8,10},{9,13},{10,... | collective-permute-start | bytes 393224 | tf_op jit(solution)/shard_map/ppermute | solution.py:336
  26.5 5.0 %collective-permute-start.16 = (bf16[64,1024]{1,0:T(8,128)(2,1)S(1)}, bf16[64,1024]{1,0:T(8,128)(2,1)S(1)}, u32[]{:S(2)}, u32[]{:S(2)}) collective-permute-start(bf16[64,1024]{1,0:T(8,128)(2,1)S(1)} %collective-permute-done.8.refs_4_), channel_id=1, source_target_pairs={{0,1},{1,0},{2,3},{3,2},{4,5},{5,4},{6,7},{7,6},{8,9},{9,8},{10,11... | collective-permute-start | bytes 393224 | tf_op jit(solution)/shard_map/ppermute | solution.py:336
  26.5 5.1 %collective-permute-start.14 = (bf16[64,1024]{1,0:T(8,128)(2,1)S(1)}, bf16[64,1024]{1,0:T(8,128)(2,1)S(1)}, u32[]{:S(2)}, u32[]{:S(2)}) collective-permute-start(bf16[64,1024]{1,0:T(8,128)(2,1)S(1)} %collective-permute-done.6.refs_2_), channel_id=1, source_target_pairs={{0,1},{1,0},{2,3},{3,2},{4,5},{5,4},{6,7},{7,6},{8,9},{9,8},{10,11... | collective-permute-start | bytes 393224 | tf_op jit(solution)/shard_map/ppermute | solution.py:336
  28.8 2.8 %collective-permute-start.15 = (bf16[64,1024]{1,0:T(8,128)(2,1)S(1)}, bf16[64,1024]{1,0:T(8,128)(2,1)S(1)}, u32[]{:S(2)}, u32[]{:S(2)}) collective-permute-start(bf16[64,1024]{1,0:T(8,128)(2,1)S(1)} %collective-permute-done.7.refs_3_), channel_id=1, source_target_pairs={{0,1},{1,0},{2,3},{3,2},{4,5},{5,4},{6,7},{7,6},{8,9},{9,8},{10,11... | collective-permute-start | bytes 393224 | tf_op jit(solution)/shard_map/ppermute | solution.py:336
  28.8 5.0 %collective-permute-start.11 = (bf16[64,1024]{1,0:T(8,128)(2,1)S(1)}, bf16[64,1024]{1,0:T(8,128)(2,1)S(1)}, u32[]{:S(2)}, u32[]{:S(2)}) collective-permute-start(bf16[64,1024]{1,0:T(8,128)(2,1)S(1)} %collective-permute-done.7.refs_3_), channel_id=1, source_target_pairs={{0,2},{1,5},{2,0},{3,7},{4,6},{5,1},{6,4},{7,3},{8,10},{9,13},{10,... | collective-permute-start | bytes 393224 | tf_op jit(solution)/shard_map/ppermute | solution.py:336
  30.4 5.0 %collective-permute-start.10 = (bf16[64,1024]{1,0:T(8,128)(2,1)S(1)}, bf16[64,1024]{1,0:T(8,128)(2,1)S(1)}, u32[]{:S(2)}, u32[]{:S(2)}) collective-permute-start(bf16[64,1024]{1,0:T(8,128)(2,1)S(1)} %collective-permute-done.6.refs_2_), channel_id=1, source_target_pairs={{0,2},{1,5},{2,0},{3,7},{4,6},{5,1},{6,4},{7,3},{8,10},{9,13},{10,... | collective-permute-start | bytes 393224 | tf_op jit(solution)/shard_map/ppermute | solution.py:336
  31.5 4.4 %collective-permute-start.17 = (bf16[64,1024]{1,0:T(8,128)(2,1)S(1)}, bf16[64,1024]{1,0:T(8,128)(2,1)S(1)}, u32[]{:S(2)}, u32[]{:S(2)}) collective-permute-start(bf16[64,1024]{1,0:T(8,128)(2,1)S(1)} %collective-permute-done.9.refs_5_), channel_id=1, source_target_pairs={{0,1},{1,0},{2,3},{3,2},{4,5},{5,4},{6,7},{7,6},{8,9},{9,8},{10,11... | collective-permute-start | bytes 393224 | tf_op jit(solution)/shard_map/ppermute | solution.py:336
  35.3 1.3 %collective-permute-start.18 = (bf16[64,1024]{1,0:T(8,128)(2,1)S(1)}, bf16[64,1024]{1,0:T(8,128)(2,1)S(1)}, u32[]{:S(2)}, u32[]{:S(2)}) collective-permute-start(bf16[64,1024]{1,0:T(8,128)(2,1)S(1)} %collective-permute-done.10.refs_6_), channel_id=1, source_target_pairs={{0,1},{1,0},{2,3},{3,2},{4,5},{5,4},{6,7},{7,6},{8,9},{9,8},{10,11... | collective-permute-start | bytes 393224 | tf_op jit(solution)/shard_map/ppermute | solution.py:336
  35.5 1.4 %collective-permute-start.19 = (bf16[64,1024]{1,0:T(8,128)(2,1)S(1)}, bf16[64,1024]{1,0:T(8,128)(2,1)S(1)}, u32[]{:S(2)}, u32[]{:S(2)}) collective-permute-start(bf16[64,1024]{1,0:T(8,128)(2,1)S(1)} %collective-permute-done.11.refs_7_), channel_id=1, source_target_pairs={{0,1},{1,0},{2,3},{3,2},{4,5},{5,4},{6,7},{7,6},{8,9},{9,8},{10,11... | collective-permute-start | bytes 393224 | tf_op jit(solution)/shard_map/ppermute | solution.py:336
  49.7 7.2 %collective-permute-start.22 = (bf16[144,256]{1,0:T(8,128)(2,1)S(1)}, bf16[144,256]{1,0:T(8,128)(2,1)S(1)}, u32[]{:S(2)}, u32[]{:S(2)}) collective-permute-start(bf16[144,256]{1,0:T(8,128)(2,1)S(1)} %sums.1.refs_0_), channel_id=1, source_target_pairs={{0,24},{8,16},{16,8},{24,0},{1,25},{9,17},{17,9},{25,1},{2,26},{10... | collective-permute-start | bytes 221192 | tf_op jit(solution)/shard_map/ppermute | solution.py:336
  51.7 7.5 %collective-permute-start.21 = (bf16[144,256]{1,0:T(8,128)(2,1)S(1)}, bf16[144,256]{1,0:T(8,128)(2,1)S(1)}, u32[]{:S(2)}, u32[]{:S(2)}) collective-permute-start(bf16[144,256]{1,0:T(8,128)(2,1)S(1)} %sums.1.refs_0_), channel_id=1, source_target_pairs={{0,16},{8,24},{16,0},{24,8},{1,17},{9,25},{17,1},{25,9},{2,18},{10... | collective-permute-start | bytes 221192 | tf_op jit(solution)/shard_map/ppermute | solution.py:336
  51.7 7.5 %collective-permute-start.20 = (bf16[144,256]{1,0:T(8,128)(2,1)S(1)}, bf16[144,256]{1,0:T(8,128)(2,1)S(1)}, u32[]{:S(2)}, u32[]{:S(2)}) collective-permute-start(bf16[144,256]{1,0:T(8,128)(2,1)S(1)} %sums.1.refs_0_), channel_id=1, source_target_pairs={{0,8},{8,0},{16,24},{24,16},{1,9},{9,1},{17,25},{25,17},{2,10},{10... | collective-permute-start | bytes 221192 | tf_op jit(solution)/shard_map/ppermute | solution.py:336

commit v5 on v4

--- a/solution.py
+++ b/solution.py
@@ -14,7 +14,7 @@
 epsilon = 1e-06
 f32, bf16 = jnp.float32, jnp.bfloat16
 MIB = 1024 * 1024
-ROW_CHUNKS = 4
+ROW_CHUNKS = 8
 NT = (((1,), (1,)), ((), ()))
 
 
@@ -377,11 +377,8 @@
         far = strides[:-1]
         for even, odd in zip(far, far[::-1]):
             held = held + [swap(t, "code", code, even, odd) for t in held]
-        near = strides[-1:]
-        crossed = [swap(t, "code", code, stride) for stride in near for t in held[:-1]]
-        last, early = lax.optimization_barrier((held[-1], crossed[: len(held) // 2 + 1]))
-        held = held[:-1] + [last] + early + crossed[len(held) // 2 + 1 :]
-        held += [swap(last, "code", code, stride) for stride in near]
+        for stride in strides[-1:]:
+            held = held + [swap(t, "code", code, stride) for t in held]
         rotation_t = polar(held, own, 1 if thin else dp)
         scratch = [pltpu.VMEM((own, words), f32)]
         operands = (rotation_t, res_t, *ready)

time: 60.1 us -> 58.4 us (0.972)
  starting transfers between devices: 22.9 us -> 21.9 us
  waiting for transfers between devices: 14.3 us -> 13.5 us
    ppermute x23, starting transfers between devices: 22.9 us -> 21.9 us  [swap(): lax.ppermute(value, axis, [(i, i ^ (odd_mask if i % 2 else mask)) for i i...]
    ppermute x23, waiting for transfers between devices: 14.3 us -> 13.5 us  [swap(): lax.ppermute(value, axis, [(i, i ^ (odd_mask if i % 2 else mask)) for i i...]
  transfers between devices with their start and end apart: 23 -> 23, of which waited for: 9 -> 8; matrix products, arithmetic and copies ran while one was open for 0% -> 0% of each run, Pallas kernels for 9% -> 10%
where the time goes in v5:
time: 58.4 us; the launch traced here: 58.3 us
  Pallas kernels  22.1 us (38%)
  starting transfers between devices  21.9 us (38%)
  waiting for transfers between devices  13.5 us (23%)
  between operations  0.74 us (1%)
    ppermute x23, starting transfers between devices, swap(): lax.ppermute(value, axis, [(i, i ^ (odd_mask if i % 2 else mask)) for i i...  21.9 us
    ppermute x23, waiting for transfers between devices, swap(): lax.ppermute(value, axis, [(i, i ^ (odd_mask if i % 2 else mask)) for i i...  13.5 us
    pallas_call x1, Pallas kernels, polar(): pl.pallas_call(kernel, out_shape=jax.ShapeDtypeStruct((own, dim), bf16),...  11.4 us
    pallas_call x4, Pallas kernels, small_call(): pl.pallas_call(kernel, out_shape=jax.ShapeDtypeStruct(shape, dtype), in_s...  4.89 us
    pallas_call x1, Pallas kernels, onehot_call(): pl.pallas_call(onehot_kernel, out_shape=(jax.ShapeDtypeStruct((rows, subs...  2.99 us
    pallas_call x1, Pallas kernels, cross_partial(): pl.pallas_call(functools.partial(cross_kernel, dp=dp), out_shape=shapes,...  2.8 us
  transfers between devices with their start and end apart: 23, of which 8 were waited for; matrix products, arithmetic and copies ran while one was open for 0% of the time, Pallas kernels for 10%

profile of v5, /device:TPU:0, one launch (start us, length us, event | category | flops | bytes accessed | tf_op | source)
XLA Modules:
  0.0 58.3 jit_solution(9731718869525012390)
XLA Ops:
  0.6 2.8 %cross_partial.1 = (f32[32,1024]{1,0:T(8,128)S(1)}, bf16[32,1024]{1,0:T(8,128)(2,1)S(1)}, bf16[32,1024]{1,0:T(8,128)(2,1)S(1)}, bf16[32,1024]{1,0:T(8,128)(2,1)S...) custom-call(s32[16,2048]{1,0:T(8,128)} %bitcast.7, f32[128,256]{1,0:T(8,128)} %bitcast.8, ...), custom_call_target="tpu_custom_call" | custom-call | tf_op jit(solution)/shard_map/cross_partial/pallas_call | solution.py:86
  3.4 5.1 %collective-permute-start = (bf16[32,1024]{1,0:T(8,128)(2,1)S(1)}, bf16[32,1024]{1,0:T(8,128)(2,1)S(1)}, u32[]{:S(2)}, u32[]{:S(2)}) collective-permute-start(bf16[32,1024]{1,0:T(8,128)(2,1)S(1)} %get-tuple-element.21), channel_id=1, source_target_pairs={{0,24},{8,16},{16,8},{24,0},{1,25},{9,17},{17,9},{25,1},{2,26},{10... | collective-permute-start | bytes 196616 | tf_op jit(solution)/shard_map/ppermute | solution.py:336
  8.6 0.0 collective-permute-start.1
  8.6 0.6 %collective-permute-start.2 = (bf16[32,1024]{1,0:T(8,128)(2,1)S(1)}, bf16[32,1024]{1,0:T(8,128)(2,1)S(1)}, u32[]{:S(2)}, u32[]{:S(2)}) collective-permute-start(bf16[32,1024]{1,0:T(8,128)(2,1)S(1)} %get-tuple-element.23), channel_id=1, source_target_pairs={{0,8},{8,0},{16,24},{24,16},{1,9},{9,1},{17,25},{25,17},{2,10},{10... | collective-permute-start | bytes 196616 | tf_op jit(solution)/shard_map/ppermute | solution.py:336
  9.2 3.0 %onehot.1 = (bf16[2048,1024]{1,0:T(8,128)(2,1)S(1)}, bf16[512,2048]{1,0:T(8,128)(2,1)S(1)}, f32[16,256]{1,0:T(8,128)S(1)}, bf16[1024,2048]{1,0:T(8,128)(2,1)S(1)}) custom-call(s32[16,2048]{1,0:T(8,128)S(1)} %get-tuple-element.24.codes_ref, bf16[2048,1024]{1,0:T(8,128)(2,1)S(1)} %get-tuple-element.25.res_ref), custom_call_target="tpu_custom_call" | custom-call | flops 1073741824 | bytes 4194304 | tf_op jit(solution)/shard_map/onehot/pallas_call | solution.py:223
  12.2 0.0 collective-permute-done.refs_1_
  12.2 1.9 %collective-permute-done.1.refs_2_ = bf16[32,1024]{1,0:T(8,128)(2,1)S(1)} collective-permute-done((bf16[32,1024]{1,0:T(8,128)(2,1)S(1)}, bf16[32,1024]{1,0:T(8,128)(2,1)S(1)}, u32[]{:S(2)}, u32[]{:S(2)}) %collective-permute-start.1) | collective-permute-done | bytes 65568 | tf_op jit(solution)/shard_map/ppermute | solution.py:336
  14.2 0.0 collective-permute-done.2.refs_3_
  14.2 1.1 %collective-permute-start.3 = (bf16[32,1024]{1,0:T(8,128)(2,1)S(1)}, bf16[32,1024]{1,0:T(8,128)(2,1)S(1)}, u32[]{:S(2)}, u32[]{:S(2)}) collective-permute-start(bf16[32,1024]{1,0:T(8,128)(2,1)S(1)} %share.1), channel_id=1, source_target_pairs={{0,8},{8,0},{16,24},{24,16},{1,9},{9,1},{17,25},{25,17},{2,10},{10... | collective-permute-start | bytes 196616 | tf_op jit(solution)/shard_map/ppermute | solution.py:336
  15.4 2.0 %collective-permute-start.5 = (bf16[32,1024]{1,0:T(8,128)(2,1)S(1)}, bf16[32,1024]{1,0:T(8,128)(2,1)S(1)}, u32[]{:S(2)}, u32[]{:S(2)}) collective-permute-start(bf16[32,1024]{1,0:T(8,128)(2,1)S(1)} %share.1), channel_id=1, source_target_pairs={{0,24},{8,16},{16,8},{24,0},{1,25},{9,17},{17,9},{25,1},{2,26},{10... | collective-permute-start | bytes 196616 | tf_op jit(solution)/shard_map/ppermute | solution.py:336
  17.3 0.4 collective-permute-start.4
  17.8 1.8 %collective-permute-done.3 = bf16[32,1024]{1,0:T(8,128)(2,1)S(1)} collective-permute-done((bf16[32,1024]{1,0:T(8,128)(2,1)S(1)}, bf16[32,1024]{1,0:T(8,128)(2,1)S(1)}, u32[]{:S(2)}, u32[]{:S(2)}) %collective-permute-start.3) | collective-permute-done | bytes 65568 | tf_op jit(solution)/shard_map/ppermute | solution.py:336
  19.6 0.1 collective-permute-start.12
  19.6 0.5 collective-permute-start.8
  20.2 1.5 %collective-permute-start.6 = (bf16[64,1024]{1,0:T(8,128)(2,1)S(1)}, bf16[64,1024]{1,0:T(8,128)(2,1)S(1)}, u32[]{:S(2)}, u32[]{:S(2)}) collective-permute-start(bf16[64,1024]{1,0:T(8,128)(2,1)S(1)} %pad_maximum_fusion.refs_0_), channel_id=1, source_target_pairs={{0,4},{1,3},{2,6},{3,1},{4,0},{5,7},{6,2},{7,5},{8,12},{9,11},{10,... | collective-permute-start | bytes 393224 | tf_op jit(solution)/shard_map/ppermute | solution.py:336
  21.7 1.6 %collective-permute-done.4 = bf16[32,1024]{1,0:T(8,128)(2,1)S(1)} collective-permute-done((bf16[32,1024]{1,0:T(8,128)(2,1)S(1)}, bf16[32,1024]{1,0:T(8,128)(2,1)S(1)}, u32[]{:S(2)}, u32[]{:S(2)}) %collective-permute-start.4) | collective-permute-done | bytes 65568 | tf_op jit(solution)/shard_map/ppermute | solution.py:336
  23.3 0.0 collective-permute-done.5
  23.4 1.8 %collective-permute-start.7 = (bf16[64,1024]{1,0:T(8,128)(2,1)S(1)}, bf16[64,1024]{1,0:T(8,128)(2,1)S(1)}, u32[]{:S(2)}, u32[]{:S(2)}) collective-permute-start(bf16[64,1024]{1,0:T(8,128)(2,1)S(1)} %constant_dynamic-update-slice_fusion.refs_1_), channel_id=1, source_target_pairs={{0,4},{1,3},{2,6},{3,1},{4,0},{5,7},{6,2},{7,5},{8,12},{9,11},{10,... | collective-permute-start | bytes 393224 | tf_op jit(solution)/shard_map/ppermute | solution.py:336
  25.1 0.0 collective-permute-start.13
  25.1 0.0 collective-permute-done.12.refs_8_
  25.1 1.5 %collective-permute-start.9 = (bf16[64,1024]{1,0:T(8,128)(2,1)S(1)}, bf16[64,1024]{1,0:T(8,128)(2,1)S(1)}, u32[]{:S(2)}, u32[]{:S(2)}) collective-permute-start(bf16[64,1024]{1,0:T(8,128)(2,1)S(1)} %constant_dynamic-update-slice_fusion.refs_1_), channel_id=1, source_target_pairs={{0,2},{1,5},{2,0},{3,7},{4,6},{5,1},{6,4},{7,3},{8,10},{9,13},{10,... | collective-permute-start | bytes 393224 | tf_op jit(solution)/shard_map/ppermute | solution.py:336
  26.6 0.0 collective-permute-done.8.refs_4_
  26.6 0.0 collective-permute-start.16
  26.6 0.0 collective-permute-done.6.refs_2_
  26.6 0.7 %collective-permute-start.10 = (bf16[64,1024]{1,0:T(8,128)(2,1)S(1)}, bf16[64,1024]{1,0:T(8,128)(2,1)S(1)}, u32[]{:S(2)}, u32[]{:S(2)}) collective-permute-start(bf16[64,1024]{1,0:T(8,128)(2,1)S(1)} %collective-permute-done.6.refs_2_), channel_id=1, source_target_pairs={{0,2},{1,5},{2,0},{3,7},{4,6},{5,1},{6,4},{7,3},{8,10},{9,13},{10,... | collective-permute-start | bytes 393224 | tf_op jit(solution)/shard_map/ppermute | solution.py:336
  27.4 1.6 %collective-permute-done.7.refs_3_ = bf16[64,1024]{1,0:T(8,128)(2,1)S(1)} collective-permute-done((bf16[64,1024]{1,0:T(8,128)(2,1)S(1)}, bf16[64,1024]{1,0:T(8,128)(2,1)S(1)}, u32[]{:S(2)}, u32[]{:S(2)}) %collective-permute-start.7) | collective-permute-done | bytes 131104 | tf_op jit(solution)/shard_map/ppermute | solution.py:336
  29.0 1.4 %collective-permute-start.11 = (bf16[64,1024]{1,0:T(8,128)(2,1)S(1)}, bf16[64,1024]{1,0:T(8,128)(2,1)S(1)}, u32[]{:S(2)}, u32[]{:S(2)}) collective-permute-start(bf16[64,1024]{1,0:T(8,128)(2,1)S(1)} %collective-permute-done.7.refs_3_), channel_id=1, source_target_pairs={{0,2},{1,5},{2,0},{3,7},{4,6},{5,1},{6,4},{7,3},{8,10},{9,13},{10,... | collective-permute-start | bytes 393224 | tf_op jit(solution)/shard_map/ppermute | solution.py:336
  30.5 0.0 collective-permute-done.13.refs_9_
  30.5 0.0 collective-permute-start.14
  30.5 0.0 collective-permute-done.9.refs_5_
  30.5 0.5 collective-permute-start.15
  31.0 0.0 collective-permute-done.16.refs_12_
  31.0 0.1 collective-permute-start.17
  31.0 0.6 %collective-permute-done.10.refs_6_ = bf16[64,1024]{1,0:T(8,128)(2,1)S(1)} collective-permute-done((bf16[64,1024]{1,0:T(8,128)(2,1)S(1)}, bf16[64,1024]{1,0:T(8,128)(2,1)S(1)}, u32[]{:S(2)}, u32[]{:S(2)}) %collective-permute-start.10) | collective-permute-done | bytes 131104 | tf_op jit(solution)/shard_map/ppermute | solution.py:336
  31.7 0.0 collective-permute-start.18
  31.7 2.3 %collective-permute-done.11.refs_7_ = bf16[64,1024]{1,0:T(8,128)(2,1)S(1)} collective-permute-done((bf16[64,1024]{1,0:T(8,128)(2,1)S(1)}, bf16[64,1024]{1,0:T(8,128)(2,1)S(1)}, u32[]{:S(2)}, u32[]{:S(2)}) %collective-permute-start.11) | collective-permute-done | bytes 131104 | tf_op jit(solution)/shard_map/ppermute | solution.py:336
  34.0 0.0 collective-permute-start.19
  34.0 0.0 collective-permute-done.14.refs_10_
  34.0 0.0 collective-permute-done.17.refs_13_
  34.0 0.0 collective-permute-done.15.refs_11_
  34.0 0.0 collective-permute-done.18.refs_14_
  34.0 1.3 %collective-permute-done.19.refs_15_ = bf16[64,1024]{1,0:T(8,128)(2,1)S(1)} collective-permute-done((bf16[64,1024]{1,0:T(8,128)(2,1)S(1)}, bf16[64,1024]{1,0:T(8,128)(2,1)S(1)}, u32[]{:S(2)}, u32[]{:S(2)}) %collective-permute-start.19) | collective-permute-done | bytes 131104 | tf_op jit(solution)/shard_map/ppermute | solution.py:336
  35.3 11.4 %polar.1.rot_ref = bf16[128,1024]{1,0:T(8,128)(2,1)S(1)} custom-call(bf16[64,1024]{1,0:T(8,128)(2,1)S(1)} %pad_maximum_fusion.refs_0_, bf16[64,1024]{1,0:T(8,128)(2,1)S(1)} %constant_dynamic-update-slice_fusion.refs_1_, bf16[64,1024]{1,0:T(8,128)(2,1)S(1)} %collective-permute-done.6.refs_2_, bf16[64,1024]{1,0:T(8,128)(2,1)S(1)} %collective-permute-done.7.refs_3_, ...), custom_call_target="tpu_custom_call" | custom-call | tf_op jit(solution)/shard_map/polar/pallas_call | solution.py:280
  46.7 1.4 %sums.1.refs_0_ = bf16[144,256]{1,0:T(8,128)(2,1)S(1)} custom-call(bf16[128,1024]{1,0:T(8,128)(2,1)S(1)} %polar.1.rot_ref, bf16[1024,2048]{1,0:T(8,128)(2,1)S(1)} %get-tuple-element.34.res_ref, bf16[2048,1024]{1,0:T(8,128)(2,1)S(1)} %get-tuple-element.35.onehot_ref, bf16[512,2048]{1,0:T(8,128)(2,1)S(1)} %get-tuple-element.36.masks_ref, ...), custom_call_target="tpu_custom_call" | custom-call | tf_op jit(solution)/shard_map/sums/pallas_call | solution.py:323
  48.2 2.0 %collective-permute-start.22 = (bf16[144,256]{1,0:T(8,128)(2,1)S(1)}, bf16[144,256]{1,0:T(8,128)(2,1)S(1)}, u32[]{:S(2)}, u32[]{:S(2)}) collective-permute-start(bf16[144,256]{1,0:T(8,128)(2,1)S(1)} %sums.1.refs_0_), channel_id=1, source_target_pairs={{0,24},{8,16},{16,8},{24,0},{1,25},{9,17},{17,9},{25,1},{2,26},{10... | collective-permute-start | bytes 221192 | tf_op jit(solution)/shard_map/ppermute | solution.py:336
  50.2 0.0 collective-permute-start.21
  50.2 2.5 %collective-permute-start.20 = (bf16[144,256]{1,0:T(8,128)(2,1)S(1)}, bf16[144,256]{1,0:T(8,128)(2,1)S(1)}, u32[]{:S(2)}, u32[]{:S(2)}) collective-permute-start(bf16[144,256]{1,0:T(8,128)(2,1)S(1)} %sums.1.refs_0_), channel_id=1, source_target_pairs={{0,8},{8,0},{16,24},{24,16},{1,9},{9,1},{17,25},{25,17},{2,10},{10... | collective-permute-start | bytes 221192 | tf_op jit(solution)/shard_map/ppermute | solution.py:336
  52.6 2.7 %rotated.1 = f32[2048,128]{1,0:T(8,128)} custom-call(bf16[128,1024]{1,0:T(8,128)(2,1)S(1)} %polar.1.rot_ref, bf16[2048,1024]{1,0:T(8,128)(2,1)S(1)} %get-tuple-element.25.res_ref), custom_call_target="tpu_custom_call" | custom-call | tf_op jit(solution)/shard_map/rotated/pallas_call | solution.py:323
  55.3 0.0 collective-permute-done.22.refs_3_
  55.3 2.2 %collective-permute-done.21.refs_2_ = bf16[144,256]{1,0:T(8,128)(2,1)S(1)} collective-permute-done((bf16[144,256]{1,0:T(8,128)(2,1)S(1)}, bf16[144,256]{1,0:T(8,128)(2,1)S(1)}, u32[]{:S(2)}, u32[]{:S(2)}) %collective-permute-start.21) | collective-permute-done | bytes 73760 | tf_op jit(solution)/shard_map/ppermute | solution.py:336
  57.5 0.0 collective-permute-done.20.refs_1_
  57.5 0.7 %book.1 = f32[128,256]{1,0:T(8,128)} custom-call(f32[128,256]{1,0:T(8,128)S(1)} %get-tuple-element.33.book_ref, bf16[144,256]{1,0:T(8,128)(2,1)S(1)} %sums.1.refs_0_, bf16[144,256]{1,0:T(8,128)(2,1)S(1)} %collective-permute-done.20.refs_1_, bf16[144,256]{1,0:T(8,128)(2,1)S(1)} %collective-permute-done.21.refs_2_, ...), custom_call_target="tpu_custom_call" | custom-call | tf_op jit(solution)/shard_map/book/pallas_call | solution.py:323
  (4 shorter events, 0.1 us)
Async XLA Ops:
  3.4 8.8 %collective-permute-start = (bf16[32,1024]{1,0:T(8,128)(2,1)S(1)}, bf16[32,1024]{1,0:T(8,128)(2,1)S(1)}, u32[]{:S(2)}, u32[]{:S(2)}) collective-permute-start(bf16[32,1024]{1,0:T(8,128)(2,1)S(1)} %get-tuple-element.21), channel_id=1, source_target_pairs={{0,24},{8,16},{16,8},{24,0},{1,25},{9,17},{17,9},{25,1},{2,26},{10... | collective-permute-start | bytes 196616 | tf_op jit(solution)/shard_map/ppermute | solution.py:336
  8.6 5.6 %collective-permute-start.1 = (bf16[32,1024]{1,0:T(8,128)(2,1)S(1)}, bf16[32,1024]{1,0:T(8,128)(2,1)S(1)}, u32[]{:S(2)}, u32[]{:S(2)}) collective-permute-start(bf16[32,1024]{1,0:T(8,128)(2,1)S(1)} %get-tuple-element.22), channel_id=1, source_target_pairs={{0,16},{8,24},{16,0},{24,8},{1,17},{9,25},{17,1},{25,9},{2,18},{10... | collective-permute-start | bytes 196616 | tf_op jit(solution)/shard_map/ppermute | solution.py:336
  8.6 5.6 %collective-permute-start.2 = (bf16[32,1024]{1,0:T(8,128)(2,1)S(1)}, bf16[32,1024]{1,0:T(8,128)(2,1)S(1)}, u32[]{:S(2)}, u32[]{:S(2)}) collective-permute-start(bf16[32,1024]{1,0:T(8,128)(2,1)S(1)} %get-tuple-element.23), channel_id=1, source_target_pairs={{0,8},{8,0},{16,24},{24,16},{1,9},{9,1},{17,25},{25,17},{2,10},{10... | collective-permute-start | bytes 196616 | tf_op jit(solution)/shard_map/ppermute | solution.py:336
  14.2 5.3 %collective-permute-start.3 = (bf16[32,1024]{1,0:T(8,128)(2,1)S(1)}, bf16[32,1024]{1,0:T(8,128)(2,1)S(1)}, u32[]{:S(2)}, u32[]{:S(2)}) collective-permute-start(bf16[32,1024]{1,0:T(8,128)(2,1)S(1)} %share.1), channel_id=1, source_target_pairs={{0,8},{8,0},{16,24},{24,16},{1,9},{9,1},{17,25},{25,17},{2,10},{10... | collective-permute-start | bytes 196616 | tf_op jit(solution)/shard_map/ppermute | solution.py:336
  15.4 8.0 %collective-permute-start.5 = (bf16[32,1024]{1,0:T(8,128)(2,1)S(1)}, bf16[32,1024]{1,0:T(8,128)(2,1)S(1)}, u32[]{:S(2)}, u32[]{:S(2)}) collective-permute-start(bf16[32,1024]{1,0:T(8,128)(2,1)S(1)} %share.1), channel_id=1, source_target_pairs={{0,24},{8,16},{16,8},{24,0},{1,25},{9,17},{17,9},{25,1},{2,26},{10... | collective-permute-start | bytes 196616 | tf_op jit(solution)/shard_map/ppermute | solution.py:336
  17.3 6.0 %collective-permute-start.4 = (bf16[32,1024]{1,0:T(8,128)(2,1)S(1)}, bf16[32,1024]{1,0:T(8,128)(2,1)S(1)}, u32[]{:S(2)}, u32[]{:S(2)}) collective-permute-start(bf16[32,1024]{1,0:T(8,128)(2,1)S(1)} %share.1), channel_id=1, source_target_pairs={{0,16},{8,24},{16,0},{24,8},{1,17},{9,25},{17,1},{25,9},{2,18},{10... | collective-permute-start | bytes 196616 | tf_op jit(solution)/shard_map/ppermute | solution.py:336
  19.6 5.6 %collective-permute-start.12 = (bf16[64,1024]{1,0:T(8,128)(2,1)S(1)}, bf16[64,1024]{1,0:T(8,128)(2,1)S(1)}, u32[]{:S(2)}, u32[]{:S(2)}) collective-permute-start(bf16[64,1024]{1,0:T(8,128)(2,1)S(1)} %pad_maximum_fusion.refs_0_), channel_id=1, source_target_pairs={{0,1},{1,0},{2,3},{3,2},{4,5},{5,4},{6,7},{7,6},{8,9},{9,8},{10,11... | collective-permute-start | bytes 393224 | tf_op jit(solution)/shard_map/ppermute | solution.py:336
  19.6 7.0 %collective-permute-start.8 = (bf16[64,1024]{1,0:T(8,128)(2,1)S(1)}, bf16[64,1024]{1,0:T(8,128)(2,1)S(1)}, u32[]{:S(2)}, u32[]{:S(2)}) collective-permute-start(bf16[64,1024]{1,0:T(8,128)(2,1)S(1)} %pad_maximum_fusion.refs_0_), channel_id=1, source_target_pairs={{0,2},{1,5},{2,0},{3,7},{4,6},{5,1},{6,4},{7,3},{8,10},{9,13},{10,... | collective-permute-start | bytes 393224 | tf_op jit(solution)/shard_map/ppermute | solution.py:336
  20.2 6.4 %collective-permute-start.6 = (bf16[64,1024]{1,0:T(8,128)(2,1)S(1)}, bf16[64,1024]{1,0:T(8,128)(2,1)S(1)}, u32[]{:S(2)}, u32[]{:S(2)}) collective-permute-start(bf16[64,1024]{1,0:T(8,128)(2,1)S(1)} %pad_maximum_fusion.refs_0_), channel_id=1, source_target_pairs={{0,4},{1,3},{2,6},{3,1},{4,0},{5,7},{6,2},{7,5},{8,12},{9,11},{10,... | collective-permute-start | bytes 393224 | tf_op jit(solution)/shard_map/ppermute | solution.py:336
  23.4 5.6 %collective-permute-start.7 = (bf16[64,1024]{1,0:T(8,128)(2,1)S(1)}, bf16[64,1024]{1,0:T(8,128)(2,1)S(1)}, u32[]{:S(2)}, u32[]{:S(2)}) collective-permute-start(bf16[64,1024]{1,0:T(8,128)(2,1)S(1)} %constant_dynamic-update-slice_fusion.refs_1_), channel_id=1, source_target_pairs={{0,4},{1,3},{2,6},{3,1},{4,0},{5,7},{6,2},{7,5},{8,12},{9,11},{10,... | collective-permute-start | bytes 393224 | tf_op jit(solution)/shard_map/ppermute | solution.py:336
  25.1 5.3 %collective-permute-start.13 = (bf16[64,1024]{1,0:T(8,128)(2,1)S(1)}, bf16[64,1024]{1,0:T(8,128)(2,1)S(1)}, u32[]{:S(2)}, u32[]{:S(2)}) collective-permute-start(bf16[64,1024]{1,0:T(8,128)(2,1)S(1)} %constant_dynamic-update-slice_fusion.refs_1_), channel_id=1, source_target_pairs={{0,1},{1,0},{2,3},{3,2},{4,5},{5,4},{6,7},{7,6},{8,9},{9,8},{10,11... | collective-permute-start | bytes 393224 | tf_op jit(solution)/shard_map/ppermute | solution.py:336
  25.1 5.3 %collective-permute-start.9 = (bf16[64,1024]{1,0:T(8,128)(2,1)S(1)}, bf16[64,1024]{1,0:T(8,128)(2,1)S(1)}, u32[]{:S(2)}, u32[]{:S(2)}) collective-permute-start(bf16[64,1024]{1,0:T(8,128)(2,1)S(1)} %constant_dynamic-update-slice_fusion.refs_1_), channel_id=1, source_target_pairs={{0,2},{1,5},{2,0},{3,7},{4,6},{5,1},{6,4},{7,3},{8,10},{9,13},{10,... | collective-permute-start | bytes 393224 | tf_op jit(solution)/shard_map/ppermute | solution.py:336
  26.6 4.3 %collective-permute-start.16 = (bf16[64,1024]{1,0:T(8,128)(2,1)S(1)}, bf16[64,1024]{1,0:T(8,128)(2,1)S(1)}, u32[]{:S(2)}, u32[]{:S(2)}) collective-permute-start(bf16[64,1024]{1,0:T(8,128)(2,1)S(1)} %collective-permute-done.8.refs_4_), channel_id=1, source_target_pairs={{0,1},{1,0},{2,3},{3,2},{4,5},{5,4},{6,7},{7,6},{8,9},{9,8},{10,11... | collective-permute-start | bytes 393224 | tf_op jit(solution)/shard_map/ppermute | solution.py:336
  26.6 5.0 %collective-permute-start.10 = (bf16[64,1024]{1,0:T(8,128)(2,1)S(1)}, bf16[64,1024]{1,0:T(8,128)(2,1)S(1)}, u32[]{:S(2)}, u32[]{:S(2)}) collective-permute-start(bf16[64,1024]{1,0:T(8,128)(2,1)S(1)} %collective-permute-done.6.refs_2_), channel_id=1, source_target_pairs={{0,2},{1,5},{2,0},{3,7},{4,6},{5,1},{6,4},{7,3},{8,10},{9,13},{10,... | collective-permute-start | bytes 393224 | tf_op jit(solution)/shard_map/ppermute | solution.py:336
  29.0 5.0 %collective-permute-start.11 = (bf16[64,1024]{1,0:T(8,128)(2,1)S(1)}, bf16[64,1024]{1,0:T(8,128)(2,1)S(1)}, u32[]{:S(2)}, u32[]{:S(2)}) collective-permute-start(bf16[64,1024]{1,0:T(8,128)(2,1)S(1)} %collective-permute-done.7.refs_3_), channel_id=1, source_target_pairs={{0,2},{1,5},{2,0},{3,7},{4,6},{5,1},{6,4},{7,3},{8,10},{9,13},{10,... | collective-permute-start | bytes 393224 | tf_op jit(solution)/shard_map/ppermute | solution.py:336
  30.5 3.5 %collective-permute-start.14 = (bf16[64,1024]{1,0:T(8,128)(2,1)S(1)}, bf16[64,1024]{1,0:T(8,128)(2,1)S(1)}, u32[]{:S(2)}, u32[]{:S(2)}) collective-permute-start(bf16[64,1024]{1,0:T(8,128)(2,1)S(1)} %collective-permute-done.6.refs_2_), channel_id=1, source_target_pairs={{0,1},{1,0},{2,3},{3,2},{4,5},{5,4},{6,7},{7,6},{8,9},{9,8},{10,11... | collective-permute-start | bytes 393224 | tf_op jit(solution)/shard_map/ppermute | solution.py:336
  30.5 3.5 %collective-permute-start.15 = (bf16[64,1024]{1,0:T(8,128)(2,1)S(1)}, bf16[64,1024]{1,0:T(8,128)(2,1)S(1)}, u32[]{:S(2)}, u32[]{:S(2)}) collective-permute-start(bf16[64,1024]{1,0:T(8,128)(2,1)S(1)} %collective-permute-done.7.refs_3_), channel_id=1, source_target_pairs={{0,1},{1,0},{2,3},{3,2},{4,5},{5,4},{6,7},{7,6},{8,9},{9,8},{10,11... | collective-permute-start | bytes 393224 | tf_op jit(solution)/shard_map/ppermute | solution.py:336
  31.0 3.0 %collective-permute-start.17 = (bf16[64,1024]{1,0:T(8,128)(2,1)S(1)}, bf16[64,1024]{1,0:T(8,128)(2,1)S(1)}, u32[]{:S(2)}, u32[]{:S(2)}) collective-permute-start(bf16[64,1024]{1,0:T(8,128)(2,1)S(1)} %collective-permute-done.9.refs_5_), channel_id=1, source_target_pairs={{0,1},{1,0},{2,3},{3,2},{4,5},{5,4},{6,7},{7,6},{8,9},{9,8},{10,11... | collective-permute-start | bytes 393224 | tf_op jit(solution)/shard_map/ppermute | solution.py:336
  31.7 2.3 %collective-permute-start.18 = (bf16[64,1024]{1,0:T(8,128)(2,1)S(1)}, bf16[64,1024]{1,0:T(8,128)(2,1)S(1)}, u32[]{:S(2)}, u32[]{:S(2)}) collective-permute-start(bf16[64,1024]{1,0:T(8,128)(2,1)S(1)} %collective-permute-done.10.refs_6_), channel_id=1, source_target_pairs={{0,1},{1,0},{2,3},{3,2},{4,5},{5,4},{6,7},{7,6},{8,9},{9,8},{10,11... | collective-permute-start | bytes 393224 | tf_op jit(solution)/shard_map/ppermute | solution.py:336
  34.0 1.3 %collective-permute-start.19 = (bf16[64,1024]{1,0:T(8,128)(2,1)S(1)}, bf16[64,1024]{1,0:T(8,128)(2,1)S(1)}, u32[]{:S(2)}, u32[]{:S(2)}) collective-permute-start(bf16[64,1024]{1,0:T(8,128)(2,1)S(1)} %collective-permute-done.11.refs_7_), channel_id=1, source_target_pairs={{0,1},{1,0},{2,3},{3,2},{4,5},{5,4},{6,7},{7,6},{8,9},{9,8},{10,11... | collective-permute-start | bytes 393224 | tf_op jit(solution)/shard_map/ppermute | solution.py:336
  48.2 7.2 %collective-permute-start.22 = (bf16[144,256]{1,0:T(8,128)(2,1)S(1)}, bf16[144,256]{1,0:T(8,128)(2,1)S(1)}, u32[]{:S(2)}, u32[]{:S(2)}) collective-permute-start(bf16[144,256]{1,0:T(8,128)(2,1)S(1)} %sums.1.refs_0_), channel_id=1, source_target_pairs={{0,24},{8,16},{16,8},{24,0},{1,25},{9,17},{17,9},{25,1},{2,26},{10... | collective-permute-start | bytes 221192 | tf_op jit(solution)/shard_map/ppermute | solution.py:336
  50.2 7.3 %collective-permute-start.21 = (bf16[144,256]{1,0:T(8,128)(2,1)S(1)}, bf16[144,256]{1,0:T(8,128)(2,1)S(1)}, u32[]{:S(2)}, u32[]{:S(2)}) collective-permute-start(bf16[144,256]{1,0:T(8,128)(2,1)S(1)} %sums.1.refs_0_), channel_id=1, source_target_pairs={{0,16},{8,24},{16,0},{24,8},{1,17},{9,25},{17,1},{25,9},{2,18},{10... | collective-permute-start | bytes 221192 | tf_op jit(solution)/shard_map/ppermute | solution.py:336
  50.2 7.3 %collective-permute-start.20 = (bf16[144,256]{1,0:T(8,128)(2,1)S(1)}, bf16[144,256]{1,0:T(8,128)(2,1)S(1)}, u32[]{:S(2)}, u32[]{:S(2)}) collective-permute-start(bf16[144,256]{1,0:T(8,128)(2,1)S(1)} %sums.1.refs_0_), channel_id=1, source_target_pairs={{0,8},{8,0},{16,24},{24,16},{1,9},{9,1},{17,25},{25,17},{2,10},{10... | collective-permute-start | bytes 221192 | tf_op jit(solution)/shard_map/ppermute | solution.py:336

commit v6 on v5

--- a/solution.py
+++ b/solution.py
@@ -14,7 +14,7 @@
 epsilon = 1e-06
 f32, bf16 = jnp.float32, jnp.bfloat16
 MIB = 1024 * 1024
-ROW_CHUNKS = 8
+ROW_CHUNKS = 2
 NT = (((1,), (1,)), ((), ()))
 
 

time: 58.4 us -> 58.5 us (level)
  no operation moved by 1% of the time
where the time goes in v6:
time: 58.5 us; the launch traced here: 58.4 us
  Pallas kernels  22.2 us (38%)
  starting transfers between devices  21.9 us (37%)
  waiting for transfers between devices  13.5 us (23%)
  between operations  0.74 us (1%)
    ppermute x23, starting transfers between devices, swap(): lax.ppermute(value, axis, [(i, i ^ (odd_mask if i % 2 else mask)) for i i...  21.9 us
    ppermute x23, waiting for transfers between devices, swap(): lax.ppermute(value, axis, [(i, i ^ (odd_mask if i % 2 else mask)) for i i...  13.5 us
    pallas_call x1, Pallas kernels, polar(): pl.pallas_call(kernel, out_shape=jax.ShapeDtypeStruct((own, dim), bf16),...  11.4 us
    pallas_call x4, Pallas kernels, small_call(): pl.pallas_call(kernel, out_shape=jax.ShapeDtypeStruct(shape, dtype), in_s...  4.9 us
    pallas_call x1, Pallas kernels, onehot_call(): pl.pallas_call(onehot_kernel, out_shape=(jax.ShapeDtypeStruct((rows, subs...  2.99 us
    pallas_call x1, Pallas kernels, cross_partial(): pl.pallas_call(functools.partial(cross_kernel, dp=dp), out_shape=shapes,...  2.9 us
  transfers between devices with their start and end apart: 23, of which 8 were waited for; matrix products, arithmetic and copies ran while one was open for 0% of the time, Pallas kernels for 10%

profile of v6, /device:TPU:0, one launch (start us, length us, event | category | flops | bytes accessed | tf_op | source)
XLA Modules:
  0.0 58.4 jit_solution(18106896518870525470)
XLA Ops:
  0.6 2.9 %cross_partial.1 = (f32[32,1024]{1,0:T(8,128)S(1)}, bf16[32,1024]{1,0:T(8,128)(2,1)S(1)}, bf16[32,1024]{1,0:T(8,128)(2,1)S(1)}, bf16[32,1024]{1,0:T(8,128)(2,1)S...) custom-call(s32[16,2048]{1,0:T(8,128)} %bitcast.7, f32[128,256]{1,0:T(8,128)} %bitcast.8, ...), custom_call_target="tpu_custom_call" | custom-call | tf_op jit(solution)/shard_map/cross_partial/pallas_call | solution.py:86
  3.5 5.1 %collective-permute-start = (bf16[32,1024]{1,0:T(8,128)(2,1)S(1)}, bf16[32,1024]{1,0:T(8,128)(2,1)S(1)}, u32[]{:S(2)}, u32[]{:S(2)}) collective-permute-start(bf16[32,1024]{1,0:T(8,128)(2,1)S(1)} %get-tuple-element.21), channel_id=1, source_target_pairs={{0,24},{8,16},{16,8},{24,0},{1,25},{9,17},{17,9},{25,1},{2,26},{10... | collective-permute-start | bytes 196616 | tf_op jit(solution)/shard_map/ppermute | solution.py:336
  8.7 0.0 collective-permute-start.1
  8.7 0.6 %collective-permute-start.2 = (bf16[32,1024]{1,0:T(8,128)(2,1)S(1)}, bf16[32,1024]{1,0:T(8,128)(2,1)S(1)}, u32[]{:S(2)}, u32[]{:S(2)}) collective-permute-start(bf16[32,1024]{1,0:T(8,128)(2,1)S(1)} %get-tuple-element.23), channel_id=1, source_target_pairs={{0,8},{8,0},{16,24},{24,16},{1,9},{9,1},{17,25},{25,17},{2,10},{10... | collective-permute-start | bytes 196616 | tf_op jit(solution)/shard_map/ppermute | solution.py:336
  9.3 3.0 %onehot.1 = (bf16[2048,1024]{1,0:T(8,128)(2,1)S(1)}, bf16[512,2048]{1,0:T(8,128)(2,1)S(1)}, f32[16,256]{1,0:T(8,128)S(1)}, bf16[1024,2048]{1,0:T(8,128)(2,1)S(1)}) custom-call(s32[16,2048]{1,0:T(8,128)S(1)} %get-tuple-element.24.codes_ref, bf16[2048,1024]{1,0:T(8,128)(2,1)S(1)} %get-tuple-element.25.res_ref), custom_call_target="tpu_custom_call" | custom-call | flops 1073741824 | bytes 4194304 | tf_op jit(solution)/shard_map/onehot/pallas_call | solution.py:223
  12.3 0.0 collective-permute-done.refs_1_
  12.3 2.0 %collective-permute-done.1.refs_2_ = bf16[32,1024]{1,0:T(8,128)(2,1)S(1)} collective-permute-done((bf16[32,1024]{1,0:T(8,128)(2,1)S(1)}, bf16[32,1024]{1,0:T(8,128)(2,1)S(1)}, u32[]{:S(2)}, u32[]{:S(2)}) %collective-permute-start.1) | collective-permute-done | bytes 65568 | tf_op jit(solution)/shard_map/ppermute | solution.py:336
  14.3 0.0 collective-permute-done.2.refs_3_
  14.3 1.1 %collective-permute-start.3 = (bf16[32,1024]{1,0:T(8,128)(2,1)S(1)}, bf16[32,1024]{1,0:T(8,128)(2,1)S(1)}, u32[]{:S(2)}, u32[]{:S(2)}) collective-permute-start(bf16[32,1024]{1,0:T(8,128)(2,1)S(1)} %share.1), channel_id=1, source_target_pairs={{0,8},{8,0},{16,24},{24,16},{1,9},{9,1},{17,25},{25,17},{2,10},{10... | collective-permute-start | bytes 196616 | tf_op jit(solution)/shard_map/ppermute | solution.py:336
  15.4 2.0 %collective-permute-start.5 = (bf16[32,1024]{1,0:T(8,128)(2,1)S(1)}, bf16[32,1024]{1,0:T(8,128)(2,1)S(1)}, u32[]{:S(2)}, u32[]{:S(2)}) collective-permute-start(bf16[32,1024]{1,0:T(8,128)(2,1)S(1)} %share.1), channel_id=1, source_target_pairs={{0,24},{8,16},{16,8},{24,0},{1,25},{9,17},{17,9},{25,1},{2,26},{10... | collective-permute-start | bytes 196616 | tf_op jit(solution)/shard_map/ppermute | solution.py:336
  17.4 0.4 collective-permute-start.4
  17.9 1.8 %collective-permute-done.3 = bf16[32,1024]{1,0:T(8,128)(2,1)S(1)} collective-permute-done((bf16[32,1024]{1,0:T(8,128)(2,1)S(1)}, bf16[32,1024]{1,0:T(8,128)(2,1)S(1)}, u32[]{:S(2)}, u32[]{:S(2)}) %collective-permute-start.3) | collective-permute-done | bytes 65568 | tf_op jit(solution)/shard_map/ppermute | solution.py:336
  19.7 0.1 collective-permute-start.12
  19.7 0.5 collective-permute-start.8
  20.3 1.5 %collective-permute-start.6 = (bf16[64,1024]{1,0:T(8,128)(2,1)S(1)}, bf16[64,1024]{1,0:T(8,128)(2,1)S(1)}, u32[]{:S(2)}, u32[]{:S(2)}) collective-permute-start(bf16[64,1024]{1,0:T(8,128)(2,1)S(1)} %pad_maximum_fusion.refs_0_), channel_id=1, source_target_pairs={{0,4},{1,3},{2,6},{3,1},{4,0},{5,7},{6,2},{7,5},{8,12},{9,11},{10,... | collective-permute-start | bytes 393224 | tf_op jit(solution)/shard_map/ppermute | solution.py:336
  21.8 1.6 %collective-permute-done.4 = bf16[32,1024]{1,0:T(8,128)(2,1)S(1)} collective-permute-done((bf16[32,1024]{1,0:T(8,128)(2,1)S(1)}, bf16[32,1024]{1,0:T(8,128)(2,1)S(1)}, u32[]{:S(2)}, u32[]{:S(2)}) %collective-permute-start.4) | collective-permute-done | bytes 65568 | tf_op jit(solution)/shard_map/ppermute | solution.py:336
  23.4 0.0 collective-permute-done.5
  23.5 1.8 %collective-permute-start.7 = (bf16[64,1024]{1,0:T(8,128)(2,1)S(1)}, bf16[64,1024]{1,0:T(8,128)(2,1)S(1)}, u32[]{:S(2)}, u32[]{:S(2)}) collective-permute-start(bf16[64,1024]{1,0:T(8,128)(2,1)S(1)} %constant_dynamic-update-slice_fusion.refs_1_), channel_id=1, source_target_pairs={{0,4},{1,3},{2,6},{3,1},{4,0},{5,7},{6,2},{7,5},{8,12},{9,11},{10,... | collective-permute-start | bytes 393224 | tf_op jit(solution)/shard_map/ppermute | solution.py:336
  25.2 0.0 collective-permute-start.13
  25.2 0.0 collective-permute-done.12.refs_8_
  25.2 1.5 %collective-permute-start.9 = (bf16[64,1024]{1,0:T(8,128)(2,1)S(1)}, bf16[64,1024]{1,0:T(8,128)(2,1)S(1)}, u32[]{:S(2)}, u32[]{:S(2)}) collective-permute-start(bf16[64,1024]{1,0:T(8,128)(2,1)S(1)} %constant_dynamic-update-slice_fusion.refs_1_), channel_id=1, source_target_pairs={{0,2},{1,5},{2,0},{3,7},{4,6},{5,1},{6,4},{7,3},{8,10},{9,13},{10,... | collective-permute-start | bytes 393224 | tf_op jit(solution)/shard_map/ppermute | solution.py:336
  26.7 0.0 collective-permute-done.8.refs_4_
  26.7 0.0 collective-permute-start.16
  26.7 0.0 collective-permute-done.6.refs_2_
  26.7 0.7 %collective-permute-start.10 = (bf16[64,1024]{1,0:T(8,128)(2,1)S(1)}, bf16[64,1024]{1,0:T(8,128)(2,1)S(1)}, u32[]{:S(2)}, u32[]{:S(2)}) collective-permute-start(bf16[64,1024]{1,0:T(8,128)(2,1)S(1)} %collective-permute-done.6.refs_2_), channel_id=1, source_target_pairs={{0,2},{1,5},{2,0},{3,7},{4,6},{5,1},{6,4},{7,3},{8,10},{9,13},{10,... | collective-permute-start | bytes 393224 | tf_op jit(solution)/shard_map/ppermute | solution.py:336
  27.5 1.7 %collective-permute-done.7.refs_3_ = bf16[64,1024]{1,0:T(8,128)(2,1)S(1)} collective-permute-done((bf16[64,1024]{1,0:T(8,128)(2,1)S(1)}, bf16[64,1024]{1,0:T(8,128)(2,1)S(1)}, u32[]{:S(2)}, u32[]{:S(2)}) %collective-permute-start.7) | collective-permute-done | bytes 131104 | tf_op jit(solution)/shard_map/ppermute | solution.py:336
  29.1 1.4 %collective-permute-start.11 = (bf16[64,1024]{1,0:T(8,128)(2,1)S(1)}, bf16[64,1024]{1,0:T(8,128)(2,1)S(1)}, u32[]{:S(2)}, u32[]{:S(2)}) collective-permute-start(bf16[64,1024]{1,0:T(8,128)(2,1)S(1)} %collective-permute-done.7.refs_3_), channel_id=1, source_target_pairs={{0,2},{1,5},{2,0},{3,7},{4,6},{5,1},{6,4},{7,3},{8,10},{9,13},{10,... | collective-permute-start | bytes 393224 | tf_op jit(solution)/shard_map/ppermute | solution.py:336
  30.5 0.0 collective-permute-done.13.refs_9_
  30.5 0.0 collective-permute-start.14
  30.6 0.0 collective-permute-done.9.refs_5_
  30.6 0.5 collective-permute-start.15
  31.1 0.0 collective-permute-done.16.refs_12_
  31.1 0.1 collective-permute-start.17
  31.1 0.6 %collective-permute-done.10.refs_6_ = bf16[64,1024]{1,0:T(8,128)(2,1)S(1)} collective-permute-done((bf16[64,1024]{1,0:T(8,128)(2,1)S(1)}, bf16[64,1024]{1,0:T(8,128)(2,1)S(1)}, u32[]{:S(2)}, u32[]{:S(2)}) %collective-permute-start.10) | collective-permute-done | bytes 131104 | tf_op jit(solution)/shard_map/ppermute | solution.py:336
  31.8 0.0 collective-permute-start.18
  31.8 2.3 %collective-permute-done.11.refs_7_ = bf16[64,1024]{1,0:T(8,128)(2,1)S(1)} collective-permute-done((bf16[64,1024]{1,0:T(8,128)(2,1)S(1)}, bf16[64,1024]{1,0:T(8,128)(2,1)S(1)}, u32[]{:S(2)}, u32[]{:S(2)}) %collective-permute-start.11) | collective-permute-done | bytes 131104 | tf_op jit(solution)/shard_map/ppermute | solution.py:336
  34.1 0.0 collective-permute-start.19
  34.1 0.0 collective-permute-done.14.refs_10_
  34.1 0.0 collective-permute-done.17.refs_13_
  34.1 0.0 collective-permute-done.15.refs_11_
  34.1 0.0 collective-permute-done.18.refs_14_
  34.1 1.3 %collective-permute-done.19.refs_15_ = bf16[64,1024]{1,0:T(8,128)(2,1)S(1)} collective-permute-done((bf16[64,1024]{1,0:T(8,128)(2,1)S(1)}, bf16[64,1024]{1,0:T(8,128)(2,1)S(1)}, u32[]{:S(2)}, u32[]{:S(2)}) %collective-permute-start.19) | collective-permute-done | bytes 131104 | tf_op jit(solution)/shard_map/ppermute | solution.py:336
  35.4 11.4 %polar.1.rot_ref = bf16[128,1024]{1,0:T(8,128)(2,1)S(1)} custom-call(bf16[64,1024]{1,0:T(8,128)(2,1)S(1)} %pad_maximum_fusion.refs_0_, bf16[64,1024]{1,0:T(8,128)(2,1)S(1)} %constant_dynamic-update-slice_fusion.refs_1_, bf16[64,1024]{1,0:T(8,128)(2,1)S(1)} %collective-permute-done.6.refs_2_, bf16[64,1024]{1,0:T(8,128)(2,1)S(1)} %collective-permute-done.7.refs_3_, ...), custom_call_target="tpu_custom_call" | custom-call | tf_op jit(solution)/shard_map/polar/pallas_call | solution.py:280
  46.9 1.4 %sums.1.refs_0_ = bf16[144,256]{1,0:T(8,128)(2,1)S(1)} custom-call(bf16[128,1024]{1,0:T(8,128)(2,1)S(1)} %polar.1.rot_ref, bf16[1024,2048]{1,0:T(8,128)(2,1)S(1)} %get-tuple-element.34.res_ref, bf16[2048,1024]{1,0:T(8,128)(2,1)S(1)} %get-tuple-element.35.onehot_ref, bf16[512,2048]{1,0:T(8,128)(2,1)S(1)} %get-tuple-element.36.masks_ref, ...), custom_call_target="tpu_custom_call" | custom-call | tf_op jit(solution)/shard_map/sums/pallas_call | solution.py:323
  48.3 2.0 %collective-permute-start.22 = (bf16[144,256]{1,0:T(8,128)(2,1)S(1)}, bf16[144,256]{1,0:T(8,128)(2,1)S(1)}, u32[]{:S(2)}, u32[]{:S(2)}) collective-permute-start(bf16[144,256]{1,0:T(8,128)(2,1)S(1)} %sums.1.refs_0_), channel_id=1, source_target_pairs={{0,24},{8,16},{16,8},{24,0},{1,25},{9,17},{17,9},{25,1},{2,26},{10... | collective-permute-start | bytes 221192 | tf_op jit(solution)/shard_map/ppermute | solution.py:336
  50.3 0.0 collective-permute-start.21
  50.3 2.4 %collective-permute-start.20 = (bf16[144,256]{1,0:T(8,128)(2,1)S(1)}, bf16[144,256]{1,0:T(8,128)(2,1)S(1)}, u32[]{:S(2)}, u32[]{:S(2)}) collective-permute-start(bf16[144,256]{1,0:T(8,128)(2,1)S(1)} %sums.1.refs_0_), channel_id=1, source_target_pairs={{0,8},{8,0},{16,24},{24,16},{1,9},{9,1},{17,25},{25,17},{2,10},{10... | collective-permute-start | bytes 221192 | tf_op jit(solution)/shard_map/ppermute | solution.py:336
  52.8 2.7 %rotated.1 = f32[2048,128]{1,0:T(8,128)} custom-call(bf16[128,1024]{1,0:T(8,128)(2,1)S(1)} %polar.1.rot_ref, bf16[2048,1024]{1,0:T(8,128)(2,1)S(1)} %get-tuple-element.25.res_ref), custom_call_target="tpu_custom_call" | custom-call | tf_op jit(solution)/shard_map/rotated/pallas_call | solution.py:323
  55.5 0.0 collective-permute-done.22.refs_3_
  55.5 2.2 %collective-permute-done.21.refs_2_ = bf16[144,256]{1,0:T(8,128)(2,1)S(1)} collective-permute-done((bf16[144,256]{1,0:T(8,128)(2,1)S(1)}, bf16[144,256]{1,0:T(8,128)(2,1)S(1)}, u32[]{:S(2)}, u32[]{:S(2)}) %collective-permute-start.21) | collective-permute-done | bytes 73760 | tf_op jit(solution)/shard_map/ppermute | solution.py:336
  57.6 0.0 collective-permute-done.20.refs_1_
  57.7 0.7 %book.1 = f32[128,256]{1,0:T(8,128)} custom-call(f32[128,256]{1,0:T(8,128)S(1)} %get-tuple-element.33.book_ref, bf16[144,256]{1,0:T(8,128)(2,1)S(1)} %sums.1.refs_0_, bf16[144,256]{1,0:T(8,128)(2,1)S(1)} %collective-permute-done.20.refs_1_, bf16[144,256]{1,0:T(8,128)(2,1)S(1)} %collective-permute-done.21.refs_2_, ...), custom_call_target="tpu_custom_call" | custom-call | tf_op jit(solution)/shard_map/book/pallas_call | solution.py:323
  (4 shorter events, 0.1 us)
Async XLA Ops:
  3.5 8.8 %collective-permute-start = (bf16[32,1024]{1,0:T(8,128)(2,1)S(1)}, bf16[32,1024]{1,0:T(8,128)(2,1)S(1)}, u32[]{:S(2)}, u32[]{:S(2)}) collective-permute-start(bf16[32,1024]{1,0:T(8,128)(2,1)S(1)} %get-tuple-element.21), channel_id=1, source_target_pairs={{0,24},{8,16},{16,8},{24,0},{1,25},{9,17},{17,9},{25,1},{2,26},{10... | collective-permute-start | bytes 196616 | tf_op jit(solution)/shard_map/ppermute | solution.py:336
  8.7 5.6 %collective-permute-start.1 = (bf16[32,1024]{1,0:T(8,128)(2,1)S(1)}, bf16[32,1024]{1,0:T(8,128)(2,1)S(1)}, u32[]{:S(2)}, u32[]{:S(2)}) collective-permute-start(bf16[32,1024]{1,0:T(8,128)(2,1)S(1)} %get-tuple-element.22), channel_id=1, source_target_pairs={{0,16},{8,24},{16,0},{24,8},{1,17},{9,25},{17,1},{25,9},{2,18},{10... | collective-permute-start | bytes 196616 | tf_op jit(solution)/shard_map/ppermute | solution.py:336
  8.7 5.6 %collective-permute-start.2 = (bf16[32,1024]{1,0:T(8,128)(2,1)S(1)}, bf16[32,1024]{1,0:T(8,128)(2,1)S(1)}, u32[]{:S(2)}, u32[]{:S(2)}) collective-permute-start(bf16[32,1024]{1,0:T(8,128)(2,1)S(1)} %get-tuple-element.23), channel_id=1, source_target_pairs={{0,8},{8,0},{16,24},{24,16},{1,9},{9,1},{17,25},{25,17},{2,10},{10... | collective-permute-start | bytes 196616 | tf_op jit(solution)/shard_map/ppermute | solution.py:336
  14.3 5.4 %collective-permute-start.3 = (bf16[32,1024]{1,0:T(8,128)(2,1)S(1)}, bf16[32,1024]{1,0:T(8,128)(2,1)S(1)}, u32[]{:S(2)}, u32[]{:S(2)}) collective-permute-start(bf16[32,1024]{1,0:T(8,128)(2,1)S(1)} %share.1), channel_id=1, source_target_pairs={{0,8},{8,0},{16,24},{24,16},{1,9},{9,1},{17,25},{25,17},{2,10},{10... | collective-permute-start | bytes 196616 | tf_op jit(solution)/shard_map/ppermute | solution.py:336
  15.4 8.0 %collective-permute-start.5 = (bf16[32,1024]{1,0:T(8,128)(2,1)S(1)}, bf16[32,1024]{1,0:T(8,128)(2,1)S(1)}, u32[]{:S(2)}, u32[]{:S(2)}) collective-permute-start(bf16[32,1024]{1,0:T(8,128)(2,1)S(1)} %share.1), channel_id=1, source_target_pairs={{0,24},{8,16},{16,8},{24,0},{1,25},{9,17},{17,9},{25,1},{2,26},{10... | collective-permute-start | bytes 196616 | tf_op jit(solution)/shard_map/ppermute | solution.py:336
  17.4 6.0 %collective-permute-start.4 = (bf16[32,1024]{1,0:T(8,128)(2,1)S(1)}, bf16[32,1024]{1,0:T(8,128)(2,1)S(1)}, u32[]{:S(2)}, u32[]{:S(2)}) collective-permute-start(bf16[32,1024]{1,0:T(8,128)(2,1)S(1)} %share.1), channel_id=1, source_target_pairs={{0,16},{8,24},{16,0},{24,8},{1,17},{9,25},{17,1},{25,9},{2,18},{10... | collective-permute-start | bytes 196616 | tf_op jit(solution)/shard_map/ppermute | solution.py:336
  19.7 5.6 %collective-permute-start.12 = (bf16[64,1024]{1,0:T(8,128)(2,1)S(1)}, bf16[64,1024]{1,0:T(8,128)(2,1)S(1)}, u32[]{:S(2)}, u32[]{:S(2)}) collective-permute-start(bf16[64,1024]{1,0:T(8,128)(2,1)S(1)} %pad_maximum_fusion.refs_0_), channel_id=1, source_target_pairs={{0,1},{1,0},{2,3},{3,2},{4,5},{5,4},{6,7},{7,6},{8,9},{9,8},{10,11... | collective-permute-start | bytes 393224 | tf_op jit(solution)/shard_map/ppermute | solution.py:336
  19.7 7.0 %collective-permute-start.8 = (bf16[64,1024]{1,0:T(8,128)(2,1)S(1)}, bf16[64,1024]{1,0:T(8,128)(2,1)S(1)}, u32[]{:S(2)}, u32[]{:S(2)}) collective-permute-start(bf16[64,1024]{1,0:T(8,128)(2,1)S(1)} %pad_maximum_fusion.refs_0_), channel_id=1, source_target_pairs={{0,2},{1,5},{2,0},{3,7},{4,6},{5,1},{6,4},{7,3},{8,10},{9,13},{10,... | collective-permute-start | bytes 393224 | tf_op jit(solution)/shard_map/ppermute | solution.py:336
  20.3 6.4 %collective-permute-start.6 = (bf16[64,1024]{1,0:T(8,128)(2,1)S(1)}, bf16[64,1024]{1,0:T(8,128)(2,1)S(1)}, u32[]{:S(2)}, u32[]{:S(2)}) collective-permute-start(bf16[64,1024]{1,0:T(8,128)(2,1)S(1)} %pad_maximum_fusion.refs_0_), channel_id=1, source_target_pairs={{0,4},{1,3},{2,6},{3,1},{4,0},{5,7},{6,2},{7,5},{8,12},{9,11},{10,... | collective-permute-start | bytes 393224 | tf_op jit(solution)/shard_map/ppermute | solution.py:336
  23.5 5.7 %collective-permute-start.7 = (bf16[64,1024]{1,0:T(8,128)(2,1)S(1)}, bf16[64,1024]{1,0:T(8,128)(2,1)S(1)}, u32[]{:S(2)}, u32[]{:S(2)}) collective-permute-start(bf16[64,1024]{1,0:T(8,128)(2,1)S(1)} %constant_dynamic-update-slice_fusion.refs_1_), channel_id=1, source_target_pairs={{0,4},{1,3},{2,6},{3,1},{4,0},{5,7},{6,2},{7,5},{8,12},{9,11},{10,... | collective-permute-start | bytes 393224 | tf_op jit(solution)/shard_map/ppermute | solution.py:336
  25.2 5.3 %collective-permute-start.13 = (bf16[64,1024]{1,0:T(8,128)(2,1)S(1)}, bf16[64,1024]{1,0:T(8,128)(2,1)S(1)}, u32[]{:S(2)}, u32[]{:S(2)}) collective-permute-start(bf16[64,1024]{1,0:T(8,128)(2,1)S(1)} %constant_dynamic-update-slice_fusion.refs_1_), channel_id=1, source_target_pairs={{0,1},{1,0},{2,3},{3,2},{4,5},{5,4},{6,7},{7,6},{8,9},{9,8},{10,11... | collective-permute-start | bytes 393224 | tf_op jit(solution)/shard_map/ppermute | solution.py:336
  25.2 5.3 %collective-permute-start.9 = (bf16[64,1024]{1,0:T(8,128)(2,1)S(1)}, bf16[64,1024]{1,0:T(8,128)(2,1)S(1)}, u32[]{:S(2)}, u32[]{:S(2)}) collective-permute-start(bf16[64,1024]{1,0:T(8,128)(2,1)S(1)} %constant_dynamic-update-slice_fusion.refs_1_), channel_id=1, source_target_pairs={{0,2},{1,5},{2,0},{3,7},{4,6},{5,1},{6,4},{7,3},{8,10},{9,13},{10,... | collective-permute-start | bytes 393224 | tf_op jit(solution)/shard_map/ppermute | solution.py:336
  26.7 4.3 %collective-permute-start.16 = (bf16[64,1024]{1,0:T(8,128)(2,1)S(1)}, bf16[64,1024]{1,0:T(8,128)(2,1)S(1)}, u32[]{:S(2)}, u32[]{:S(2)}) collective-permute-start(bf16[64,1024]{1,0:T(8,128)(2,1)S(1)} %collective-permute-done.8.refs_4_), channel_id=1, source_target_pairs={{0,1},{1,0},{2,3},{3,2},{4,5},{5,4},{6,7},{7,6},{8,9},{9,8},{10,11... | collective-permute-start | bytes 393224 | tf_op jit(solution)/shard_map/ppermute | solution.py:336
  26.7 5.0 %collective-permute-start.10 = (bf16[64,1024]{1,0:T(8,128)(2,1)S(1)}, bf16[64,1024]{1,0:T(8,128)(2,1)S(1)}, u32[]{:S(2)}, u32[]{:S(2)}) collective-permute-start(bf16[64,1024]{1,0:T(8,128)(2,1)S(1)} %collective-permute-done.6.refs_2_), channel_id=1, source_target_pairs={{0,2},{1,5},{2,0},{3,7},{4,6},{5,1},{6,4},{7,3},{8,10},{9,13},{10,... | collective-permute-start | bytes 393224 | tf_op jit(solution)/shard_map/ppermute | solution.py:336
  29.1 5.0 %collective-permute-start.11 = (bf16[64,1024]{1,0:T(8,128)(2,1)S(1)}, bf16[64,1024]{1,0:T(8,128)(2,1)S(1)}, u32[]{:S(2)}, u32[]{:S(2)}) collective-permute-start(bf16[64,1024]{1,0:T(8,128)(2,1)S(1)} %collective-permute-done.7.refs_3_), channel_id=1, source_target_pairs={{0,2},{1,5},{2,0},{3,7},{4,6},{5,1},{6,4},{7,3},{8,10},{9,13},{10,... | collective-permute-start | bytes 393224 | tf_op jit(solution)/shard_map/ppermute | solution.py:336
  30.5 3.5 %collective-permute-start.14 = (bf16[64,1024]{1,0:T(8,128)(2,1)S(1)}, bf16[64,1024]{1,0:T(8,128)(2,1)S(1)}, u32[]{:S(2)}, u32[]{:S(2)}) collective-permute-start(bf16[64,1024]{1,0:T(8,128)(2,1)S(1)} %collective-permute-done.6.refs_2_), channel_id=1, source_target_pairs={{0,1},{1,0},{2,3},{3,2},{4,5},{5,4},{6,7},{7,6},{8,9},{9,8},{10,11... | collective-permute-start | bytes 393224 | tf_op jit(solution)/shard_map/ppermute | solution.py:336
  30.6 3.5 %collective-permute-start.15 = (bf16[64,1024]{1,0:T(8,128)(2,1)S(1)}, bf16[64,1024]{1,0:T(8,128)(2,1)S(1)}, u32[]{:S(2)}, u32[]{:S(2)}) collective-permute-start(bf16[64,1024]{1,0:T(8,128)(2,1)S(1)} %collective-permute-done.7.refs_3_), channel_id=1, source_target_pairs={{0,1},{1,0},{2,3},{3,2},{4,5},{5,4},{6,7},{7,6},{8,9},{9,8},{10,11... | collective-permute-start | bytes 393224 | tf_op jit(solution)/shard_map/ppermute | solution.py:336
  31.1 3.0 %collective-permute-start.17 = (bf16[64,1024]{1,0:T(8,128)(2,1)S(1)}, bf16[64,1024]{1,0:T(8,128)(2,1)S(1)}, u32[]{:S(2)}, u32[]{:S(2)}) collective-permute-start(bf16[64,1024]{1,0:T(8,128)(2,1)S(1)} %collective-permute-done.9.refs_5_), channel_id=1, source_target_pairs={{0,1},{1,0},{2,3},{3,2},{4,5},{5,4},{6,7},{7,6},{8,9},{9,8},{10,11... | collective-permute-start | bytes 393224 | tf_op jit(solution)/shard_map/ppermute | solution.py:336
  31.8 2.3 %collective-permute-start.18 = (bf16[64,1024]{1,0:T(8,128)(2,1)S(1)}, bf16[64,1024]{1,0:T(8,128)(2,1)S(1)}, u32[]{:S(2)}, u32[]{:S(2)}) collective-permute-start(bf16[64,1024]{1,0:T(8,128)(2,1)S(1)} %collective-permute-done.10.refs_6_), channel_id=1, source_target_pairs={{0,1},{1,0},{2,3},{3,2},{4,5},{5,4},{6,7},{7,6},{8,9},{9,8},{10,11... | collective-permute-start | bytes 393224 | tf_op jit(solution)/shard_map/ppermute | solution.py:336
  34.1 1.3 %collective-permute-start.19 = (bf16[64,1024]{1,0:T(8,128)(2,1)S(1)}, bf16[64,1024]{1,0:T(8,128)(2,1)S(1)}, u32[]{:S(2)}, u32[]{:S(2)}) collective-permute-start(bf16[64,1024]{1,0:T(8,128)(2,1)S(1)} %collective-permute-done.11.refs_7_), channel_id=1, source_target_pairs={{0,1},{1,0},{2,3},{3,2},{4,5},{5,4},{6,7},{7,6},{8,9},{9,8},{10,11... | collective-permute-start | bytes 393224 | tf_op jit(solution)/shard_map/ppermute | solution.py:336
  48.3 7.2 %collective-permute-start.22 = (bf16[144,256]{1,0:T(8,128)(2,1)S(1)}, bf16[144,256]{1,0:T(8,128)(2,1)S(1)}, u32[]{:S(2)}, u32[]{:S(2)}) collective-permute-start(bf16[144,256]{1,0:T(8,128)(2,1)S(1)} %sums.1.refs_0_), channel_id=1, source_target_pairs={{0,24},{8,16},{16,8},{24,0},{1,25},{9,17},{17,9},{25,1},{2,26},{10... | collective-permute-start | bytes 221192 | tf_op jit(solution)/shard_map/ppermute | solution.py:336
  50.3 7.3 %collective-permute-start.21 = (bf16[144,256]{1,0:T(8,128)(2,1)S(1)}, bf16[144,256]{1,0:T(8,128)(2,1)S(1)}, u32[]{:S(2)}, u32[]{:S(2)}) collective-permute-start(bf16[144,256]{1,0:T(8,128)(2,1)S(1)} %sums.1.refs_0_), channel_id=1, source_target_pairs={{0,16},{8,24},{16,0},{24,8},{1,17},{9,25},{17,1},{25,9},{2,18},{10... | collective-permute-start | bytes 221192 | tf_op jit(solution)/shard_map/ppermute | solution.py:336
  50.3 7.3 %collective-permute-start.20 = (bf16[144,256]{1,0:T(8,128)(2,1)S(1)}, bf16[144,256]{1,0:T(8,128)(2,1)S(1)}, u32[]{:S(2)}, u32[]{:S(2)}) collective-permute-start(bf16[144,256]{1,0:T(8,128)(2,1)S(1)} %sums.1.refs_0_), channel_id=1, source_target_pairs={{0,8},{8,0},{16,24},{24,16},{1,9},{9,1},{17,25},{25,17},{2,10},{10... | collective-permute-start | bytes 221192 | tf_op jit(solution)/shard_map/ppermute | solution.py:336
